TPU v7x, 32 devices: a whole 2x2x4 slice. The times are simulated.
32 devices in a mesh: role: 4 (over y, x), gx: 2 (over core), gz: 4 (over z).
Axes of the slice: x: 2, y: 2, z: 4, core: 2. Of those that a mesh axis runs over, the one named last changes fastest.
Arguments:
- pressure_old: float32 [64, 128, 512], P('gz', 'gx', 'role'), may hold values from -2.5 to -0.2
- vg_alpha: float32 [64, 128, 512], P('gz', 'gx', 'role'), may hold values from 0.5 to 1.5
- vg_n: float32 [64, 128, 512], P('gz', 'gx', 'role'), may hold values from 1.3 to 2.5
- conductivity_sat: float32 [64, 128, 512], P('gz', 'gx', 'role'), may hold values from 0.05 to 1
- porosity: float32 [64, 128, 512], P('gz', 'gx', 'role'), may hold values from 0.25 to 0.45
- tile_owner: int32 [128, 4], replicated, may hold values from -1 to 7, as said below
- land_temp: float32 [4, 8, 6, 16, 128], P('role', ('gx', 'gz')), may hold values from -6 to 6
- transpiration: float32 [4, 8, 6, 128], P('role', ('gx', 'gz')), may hold values from 0.2 to 1
- air_temp: float32 [4, 8, 6, 128], P('role', ('gx', 'gz')), may hold values from -6 to 6
- root_layers: int32 [4, 8, 6, 128], P('role', ('gx', 'gz')), may hold values from 1 to 16
Outputs:
- pressure_new: float32 [64, 128, 512], P('gz', 'gx', 'role')
- land_temp_new: float32 [4, 8, 6, 16, 128], P('role', ('gx', 'gz'))
Inputs may be any that keep to these rules, and one draw needn't show every extreme that they name: `tile_owner`: -1 marks an inactive tile; otherwise the value is the land device, numbered along gx and gz with gz fastest, within the tile's role group; at most 3 tiles of one block have the same owner, and in every block one owner holds exactly 3 of them.
All inputs are finite; a program needn't handle non-finite values.
Results may differ from a plain program's by a relative error of at most 0.00002.
Values sent between devices are 32-bit elements; how exact they have to be, the bound alone decides.
No kernel may reach another device: no remote copies, remote signals or barrier semaphores. Data moves between devices by JAX's collectives and lax.ppermute only.
A program may use at most 64 MiB of HBM per device.

v0:
```python
import math

import jax
import jax.numpy as jnp
from jax import lax
from jax.sharding import PartitionSpec as P

LAYERS = 16
LEVELS_PER_LAYER = 4
CAP = 3
SWEEPS = 3
HEAT_STEPS = 4


def with_halo(cells, sides, width):
    for axis, dim in sides:
        count = lax.axis_size(axis)
        ends = count - 1
        head = lax.slice_in_dim(cells, 0, width, axis=dim)
        tail = lax.slice_in_dim(cells, cells.shape[dim] - width, cells.shape[dim], axis=dim)
        cells = jnp.concatenate(
            [
                lax.ppermute(tail, axis, [(i, (i + 1) % count) for i in range(ends)]),
                cells,
                lax.ppermute(head, axis, [((i + 1) % count, i) for i in range(ends)]),
            ],
            axis=dim,
        )
    return cells


def soil_curves(head, alpha, vgn, ksat):
    suction = jnp.sqrt(head * head + 0.01)
    logx = vgn * jnp.log(alpha * suction)
    expo = 1.0 - 1.0 / vgn
    softer = jnp.log1p(jnp.exp(logx))
    satur = jnp.exp(-expo * softer)
    cond = ksat * jnp.sqrt(satur) * (1.0 - jnp.exp(expo * (logx - softer))) ** 2
    return (satur, cond)


def layer_mean(values, axis):
    shape = values.shape
    split = shape[:axis] + (shape[axis] // 4, 4) + shape[axis + 1 :]
    parts = values.reshape(split)
    first = lax.index_in_dim(parts, 0, axis + 1, keepdims=False)
    second = lax.index_in_dim(parts, 1, axis + 1, keepdims=False)
    third = lax.index_in_dim(parts, 2, axis + 1, keepdims=False)
    fourth = lax.index_in_dim(parts, 3, axis + 1, keepdims=False)
    return (first + second + third + fourth) * 0.25


def land_step(satur, head, temps, tpot, air, roots):
    nlayer = satur.shape[-2]
    layer = jnp.arange(nlayer, dtype=jnp.float32)[:, None]
    depth = jnp.arange(nlayer, dtype=jnp.int32)[:, None]
    weights = jnp.exp(-layer / 4.0) * (depth < roots[..., None, :]).astype(jnp.float32)
    weights = weights / jnp.sum(weights, axis=-2, keepdims=True)
    stress = 1.0 / (1.0 + head * head / 2.25)
    uptake = tpot[..., None, :] * weights * stress
    kappa = 0.25 + 0.9 * satur
    inner = 0.5 * (kappa[..., :-1, :] + kappa[..., 1:, :])
    k_above = jnp.concatenate([kappa[..., :1, :], inner], axis=-2)
    k_below = jnp.concatenate([inner, jnp.zeros_like(kappa[..., :1, :])], axis=-2)
    for substep in range(HEAT_STEPS):
        above = jnp.concatenate([air[..., None, :], temps[..., :-1, :]], axis=-2)
        below = jnp.concatenate([temps[..., 1:, :], temps[..., -1:, :]], axis=-2)
        temps = temps + 0.2 * (k_above * (above - temps) + k_below * (below - temps)) - 0.3 * uptake
    return (uptake, temps)


def sweep_update(padh, padk, masks, head, cond, water, theta_old, sink, omega):
    mask_up, mask_down, mask_xm, mask_xp, mask_ym, mask_yp = masks
    near_up = padh[:-2, 1:-1, 1:-1]
    near_down = padh[2:, 1:-1, 1:-1]
    near_xm = padh[1:-1, :-2, 1:-1]
    near_xp = padh[1:-1, 2:, 1:-1]
    near_ym = padh[1:-1, 1:-1, :-2]
    near_yp = padh[1:-1, 1:-1, 2:]
    kf_up = 0.5 * (cond + padk[:-2, 1:-1, 1:-1]) * mask_up
    kf_down = 0.5 * (cond + padk[2:, 1:-1, 1:-1]) * mask_down
    kf_xm = 0.5 * (cond + padk[1:-1, :-2, 1:-1]) * mask_xm
    kf_xp = 0.5 * (cond + padk[1:-1, 2:, 1:-1]) * mask_xp
    kf_ym = 0.5 * (cond + padk[1:-1, 1:-1, :-2]) * mask_ym
    kf_yp = 0.5 * (cond + padk[1:-1, 1:-1, 2:]) * mask_yp
    flux = kf_up * (head - near_up) + kf_down * (head - near_down)
    flux = flux + kf_xm * (head - near_xm) + kf_xp * (head - near_xp)
    flux = flux + kf_ym * (head - near_ym) + kf_yp * (head - near_yp)
    resid = water - theta_old + flux + (kf_down - kf_up) + sink
    diag = 1.0 + (kf_up + kf_down + kf_xm + kf_xp + kf_ym + kf_yp)
    return head - omega * resid / diag


def local(
    pressure_old,
    vg_alpha,
    vg_n,
    conductivity_sat,
    porosity,
    tile_owner,
    land_temp,
    transpiration,
    air_temp,
    root_layers,
):
    levels, rows, columns = pressure_old.shape
    count_gx = lax.axis_size("gx")
    count_gz = lax.axis_size("gz")
    groups = count_gx * count_gz
    total_levels = levels * count_gz
    total_rows = rows * count_gx
    total_columns = columns * lax.axis_size("role")
    local_layers = levels // LEVELS_PER_LAYER
    index_gx = lax.axis_index("gx")
    index_gz = lax.axis_index("gz")
    index_role = lax.axis_index("role")
    satur_old, cond_old = soil_curves(pressure_old, vg_alpha, vg_n, conductivity_sat)
    theta_old = porosity * satur_old
    owners = lax.dynamic_slice(tile_owner, (index_gx * rows, index_role), (rows, 1))[:, 0]
    same_owner = owners[:, None] == owners[None, :]
    earlier = jnp.arange(rows)[:, None] > jnp.arange(rows)[None, :]
    rank = jnp.sum((same_owner & earlier).astype(jnp.int32), axis=1)
    active = owners >= 0
    flat_slot = jnp.where(active, owners * CAP + rank, groups * CAP)
    payload = jnp.stack([satur_old, pressure_old]).transpose(2, 0, 1, 3)
    payload = layer_mean(payload, 2)
    outgoing = (
        jnp.zeros((groups * CAP,) + payload.shape[1:], jnp.float32)
        .at[flat_slot]
        .set(payload, mode="drop")
    )
    received = lax.all_to_all(
        outgoing.reshape((groups, CAP) + payload.shape[1:]),
        ("gx", "gz"),
        split_axis=0,
        concat_axis=0,
        tiled=True,
    )
    received = received.reshape((count_gx, count_gz, CAP) + payload.shape[1:])
    gathered = received.transpose(0, 2, 3, 1, 4, 5).reshape(count_gx * CAP, 2, LAYERS, columns)
    temps = land_temp[0, 0]
    uptake, new_temps = land_step(
        gathered[:, 0],
        gathered[:, 1],
        temps,
        transpiration[0, 0],
        air_temp[0, 0],
        root_layers[0, 0],
    )
    my_owner = index_gx * count_gz + index_gz
    role_owners = lax.dynamic_slice(tile_owner, (0, index_role), (total_rows, 1))[:, 0].reshape(
        count_gx, rows
    )
    counts = jnp.sum((role_owners == my_owner).astype(jnp.int32), axis=1)
    slot_index = jnp.arange(count_gx * CAP, dtype=jnp.int32)
    filled = slot_index % CAP < jnp.repeat(counts, CAP)
    land_temp_new = jnp.where(filled[:, None, None], new_temps, temps)[None, None]
    returning = uptake.reshape(count_gx, CAP, count_gz, local_layers, columns).transpose(
        0, 2, 1, 3, 4
    )
    came_back = lax.all_to_all(
        returning.reshape(groups, CAP, local_layers, columns),
        ("gx", "gz"),
        split_axis=0,
        concat_axis=0,
        tiled=True,
    )
    came_back = came_back.reshape(groups * CAP, local_layers, columns)
    tile_uptake = (
        came_back[jnp.clip(flat_slot, 0, groups * CAP - 1)]
        * active.astype(jnp.float32)[:, None, None]
    )
    sink = jnp.repeat(tile_uptake, LEVELS_PER_LAYER, axis=1).transpose(1, 0, 2)
    zglob = index_gz * levels + jnp.arange(levels)
    xglob = index_gx * rows + jnp.arange(rows)
    yglob = index_role * columns + jnp.arange(columns)
    masks = (
        (zglob > 0).astype(jnp.float32)[:, None, None],
        (zglob < total_levels - 1).astype(jnp.float32)[:, None, None],
        (xglob > 0).astype(jnp.float32)[None, :, None],
        (xglob < total_rows - 1).astype(jnp.float32)[None, :, None],
        (yglob > 0).astype(jnp.float32)[None, None, :],
        (yglob < total_columns - 1).astype(jnp.float32)[None, None, :],
    )
    head = pressure_old
    cond = cond_old
    water = theta_old
    for sweep_index in range(SWEEPS):
        if sweep_index > 0:
            satur, cond = soil_curves(head, vg_alpha, vg_n, conductivity_sat)
            water = porosity * satur
        omega = 1.0 / (1.0 + 0.6 * math.cos(math.pi * (2 * sweep_index + 1) / (2 * SWEEPS)))
        padded = with_halo(jnp.stack([head, cond]), (("role", 3), ("gx", 2), ("gz", 1)), 1)
        head = sweep_update(padded[0], padded[1], masks, head, cond, water, theta_old, sink, omega)
    return (head, land_temp_new)


def solution(mesh):
    in_specs = (
        P("gz", "gx", "role"),
        P("gz", "gx", "role"),
        P("gz", "gx", "role"),
        P("gz", "gx", "role"),
        P("gz", "gx", "role"),
        P(),
        P("role", ("gx", "gz"), None, None, None),
        P("role", ("gx", "gz"), None, None),
        P("role", ("gx", "gz"), None, None),
        P("role", ("gx", "gz"), None, None),
    )
    out_specs = (P("gz", "gx", "role"), P("role", ("gx", "gz"), None, None, None))
    return jax.shard_map(local, mesh=mesh, in_specs=in_specs, out_specs=out_specs, check_vma=False)
```

profile of v0, /device:TPU:6, one launch (start us, length us, event | category | flops | bytes accessed | tf_op | source)
XLA Modules:
  0.0 144.4 jit_solution(13444537517067042189)
XLA Ops:
  0.6 1.3 compare_convert_fusion.1
  2.2 1.9 %fusion.67 = (f32[1,16,64,128]{3,2,1,0:T(8,128)S(1)}, f32[16,64,128]{2,1,0:T(8,128)S(1)}) fusion(f32[16,64,128]{2,1,0:T(8,128)} %param.12, f32[16,64,128]{2,1,0:T(8,128)} %param.11, f32[16,64,128]{2,1,0:T(8,128)} %param.10), kind=kLoop, calls=%fused_computation.140 | loop fusion | flops 1048576 | bytes 2621440 | tf_op jit(solution)/shard_map/stack | solution.py:125
  4.3 0.6 fusion.66
  4.9 0.7 broadcast_in_dim.20
  5.6 7.6 %scatter_fusion = f32[24,2,4,128]{3,2,1,0:T(4,128)} fusion(f32[24,2,4,128]{3,2,1,0:T(4,128)} %broadcast_in_dim.20, s32[64]{0:T(128)S(1)} %fusion.112, f32[64,2,4,128]{3,2,1,0:T(4,128)S(1)} %fusion.66), kind=kCustom, calls=%fused_computation.1 | custom fusion | bytes 786688 | tf_op jit(solution)/shard_map/scatter | solution.py:130
  13.2 4.9 %all-to-all-start = ((f32[8,3,2,4,128]{4,3,2,1,0:T(4,128)}), f32[8,3,2,4,128]{4,3,2,1,0:T(4,128)S(1)}, u32[]{:S(2)}, u32[]{:S(2)}) async-start(f32[8,3,2,4,128]{4,3,2,1,0:T(4,128)} %bitcast.11), calls=%async_computation | async-start | bytes 196608 | tf_op jit(solution)/shard_map/all_to_all | solution.py:132
  18.7 1.4 slice_maximum_fusion.2
  20.1 1.6 %copy.172 = f32[2,16,64,1]{2,1,3,0:T(8,128)S(1)} copy(f32[2,16,64,1]{3,2,1,0:T(8,128)} %get-tuple-element.41) | data formatting | bytes 16384 | tf_op jit(solution)/shard_map/slice | solution.py:19
  21.7 2.3 %collective-permute-start.1 = (f32[2,16,64,1]{2,1,3,0:T(8,128)S(1)}, f32[2,16,64,1]{2,1,3,0:T(8,128)S(1)}, u32[]{:S(2)}, u32[]{:S(2)}) collective-permute-start(f32[2,16,64,1]{2,1,3,0:T(8,128)S(1)} %copy.172), channel_id=1, source_target_pairs={{8,0},{16,8},{24,16},{9,1},{17,9},{25,17},{10,2},{18,10},{26,18},{... | collective-permute-start | bytes 24584 | tf_op jit(solution)/shard_map/ppermute | solution.py:25
  24.4 1.3 collective-permute-start
  25.7 0.6 multiply_exponential_fusion.3
  26.3 0.7 fusion.111
  27.4 0.6 fusion.110
  29.3 0.8 collective-permute-done
  30.8 1.1 pad_maximum_fusion.41
  32.0 1.3 collective-permute-start.3
  33.3 3.0 %collective-permute-start.2 = (f32[2,16,1,130]{3,1,2,0:T(8,128)S(1)}, f32[2,16,1,130]{3,1,2,0:T(8,128)S(1)}, u32[]{:S(2)}, u32[]{:S(2)}) collective-permute-start(f32[2,16,1,130]{3,1,2,0:T(8,128)S(1)} %copy.175), channel_id=1, source_target_pairs={{0,4},{1,5},{2,6},{3,7},{8,12},{9,13},{10,14},{11,15},{16,20},{17,... | collective-permute-start | bytes 49928 | tf_op jit(solution)/shard_map/ppermute | solution.py:23
  36.4 0.6 compare_select_fusion.7
  37.2 1.0 pad_maximum_fusion.24
  38.2 3.9 %collective-permute-start.4 = (f32[2,1,66,130]{3,2,1,0:T(8,128)S(1)}, f32[2,1,66,130]{3,2,1,0:T(8,128)S(1)}, u32[]{:S(2)}, u32[]{:S(2)}) collective-permute-start(f32[2,1,66,130]{3,2,1,0:T(8,128)S(1)} %get-tuple-element.22), channel_id=1, source_target_pairs={{0,1},{1,2},{2,3},{4,5},{5,6},{6,7},{8,9},{9,10},{10,11},{12,13},{... | collective-permute-start | bytes 205928 | tf_op jit(solution)/shard_map/ppermute | solution.py:23
  42.2 1.3 collective-permute-start.5
  44.0 1.7 %collective-permute-done.4 = f32[2,1,66,130]{3,2,1,0:T(8,128)S(1)} collective-permute-done((f32[2,1,66,130]{3,2,1,0:T(8,128)S(1)}, f32[2,1,66,130]{3,2,1,0:T(8,128)S(1)}, u32[]{:S(2)}, u32[]{:S(2)}) %collective-permute-start.4) | collective-permute-done | bytes 68672 | tf_op jit(solution)/shard_map/ppermute | solution.py:23
  45.7 4.1 %collective-permute-done.5 = f32[2,1,66,130]{3,2,1,0:T(8,128)S(1)} collective-permute-done((f32[2,1,66,130]{3,2,1,0:T(8,128)S(1)}, f32[2,1,66,130]{3,2,1,0:T(8,128)S(1)}, u32[]{:S(2)}, u32[]{:S(2)}) %collective-permute-start.5) | collective-permute-done | bytes 68672 | tf_op jit(solution)/shard_map/ppermute | solution.py:25
  49.9 1.0 pad_maximum_fusion
  51.0 1.3 slice_bitcast_fusion.5
  52.5 0.6 copy.190
  53.1 3.6 %all-to-all-start.1 = ((f32[8,3,4,128]{3,2,1,0:T(4,128)}), f32[8,3,4,128]{3,2,1,0:T(4,128)S(1)}, u32[]{:S(2)}, u32[]{:S(2)}) async-start(f32[8,3,4,128]{3,2,1,0:T(4,128)} %copy.190), calls=%async_computation.1 | async-start | bytes 98304 | tf_op jit(solution)/shard_map/all_to_all | solution.py:161
  56.9 5.8 %all-to-all-done.1 = f32[8,3,4,128]{3,2,1,0:T(4,128)S(1)} async-done(((f32[8,3,4,128]{3,2,1,0:T(4,128)}), f32[8,3,4,128]{3,2,1,0:T(4,128)S(1)}, u32[]{:S(2)}, u32[]{:S(2)}) %all-to-all-start.1) | async-done | bytes 49184 | tf_op jit(solution)/shard_map/all_to_all | solution.py:161
  62.7 0.8 gather_fusion
  63.6 7.2 %fusion.115 = (f32[1,16,64,128]{3,2,1,0:T(8,128)S(1)}, f32[16,64,128]{2,1,0:T(8,128)S(1)}) fusion(f32[16,64,128]{2,1,0:T(8,128)} %param.13, f32[16,64,128]{2,1,0:T(8,128)S(1)} %copy-done.1, f32[16,64,128]{2,1,0:T(8,128)} %param.11, f32[16,64,128]{2,1,0:T(8,128)S(1)} %copy-done, f32[64,4,128]{2,0,1:T(8,128)S(1)} %copy_multiply_fusion, ...), kind=kLoop, calls=%fused_computation.259 | loop fusion | flops 8519680 | bytes 10618496 | tf_op jit(solution)/shard_map/stack | solution.py:193
  70.8 0.8 copy-done.8
  72.8 4.2 %collective-permute-start.7 = (f32[2,16,64,1]{2,1,3,0:T(8,128)S(1)}, f32[2,16,64,1]{2,1,3,0:T(8,128)S(1)}, u32[]{:S(2)}, u32[]{:S(2)}) collective-permute-start(f32[2,16,64,1]{2,1,3,0:T(8,128)S(1)} %copy.193), channel_id=1, source_target_pairs={{8,0},{16,8},{24,16},{9,1},{17,9},{25,17},{10,2},{18,10},{26,18},{... | collective-permute-start | bytes 24584 | tf_op jit(solution)/shard_map/ppermute | solution.py:25
  77.0 1.3 collective-permute-start.6
  78.3 0.6 fusion.122
  79.0 3.7 %collective-permute-done.6 = f32[2,16,64,1]{2,1,3,0:T(8,128)S(1)} collective-permute-done((f32[2,16,64,1]{2,1,3,0:T(8,128)S(1)}, f32[2,16,64,1]{2,1,3,0:T(8,128)S(1)}, u32[]{:S(2)}, u32[]{:S(2)}) %collective-permute-start.6) | collective-permute-done | bytes 8224 | tf_op jit(solution)/shard_map/ppermute | solution.py:23
  83.8 1.3 collective-permute-start.9
  85.1 3.0 %collective-permute-start.8 = (f32[2,16,1,130]{3,1,2,0:T(8,128)S(1)}, f32[2,16,1,130]{3,1,2,0:T(8,128)S(1)}, u32[]{:S(2)}, u32[]{:S(2)}) collective-permute-start(f32[2,16,1,130]{3,1,2,0:T(8,128)S(1)} %copy.196), channel_id=1, source_target_pairs={{0,4},{1,5},{2,6},{3,7},{8,12},{9,13},{10,14},{11,15},{16,20},{17,... | collective-permute-start | bytes 49928 | tf_op jit(solution)/shard_map/ppermute | solution.py:23
  88.1 0.9 fusion.83
  89.3 2.3 %collective-permute-start.10 = (f32[2,1,66,130]{3,2,1,0:T(8,128)S(1)}, f32[2,1,66,130]{3,2,1,0:T(8,128)S(1)}, u32[]{:S(2)}, u32[]{:S(2)}) collective-permute-start(f32[2,1,66,130]{3,2,1,0:T(8,128)S(1)} %get-tuple-element.20), channel_id=1, source_target_pairs={{0,1},{1,2},{2,3},{4,5},{5,6},{6,7},{8,9},{9,10},{10,11},{12,13},{... | collective-permute-start | bytes 205928 | tf_op jit(solution)/shard_map/ppermute | solution.py:23
  91.7 1.5 %collective-permute-start.11 = (f32[2,1,66,130]{3,2,1,0:T(8,128)S(1)}, f32[2,1,66,130]{3,2,1,0:T(8,128)S(1)}, u32[]{:S(2)}, u32[]{:S(2)}) collective-permute-start(f32[2,1,66,130]{3,2,1,0:T(8,128)S(1)} %get-tuple-element.21), channel_id=1, source_target_pairs={{1,0},{2,1},{3,2},{5,4},{6,5},{7,6},{9,8},{10,9},{11,10},{13,12},{... | collective-permute-start | bytes 205928 | tf_op jit(solution)/shard_map/ppermute | solution.py:25
  93.2 0.6 fusion.121
  93.8 1.3 collective-permute-done.10
  95.1 4.1 %collective-permute-done.11 = f32[2,1,66,130]{3,2,1,0:T(8,128)S(1)} collective-permute-done((f32[2,1,66,130]{3,2,1,0:T(8,128)S(1)}, f32[2,1,66,130]{3,2,1,0:T(8,128)S(1)}, u32[]{:S(2)}, u32[]{:S(2)}) %collective-permute-start.11) | collective-permute-done | bytes 68672 | tf_op jit(solution)/shard_map/ppermute | solution.py:25
  99.3 1.0 pad_maximum_fusion.1
  100.6 0.7 copy-done.2
  102.0 3.6 %fusion.116 = (f32[1,16,64,128]{3,2,1,0:T(8,128)S(1)}, f32[16,64,128]{2,1,0:T(8,128)S(1)}) fusion(f32[16,64,128]{2,1,0:T(8,128)S(1)} %copy-done.15, f32[16,64,128]{2,1,0:T(8,128)S(1)} %copy-done.2, f32[16,64,128]{2,1,0:T(8,128)S(1)} %copy-done.12, f32[16,64,128]{2,1,0:T(8,128)S(1)} %get-tuple-element.11, f32[64,4,128]{2,0,1:T(8,128)S(1)} %copy_multiply_fusion, ...), kind=kLoop, calls=%fused_computation.260 | loop fusion | flops 9175040 | bytes 10618496 | tf_op jit(solution)/shard_map/stack | solution.py:193
  105.7 1.4 slice_maximum_fusion
  107.1 1.6 %copy.200 = f32[2,16,64,1]{2,1,3,0:T(8,128)S(1)} copy(f32[2,16,64,1]{3,2,1,0:T(8,128)} %get-tuple-element.36) | data formatting | bytes 16384 | tf_op jit(solution)/shard_map/slice | solution.py:20
  109.0 5.3 %collective-permute-start.13 = (f32[2,16,64,1]{2,1,3,0:T(8,128)S(1)}, f32[2,16,64,1]{2,1,3,0:T(8,128)}, u32[]{:S(2)}, u32[]{:S(2)}) collective-permute-start(f32[2,16,64,1]{2,1,3,0:T(8,128)S(1)} %copy.201), channel_id=1, source_target_pairs={{8,0},{16,8},{24,16},{9,1},{17,9},{25,17},{10,2},{18,10},{26,18},{... | collective-permute-start | bytes 24584 | tf_op jit(solution)/shard_map/ppermute | solution.py:25
  114.3 1.3 collective-permute-start.12
  115.7 4.2 %collective-permute-done.12 = f32[2,16,64,1]{2,1,3,0:T(8,128)S(1)} collective-permute-done((f32[2,16,64,1]{2,1,3,0:T(8,128)S(1)}, f32[2,16,64,1]{2,1,3,0:T(8,128)S(1)}, u32[]{:S(2)}, u32[]{:S(2)}) %collective-permute-start.12) | collective-permute-done | bytes 8224 | tf_op jit(solution)/shard_map/ppermute | solution.py:23
  120.4 1.1 copy.203
  121.5 1.2 pad_maximum_fusion.33
  122.8 1.3 collective-permute-start.15
  124.1 3.0 %collective-permute-start.14 = (f32[2,16,1,130]{3,1,2,0:T(8,128)S(1)}, f32[2,16,1,130]{3,1,2,0:T(8,128)S(1)}, u32[]{:S(2)}, u32[]{:S(2)}) collective-permute-start(f32[2,16,1,130]{3,1,2,0:T(8,128)S(1)} %copy.204), channel_id=1, source_target_pairs={{0,4},{1,5},{2,6},{3,7},{8,12},{9,13},{10,14},{11,15},{16,20},{17,... | collective-permute-start | bytes 49928 | tf_op jit(solution)/shard_map/ppermute | solution.py:23
  127.2 0.8 collective-permute-done.14
  128.2 2.3 %collective-permute-start.16 = (f32[2,1,66,130]{3,2,1,0:T(8,128)S(1)}, f32[2,1,66,130]{3,2,1,0:T(8,128)S(1)}, u32[]{:S(2)}, u32[]{:S(2)}) collective-permute-start(f32[2,1,66,130]{3,2,1,0:T(8,128)S(1)} %get-tuple-element.18), channel_id=1, source_target_pairs={{0,1},{1,2},{2,3},{4,5},{5,6},{6,7},{8,9},{9,10},{10,11},{12,13},{... | collective-permute-start | bytes 205928 | tf_op jit(solution)/shard_map/ppermute | solution.py:23
  130.5 1.3 collective-permute-start.17
  131.8 0.7 fusion.97
  132.6 1.6 %collective-permute-done.16 = f32[2,1,66,130]{3,2,1,0:T(8,128)S(1)} collective-permute-done((f32[2,1,66,130]{3,2,1,0:T(8,128)S(1)}, f32[2,1,66,130]{3,2,1,0:T(8,128)S(1)}, u32[]{:S(2)}, u32[]{:S(2)}) %collective-permute-start.16) | collective-permute-done | bytes 68672 | tf_op jit(solution)/shard_map/ppermute | solution.py:23
  134.1 4.1 %collective-permute-done.17 = f32[2,1,66,130]{3,2,1,0:T(8,128)S(1)} collective-permute-done((f32[2,1,66,130]{3,2,1,0:T(8,128)S(1)}, f32[2,1,66,130]{3,2,1,0:T(8,128)S(1)}, u32[]{:S(2)}, u32[]{:S(2)}) %collective-permute-start.17) | collective-permute-done | bytes 68672 | tf_op jit(solution)/shard_map/ppermute | solution.py:25
  138.2 1.0 pad_maximum_fusion.2
  139.6 0.7 copy-done.5
  140.8 3.5 %fusion.7 = f32[16,64,128]{2,1,0:T(8,128)} fusion(f32[16,64,128]{2,1,0:T(8,128)S(1)} %get-tuple-element.9, f32[18,66,130]{2,1,0:T(8,128)S(1)} %get-tuple-element.31, f32[18,66,130]{2,1,0:T(8,128)S(1)} %get-tuple-element.30, f32[16,64,128]{2,1,0:T(8,128)S(1)} %copy-done.18, f32[64,4,128]{2,0,1:T(8,128)S(1)} %copy_multiply_fusion, f32[128]{0:T(128)S(1)} %copy-done.40, ...), kind=kLoop, calls=%fused_computation.28 | loop fusion | flops 7864320 | bytes 10094208 | tf_op jit(solution)/shard_map/sub | solution.py:91
  (166 shorter events, 10.1 us)
Async XLA Ops:
  0.6 3.5 %copy-start = (f32[16,64,128]{2,1,0:T(8,128)S(1)}, f32[16,64,128]{2,1,0:T(8,128)}, u32[]{:S(2)}) copy-start(f32[16,64,128]{2,1,0:T(8,128)} %param.10) | copy-start | bytes 1572868
  4.1 25.2 %copy-start.3 = (f32[16,64,128]{2,1,0:T(8,128)}, f32[16,64,128]{2,1,0:T(8,128)S(1)}, u32[]{:S(2)}) copy-start(f32[16,64,128]{2,1,0:T(8,128)S(1)} %get-tuple-element.17) | copy-start | bytes 1572868
  4.2 13.9 %copy-start.1 = (f32[16,64,128]{2,1,0:T(8,128)S(1)}, f32[16,64,128]{2,1,0:T(8,128)}, u32[]{:S(2)}) copy-start(f32[16,64,128]{2,1,0:T(8,128)} %param.12) | copy-start | bytes 1572868
  4.2 13.9 %copy-start.14 = (f32[16,64,128]{2,1,0:T(8,128)S(1)}, f32[16,64,128]{2,1,0:T(8,128)}, u32[]{:S(2)}) copy-start(f32[16,64,128]{2,1,0:T(8,128)} %param.13) | copy-start | bytes 1572868
  13.2 39.1 %all-to-all-start = ((f32[8,3,2,4,128]{4,3,2,1,0:T(4,128)}), f32[8,3,2,4,128]{4,3,2,1,0:T(4,128)S(1)}, u32[]{:S(2)}, u32[]{:S(2)}) async-start(f32[8,3,2,4,128]{4,3,2,1,0:T(4,128)} %bitcast.11), calls=%async_computation | async-start | bytes 196608 | tf_op jit(solution)/shard_map/all_to_all | solution.py:132
  18.7 10.6 %copy-start.10 = (f32[1,16,64,128]{3,2,1,0:T(8,128)}, f32[1,16,64,128]{3,2,1,0:T(8,128)S(1)}, u32[]{:S(2)}) copy-start(f32[1,16,64,128]{3,2,1,0:T(8,128)S(1)} %fusion.114) | copy-start | bytes 1572868
  18.7 9.9 %copy-start.24 = (s32[1,1,6,128]{3,1,2,0:T(1,128)S(1)}, s32[1,1,6,128]{3,1,2,0:T(1,128)}, u32[]{:S(2)}) copy-start(s32[1,1,6,128]{3,1,2,0:T(1,128)} %param.19) | copy-start | bytes 9220
  21.7 8.8 %collective-permute-start.1 = (f32[2,16,64,1]{2,1,3,0:T(8,128)S(1)}, f32[2,16,64,1]{2,1,3,0:T(8,128)S(1)}, u32[]{:S(2)}, u32[]{:S(2)}) collective-permute-start(f32[2,16,64,1]{2,1,3,0:T(8,128)S(1)} %copy.172), channel_id=1, source_target_pairs={{8,0},{16,8},{24,16},{9,1},{17,9},{25,17},{10,2},{18,10},{26,18},{... | collective-permute-start | bytes 24584 | tf_op jit(solution)/shard_map/ppermute | solution.py:25
  24.4 5.6 %collective-permute-start = (f32[2,16,64,1]{2,1,3,0:T(8,128)S(1)}, f32[2,16,64,1]{2,1,3,0:T(8,128)S(1)}, u32[]{:S(2)}, u32[]{:S(2)}) collective-permute-start(f32[2,16,64,1]{2,1,3,0:T(8,128)S(1)} %copy.171), channel_id=1, source_target_pairs={{0,8},{8,16},{16,24},{1,9},{9,17},{17,25},{2,10},{10,18},{18,26},{... | collective-permute-start | bytes 24584 | tf_op jit(solution)/shard_map/ppermute | solution.py:23
  29.3 7.7 %copy-start.19 = (f32[1,1,6,16,128]{4,3,2,1,0:T(8,128)S(1)}, f32[1,1,6,16,128]{4,3,2,1,0:T(8,128)}, u32[]{:S(2)}) copy-start(f32[1,1,6,16,128]{4,3,2,1,0:T(8,128)} %param.16) | copy-start | bytes 147460
  29.3 7.7 %copy-start.25 = (f32[1,1,6,128]{3,1,2,0:T(1,128)S(1)}, f32[1,1,6,128]{3,1,2,0:T(1,128)}, u32[]{:S(2)}) copy-start(f32[1,1,6,128]{3,1,2,0:T(1,128)} %param.17) | copy-start | bytes 9220
  32.0 5.1 %collective-permute-start.3 = (f32[2,16,1,130]{3,1,2,0:T(8,128)S(1)}, f32[2,16,1,130]{3,1,2,0:T(8,128)S(1)}, u32[]{:S(2)}, u32[]{:S(2)}) collective-permute-start(f32[2,16,1,130]{3,1,2,0:T(8,128)S(1)} %copy.176), channel_id=1, source_target_pairs={{4,0},{5,1},{6,2},{7,3},{12,8},{13,9},{14,10},{15,11},{20,16},{21,... | collective-permute-start | bytes 49928 | tf_op jit(solution)/shard_map/ppermute | solution.py:25
  33.3 3.9 %collective-permute-start.2 = (f32[2,16,1,130]{3,1,2,0:T(8,128)S(1)}, f32[2,16,1,130]{3,1,2,0:T(8,128)S(1)}, u32[]{:S(2)}, u32[]{:S(2)}) collective-permute-start(f32[2,16,1,130]{3,1,2,0:T(8,128)S(1)} %copy.175), channel_id=1, source_target_pairs={{0,4},{1,5},{2,6},{3,7},{8,12},{9,13},{10,14},{11,15},{16,20},{17,... | collective-permute-start | bytes 49928 | tf_op jit(solution)/shard_map/ppermute | solution.py:23
  37.1 12.8 %copy-start.11 = (f32[1,16,64,128]{3,2,1,0:T(8,128)S(1)}, f32[1,16,64,128]{3,2,1,0:T(8,128)}, u32[]{:S(2)}) copy-start(f32[1,16,64,128]{3,2,1,0:T(8,128)} %copy-done.10) | copy-start | bytes 1572868
  38.2 7.5 %collective-permute-start.4 = (f32[2,1,66,130]{3,2,1,0:T(8,128)S(1)}, f32[2,1,66,130]{3,2,1,0:T(8,128)S(1)}, u32[]{:S(2)}, u32[]{:S(2)}) collective-permute-start(f32[2,1,66,130]{3,2,1,0:T(8,128)S(1)} %get-tuple-element.22), channel_id=1, source_target_pairs={{0,1},{1,2},{2,3},{4,5},{5,6},{6,7},{8,9},{9,10},{10,11},{12,13},{... | collective-permute-start | bytes 205928 | tf_op jit(solution)/shard_map/ppermute | solution.py:23
  42.2 7.7 %collective-permute-start.5 = (f32[2,1,66,130]{3,2,1,0:T(8,128)S(1)}, f32[2,1,66,130]{3,2,1,0:T(8,128)S(1)}, u32[]{:S(2)}, u32[]{:S(2)}) collective-permute-start(f32[2,1,66,130]{3,2,1,0:T(8,128)S(1)} %get-tuple-element.23), channel_id=1, source_target_pairs={{1,0},{2,1},{3,2},{5,4},{6,5},{7,6},{9,8},{10,9},{11,10},{13,12},{... | collective-permute-start | bytes 205928 | tf_op jit(solution)/shard_map/ppermute | solution.py:25
  50.9 1.5 %copy-start.26 = (f32[4,4]{0,1:T(4,128)S(1)}, f32[4,4]{0,1:T(4,128)}, u32[]{:S(2)}) copy-start(f32[4,4]{0,1:T(4,128)} %multiply_exponential_fusion.3) | copy-start | bytes 196
  50.9 5.9 %copy-start.23 = (f32[1,1,6,128]{3,1,2,0:T(1,128)S(1)}, f32[1,1,6,128]{3,1,2,0:T(1,128)}, u32[]{:S(2)}) copy-start(f32[1,1,6,128]{3,1,2,0:T(1,128)} %param.18) | copy-start | bytes 9220
  50.9 12.5 %copy-start.44 = (f32[64]{0:T(128)S(1)}, f32[64]{0:T(128)}, u32[]{:S(2)}) copy-start(f32[64]{0:T(128)} %get-tuple-element.12) | copy-start | bytes 772
  50.9 12.6 %copy-start.27 = (f32[64]{0:T(128)S(1)}, f32[64]{0:T(128)}, u32[]{:S(2)}) copy-start(f32[64]{0:T(128)} %get-tuple-element.54) | copy-start | bytes 772
  50.9 12.6 %copy-start.29 = (f32[64]{0:T(128)S(1)}, f32[64]{0:T(128)}, u32[]{:S(2)}) copy-start(f32[64]{0:T(128)} %get-tuple-element.55) | copy-start | bytes 772
  50.9 12.6 %copy-start.32 = (f32[16]{0:T(128)S(1)}, f32[16]{0:T(128)}, u32[]{:S(2)}) copy-start(f32[16]{0:T(128)} %get-tuple-element.58) | copy-start | bytes 196
  51.0 12.6 %copy-start.35 = (f32[16]{0:T(128)S(1)}, f32[16]{0:T(128)}, u32[]{:S(2)}) copy-start(f32[16]{0:T(128)} %get-tuple-element.59) | copy-start | bytes 196
  51.0 12.6 %copy-start.38 = (f32[128]{0:T(128)S(1)}, f32[128]{0:T(128)}, u32[]{:S(2)}) copy-start(f32[128]{0:T(128)} %get-tuple-element.56) | copy-start | bytes 1540
  51.0 12.6 %copy-start.41 = (f32[128]{0:T(128)S(1)}, f32[128]{0:T(128)}, u32[]{:S(2)}) copy-start(f32[128]{0:T(128)} %get-tuple-element.57) | copy-start | bytes 1540
  53.1 9.5 %all-to-all-start.1 = ((f32[8,3,4,128]{3,2,1,0:T(4,128)}), f32[8,3,4,128]{3,2,1,0:T(4,128)S(1)}, u32[]{:S(2)}, u32[]{:S(2)}) async-start(f32[8,3,4,128]{3,2,1,0:T(4,128)} %copy.190), calls=%async_computation.1 | async-start | bytes 98304 | tf_op jit(solution)/shard_map/all_to_all | solution.py:161
  72.0 11.5 %copy-start.9 = (f32[1,16,64,128]{3,2,1,0:T(8,128)S(1)}, f32[1,16,64,128]{3,2,1,0:T(8,128)}, u32[]{:S(2)}) copy-start(f32[1,16,64,128]{3,2,1,0:T(8,128)} %copy-done.8) | copy-start | bytes 1572868
  72.8 10.3 %collective-permute-start.7 = (f32[2,16,64,1]{2,1,3,0:T(8,128)S(1)}, f32[2,16,64,1]{2,1,3,0:T(8,128)S(1)}, u32[]{:S(2)}, u32[]{:S(2)}) collective-permute-start(f32[2,16,64,1]{2,1,3,0:T(8,128)S(1)} %copy.193), channel_id=1, source_target_pairs={{8,0},{16,8},{24,16},{9,1},{17,9},{25,17},{10,2},{18,10},{26,18},{... | collective-permute-start | bytes 24584 | tf_op jit(solution)/shard_map/ppermute | solution.py:25
  77.0 5.6 %collective-permute-start.6 = (f32[2,16,64,1]{2,1,3,0:T(8,128)S(1)}, f32[2,16,64,1]{2,1,3,0:T(8,128)S(1)}, u32[]{:S(2)}, u32[]{:S(2)}) collective-permute-start(f32[2,16,64,1]{2,1,3,0:T(8,128)S(1)} %copy.192), channel_id=1, source_target_pairs={{0,8},{8,16},{16,24},{1,9},{9,17},{17,25},{2,10},{10,18},{18,26},{... | collective-permute-start | bytes 24584 | tf_op jit(solution)/shard_map/ppermute | solution.py:23
  83.8 5.3 %collective-permute-start.9 = (f32[2,16,1,130]{3,1,2,0:T(8,128)S(1)}, f32[2,16,1,130]{3,1,2,0:T(8,128)S(1)}, u32[]{:S(2)}, u32[]{:S(2)}) collective-permute-start(f32[2,16,1,130]{3,1,2,0:T(8,128)S(1)} %copy.197), channel_id=1, source_target_pairs={{4,0},{5,1},{6,2},{7,3},{12,8},{13,9},{14,10},{15,11},{20,16},{21,... | collective-permute-start | bytes 49928 | tf_op jit(solution)/shard_map/ppermute | solution.py:25
  85.1 4.0 %collective-permute-start.8 = (f32[2,16,1,130]{3,1,2,0:T(8,128)S(1)}, f32[2,16,1,130]{3,1,2,0:T(8,128)S(1)}, u32[]{:S(2)}, u32[]{:S(2)}) collective-permute-start(f32[2,16,1,130]{3,1,2,0:T(8,128)S(1)} %copy.196), channel_id=1, source_target_pairs={{0,4},{1,5},{2,6},{3,7},{8,12},{9,13},{10,14},{11,15},{16,20},{17,... | collective-permute-start | bytes 49928 | tf_op jit(solution)/shard_map/ppermute | solution.py:23
  89.3 5.8 %collective-permute-start.10 = (f32[2,1,66,130]{3,2,1,0:T(8,128)S(1)}, f32[2,1,66,130]{3,2,1,0:T(8,128)S(1)}, u32[]{:S(2)}, u32[]{:S(2)}) collective-permute-start(f32[2,1,66,130]{3,2,1,0:T(8,128)S(1)} %get-tuple-element.20), channel_id=1, source_target_pairs={{0,1},{1,2},{2,3},{4,5},{5,6},{6,7},{8,9},{9,10},{10,11},{12,13},{... | collective-permute-start | bytes 205928 | tf_op jit(solution)/shard_map/ppermute | solution.py:23
  91.7 7.6 %collective-permute-start.11 = (f32[2,1,66,130]{3,2,1,0:T(8,128)S(1)}, f32[2,1,66,130]{3,2,1,0:T(8,128)S(1)}, u32[]{:S(2)}, u32[]{:S(2)}) collective-permute-start(f32[2,1,66,130]{3,2,1,0:T(8,128)S(1)} %get-tuple-element.21), channel_id=1, source_target_pairs={{1,0},{2,1},{3,2},{5,4},{6,5},{7,6},{9,8},{10,9},{11,10},{13,12},{... | collective-permute-start | bytes 205928 | tf_op jit(solution)/shard_map/ppermute | solution.py:25
  100.3 1.0 copy-start.2
  100.3 1.2 copy-start.4
  100.3 1.3 copy-start.12
  100.3 1.5 %copy-start.15 = (f32[16,64,128]{2,1,0:T(8,128)S(1)}, f32[16,64,128]{2,1,0:T(8,128)}, u32[]{:S(2)}) copy-start(f32[16,64,128]{2,1,0:T(8,128)} %param.13) | copy-start | bytes 1572868
  100.3 1.6 %copy-start.17 = (f32[16,64,128]{2,1,0:T(8,128)S(1)}, f32[16,64,128]{2,1,0:T(8,128)}, u32[]{:S(2)}) copy-start(f32[16,64,128]{2,1,0:T(8,128)} %param.14) | copy-start | bytes 1572868
  100.4 1.6 %copy-start.28 = (f32[64]{0:T(128)S(1)}, f32[64]{0:T(128)}, u32[]{:S(2)}) copy-start(f32[64]{0:T(128)} %get-tuple-element.54) | copy-start | bytes 772
  100.4 1.6 %copy-start.30 = (f32[64]{0:T(128)S(1)}, f32[64]{0:T(128)}, u32[]{:S(2)}) copy-start(f32[64]{0:T(128)} %get-tuple-element.55) | copy-start | bytes 772
  100.4 1.6 %copy-start.33 = (f32[16]{0:T(128)S(1)}, f32[16]{0:T(128)}, u32[]{:S(2)}) copy-start(f32[16]{0:T(128)} %get-tuple-element.58) | copy-start | bytes 196
  100.4 1.6 %copy-start.36 = (f32[16]{0:T(128)S(1)}, f32[16]{0:T(128)}, u32[]{:S(2)}) copy-start(f32[16]{0:T(128)} %get-tuple-element.59) | copy-start | bytes 196
  100.4 1.6 %copy-start.39 = (f32[128]{0:T(128)S(1)}, f32[128]{0:T(128)}, u32[]{:S(2)}) copy-start(f32[128]{0:T(128)} %get-tuple-element.56) | copy-start | bytes 1540
  100.4 1.6 %copy-start.42 = (f32[128]{0:T(128)S(1)}, f32[128]{0:T(128)}, u32[]{:S(2)}) copy-start(f32[128]{0:T(128)} %get-tuple-element.57) | copy-start | bytes 1540
  105.6 14.7 %copy-start.6 = (f32[1,16,64,128]{3,2,1,0:T(8,128)}, f32[1,16,64,128]{3,2,1,0:T(8,128)S(1)}, u32[]{:S(2)}) copy-start(f32[1,16,64,128]{3,2,1,0:T(8,128)S(1)} %get-tuple-element.8) | copy-start | bytes 1572868
  105.6 10.0 %copy-start.21 = (f32[6,15,128]{2,1,0:T(8,128)S(1)}, f32[6,15,128]{2,1,0:T(8,128)}, u32[]{:S(2)}) copy-start(f32[6,15,128]{2,1,0:T(8,128)} %get-tuple-element.48) | copy-start | bytes 138244
  105.7 10.0 %copy-start.22 = (f32[6,15,128]{2,1,0:T(8,128)S(1)}, f32[6,15,128]{2,1,0:T(8,128)}, u32[]{:S(2)}) copy-start(f32[6,15,128]{2,1,0:T(8,128)} %get-tuple-element.49) | copy-start | bytes 138244
  109.0 11.3 %collective-permute-start.13 = (f32[2,16,64,1]{2,1,3,0:T(8,128)S(1)}, f32[2,16,64,1]{2,1,3,0:T(8,128)}, u32[]{:S(2)}, u32[]{:S(2)}) collective-permute-start(f32[2,16,64,1]{2,1,3,0:T(8,128)S(1)} %copy.201), channel_id=1, source_target_pairs={{8,0},{16,8},{24,16},{9,1},{17,9},{25,17},{10,2},{18,10},{26,18},{... | collective-permute-start | bytes 24584 | tf_op jit(solution)/shard_map/ppermute | solution.py:25
  114.3 5.6 %collective-permute-start.12 = (f32[2,16,64,1]{2,1,3,0:T(8,128)S(1)}, f32[2,16,64,1]{2,1,3,0:T(8,128)S(1)}, u32[]{:S(2)}, u32[]{:S(2)}) collective-permute-start(f32[2,16,64,1]{2,1,3,0:T(8,128)S(1)} %copy.200), channel_id=1, source_target_pairs={{0,8},{8,16},{16,24},{1,9},{9,17},{17,25},{2,10},{10,18},{18,26},{... | collective-permute-start | bytes 24584 | tf_op jit(solution)/shard_map/ppermute | solution.py:23
  121.5 6.5 %copy-start.7 = (f32[1,16,64,128]{3,2,1,0:T(8,128)S(1)}, f32[1,16,64,128]{3,2,1,0:T(8,128)}, u32[]{:S(2)}) copy-start(f32[1,16,64,128]{3,2,1,0:T(8,128)} %copy-done.6) | copy-start | bytes 1572868
  122.7 9.1 %copy-start.20 = (f32[1,1,6,16,128]{4,3,2,1,0:T(8,128)S(1)}, f32[1,1,6,16,128]{4,3,2,1,0:T(8,128)}, u32[]{:S(2)}) copy-start(f32[1,1,6,16,128]{4,3,2,1,0:T(8,128)} %param.16) | copy-start | bytes 147460
  122.7 9.1 %copy-start.45 = (pred[6]{0:T(512)(128)(4,1)S(1)}, pred[6]{0:T(512)(128)(4,1)}, u32[]{:S(2)}) copy-start(pred[6]{0:T(512)(128)(4,1)} %fusion.110) | copy-start | bytes 22
  122.8 4.4 %collective-permute-start.15 = (f32[2,16,1,130]{3,1,2,0:T(8,128)S(1)}, f32[2,16,1,130]{3,1,2,0:T(8,128)S(1)}, u32[]{:S(2)}, u32[]{:S(2)}) collective-permute-start(f32[2,16,1,130]{3,1,2,0:T(8,128)S(1)} %copy.205), channel_id=1, source_target_pairs={{4,0},{5,1},{6,2},{7,3},{12,8},{13,9},{14,10},{15,11},{20,16},{21,... | collective-permute-start | bytes 49928 | tf_op jit(solution)/shard_map/ppermute | solution.py:25
  124.1 3.9 %collective-permute-start.14 = (f32[2,16,1,130]{3,1,2,0:T(8,128)S(1)}, f32[2,16,1,130]{3,1,2,0:T(8,128)S(1)}, u32[]{:S(2)}, u32[]{:S(2)}) collective-permute-start(f32[2,16,1,130]{3,1,2,0:T(8,128)S(1)} %copy.204), channel_id=1, source_target_pairs={{0,4},{1,5},{2,6},{3,7},{8,12},{9,13},{10,14},{11,15},{16,20},{17,... | collective-permute-start | bytes 49928 | tf_op jit(solution)/shard_map/ppermute | solution.py:23
  128.2 5.9 %collective-permute-start.16 = (f32[2,1,66,130]{3,2,1,0:T(8,128)S(1)}, f32[2,1,66,130]{3,2,1,0:T(8,128)S(1)}, u32[]{:S(2)}, u32[]{:S(2)}) collective-permute-start(f32[2,1,66,130]{3,2,1,0:T(8,128)S(1)} %get-tuple-element.18), channel_id=1, source_target_pairs={{0,1},{1,2},{2,3},{4,5},{5,6},{6,7},{8,9},{9,10},{10,11},{12,13},{... | collective-permute-start | bytes 205928 | tf_op jit(solution)/shard_map/ppermute | solution.py:23
  130.5 7.7 %collective-permute-start.17 = (f32[2,1,66,130]{3,2,1,0:T(8,128)S(1)}, f32[2,1,66,130]{3,2,1,0:T(8,128)S(1)}, u32[]{:S(2)}, u32[]{:S(2)}) collective-permute-start(f32[2,1,66,130]{3,2,1,0:T(8,128)S(1)} %get-tuple-element.19), channel_id=1, source_target_pairs={{1,0},{2,1},{3,2},{5,4},{6,5},{7,6},{9,8},{10,9},{11,10},{13,12},{... | collective-permute-start | bytes 205928 | tf_op jit(solution)/shard_map/ppermute | solution.py:25
  139.3 1.2 copy-start.13
  139.3 1.3 copy-start.16
  139.3 1.5 %copy-start.18 = (f32[16,64,128]{2,1,0:T(8,128)S(1)}, f32[16,64,128]{2,1,0:T(8,128)}, u32[]{:S(2)}) copy-start(f32[16,64,128]{2,1,0:T(8,128)} %param.14) | copy-start | bytes 1572868
  139.3 1.5 %copy-start.31 = (f32[64]{0:T(128)S(1)}, f32[64]{0:T(128)}, u32[]{:S(2)}) copy-start(f32[64]{0:T(128)} %get-tuple-element.55) | copy-start | bytes 772
  139.3 1.5 %copy-start.34 = (f32[16]{0:T(128)S(1)}, f32[16]{0:T(128)}, u32[]{:S(2)}) copy-start(f32[16]{0:T(128)} %get-tuple-element.58) | copy-start | bytes 196
  139.4 1.5 %copy-start.37 = (f32[16]{0:T(128)S(1)}, f32[16]{0:T(128)}, u32[]{:S(2)}) copy-start(f32[16]{0:T(128)} %get-tuple-element.59) | copy-start | bytes 196
  139.4 1.5 %copy-start.40 = (f32[128]{0:T(128)S(1)}, f32[128]{0:T(128)}, u32[]{:S(2)}) copy-start(f32[128]{0:T(128)} %get-tuple-element.56) | copy-start | bytes 1540
  139.4 1.5 %copy-start.43 = (f32[128]{0:T(128)S(1)}, f32[128]{0:T(128)}, u32[]{:S(2)}) copy-start(f32[128]{0:T(128)} %get-tuple-element.57) | copy-start | bytes 1540
  (2 other events, 1.8 us)
where the time goes:
time: 146 us; the launch traced here: 144 us
  starting transfers between devices  49.9 us (34%)
  other arithmetic  35.7 us (24%)
  waiting for transfers between devices  32.3 us (22%)
  local copies, waits for them, and re-layouts  24.7 us (17%)
  between operations  1.81 us (1%)
    ppermute x9, starting transfers between devices, with_halo(): lax.ppermute(tail, axis, [(i, (i + 1) % count) for i in range(ends)])  21.6 us
    ppermute x9, starting transfers between devices, with_halo(): lax.ppermute(head, axis, [((i + 1) % count, i) for i in range(ends)])  19.8 us
    another operation x6, other arithmetic, local(): jnp.stack([head, cond])  14.6 us
    ppermute x9, waiting for transfers between devices, with_halo(): lax.ppermute(tail, axis, [(i, (i + 1) % count) for i in range(ends)])  14.1 us
    ppermute x9, waiting for transfers between devices, with_halo(): lax.ppermute(head, axis, [((i + 1) % count, i) for i in range(ends)])  12.4 us
    scatter x1, local copies, waits for them, and re-layouts, local(): outgoing = jnp.zeros((groups * CAP,) + payload.shape[1:], jnp.float32).at...  7.62 us
    all_to_all x1, waiting for transfers between devices, local(): lax.all_to_all(returning.reshape(groups, CAP, local_layers, columns), ('g...  5.8 us
    all_to_all x1, starting transfers between devices, local(): lax.all_to_all(outgoing.reshape((groups, CAP) + payload.shape[1:]), ('gx'...  4.88 us
  transfers between devices with their start and end apart: 20, of which 11 were waited for; matrix products, arithmetic and copies ran while one was open for 12% of the time, Pallas kernels for 0%

commit v1 on v0

v1 whole, which is shorter than its diff:
```python
import functools
import math

import jax
import jax.numpy as jnp
from jax import lax
from jax.experimental import pallas as pl
from jax.experimental.pallas import tpu as pltpu
from jax.sharding import PartitionSpec as P

LAYERS_PER_BLOCK = 4
LEVELS_PER_LAYER = 4
CAP = 3
SWEEPS = 3
HEAT_STEPS = 4
HALO = SWEEPS
AXES = ("role", "gx", "gz")
VMEM = pl.BlockSpec(memory_space=pltpu.VMEM)
SMEM = pl.BlockSpec(memory_space=pltpu.SMEM)
ANY = pl.BlockSpec(memory_space=pl.ANY)
PARAMS = pltpu.CompilerParams(vmem_limit_bytes=40 * 1024 * 1024)

LEVELS = 16
ROWS = 64
COLS = 128
EDGE = 8
WIDE = ROWS + EDGE
H0 = 0
NH = LEVELS + 2 * HALO
A0 = H0 + NH
NC = LEVELS + 2 * HALO - 2
N0 = A0 + NC
S0 = N0 + NC
K_LO = S0 + NC
K_HI = K_LO + 1
P0 = K_HI + 1
NP = LEVELS + 2 * HALO - 4
M_LO = P0 + NP
M_HI = M_LO + 1
TP = M_HI + 1
RT = TP + 1
PLANES = RT + 1
PACKS = (PLANES + 7) // 8
SIDE = 16
Z_SEND = 12
Y_SEND = (PLANES * HALO + 7) // 8 * 8


def omega(sweep):
    return 1.0 / (1.0 + 0.6 * math.cos(math.pi * (2 * sweep + 1) / (2 * SWEEPS)))


def place(axis):
    return lax.axis_index(axis)


def is_even(axis):
    return lax.rem(place(axis), 2) == 0


def pairing(sizes, axis, odd):
    pairs = []
    which = AXES.index(axis)
    for index in range(math.prod(sizes)):
        at = [index // (sizes[1] * sizes[2]), index // sizes[2] % sizes[1], index % sizes[2]]
        count = sizes[which]
        there = list(at)
        if not odd:
            there[which] = at[which] ^ 1
        else:
            there[which] = at[which] + (1 if at[which] % 2 else -1)
            if not 0 <= there[which] < count:
                there = list(at)
                if axis == "gx":
                    there[1] = count - 1 - at[1]
                else:
                    there[1] = at[1] ^ 1
        pairs.append((index, (there[0] * sizes[1] + there[1]) * sizes[2] + there[2]))
    return pairs


def xor_pairs(sizes, axis, bit):
    pairs = []
    which = AXES.index(axis)
    for index in range(math.prod(sizes)):
        at = [index // (sizes[1] * sizes[2]), index // sizes[2] % sizes[1], index % sizes[2]]
        at[which] ^= bit
        pairs.append((index, (at[0] * sizes[1] + at[1]) * sizes[2] + at[2]))
    return pairs


def curves(head, alpha2, half_n, half_ks, expo):
    logx = half_n * jnp.log(alpha2 * (head * head + 0.01))
    softer = jnp.log(1.0 + jnp.exp(logx))
    root = jnp.exp(-0.5 * expo * softer)
    gap = 1.0 - jnp.exp(expo * (logx - softer))
    return root * root, half_ks * root * (gap * gap)


def expo_of(half_n):
    return 1.0 - 0.5 / half_n


def z_faces(h, a, n, s, p, out_e, out_o, hb, ab, nb, sb, pb, sem):
    copies = []
    for side in range(2):
        for src, dst, count in ((h, hb, 4), (a, ab, 3), (n, nb, 3), (s, sb, 3), (p, pb, 1)):
            start = 0 if side == 0 else LEVELS - count
            copy = pltpu.make_async_copy(src.at[pl.ds(start, count)], dst.at[side], sem.at[len(copies)])
            copy.start()
            copies.append(copy)
    for copy in copies:
        copy.wait()

    def put(out, side):
        def level(buf, count, dist):
            return buf[side, dist - 1 if side == 0 else count - dist]

        for dist in (1, 2, 3):
            out[dist - 1] = level(hb, 4, dist)
        for dist in (1, 2):
            alpha = level(ab, 3, dist)
            out[2 + dist] = alpha * alpha
            out[4 + dist] = 0.5 * level(nb, 3, dist)
            out[6 + dist] = 0.5 * level(sb, 3, dist)
        out[9] = level(pb, 1, 1)
        alpha = level(ab, 3, 3)
        half_n = 0.5 * level(nb, 3, 3)
        out[10] = curves(level(hb, 4, 3), alpha * alpha, half_n, 0.5 * level(sb, 3, 3), expo_of(half_n))[1]
        out[11] = (hb[side, 0] + hb[side, 1] + hb[side, 2] + hb[side, 3]) * 0.25

    even = is_even("gz")

    @pl.when(even)
    def _():
        put(out_e, 1)
        put(out_o, 0)

    @pl.when(jnp.logical_not(even))
    def _():
        put(out_e, 0)
        put(out_o, 1)


def rank_rows(owners, counts, groups, visit):
    def clear(i, carry):
        counts[i] = 0
        return carry

    def step(x, carry):
        owner = owners[x]

        @pl.when(owner >= 0)
        def _():
            rank = counts[owner]
            counts[owner] = rank + 1
            visit(x, owner, rank)

        return carry

    lax.fori_loop(0, groups, clear, 0)
    lax.fori_loop(0, ROWS, step, 0)


def land_pack(count_gx, count_gz, owners, h, a, n, s, p, tr, rt, y, t, planes, means, counts, slots):
    groups = count_gx * count_gz
    me_gx = place("gx")
    me = me_gx * count_gz + place("gz")

    def clear(i, carry):
        slots[i] = -1
        return carry

    lax.fori_loop(0, groups * CAP, clear, 0)

    def visit(x, owner, rank):
        slots[owner * CAP + rank] = x

    rank_rows(owners, counts, groups, visit)
    for layer in range(LAYERS_PER_BLOCK):
        saturs = []
        heads = []
        for level in range(layer * LEVELS_PER_LAYER, (layer + 1) * LEVELS_PER_LAYER):
            head = h[level]
            alpha = a[level]
            half_n = 0.5 * n[level]
            logx = half_n * jnp.log(alpha * alpha * (head * head + 0.01))
            softer = jnp.log(1.0 + jnp.exp(logx))
            saturs.append(jnp.exp(-expo_of(half_n) * softer))
            heads.append(head)
        means[layer] = (saturs[0] + saturs[1] + saturs[2] + saturs[3]) * 0.25
        means[LAYERS_PER_BLOCK + layer] = (heads[0] + heads[1] + heads[2] + heads[3]) * 0.25
    for j in range(groups):
        for c in range(CAP):
            row = slots[(me ^ j) * CAP + c]
            safe = jnp.maximum(row, 0)
            for q in range(8):
                value = means[q, pl.ds(safe, 1), :]
                y[j, pl.ds(c * 8 + q, 1), :] = jnp.where(row >= 0, value, -1.0)
    for j in range(count_gx):
        block = me_gx ^ j
        t[j] = jnp.zeros((8, COLS), jnp.float32)
        for c in range(CAP):
            t[j, pl.ds(2 * c, 1), :] = tr[pl.ds(block * CAP + c, 1), :]
            t[j, pl.ds(2 * c + 1, 1), :] = rt[pl.ds(block * CAP + c, 1), :].astype(jnp.float32)
    for level in range(LEVELS):
        planes[H0 + HALO + level] = h[level]
        alpha = a[level]
        planes[A0 + HALO - 1 + level] = alpha * alpha
        planes[N0 + HALO - 1 + level] = 0.5 * n[level]
        planes[S0 + HALO - 1 + level] = 0.5 * s[level]
        planes[P0 + HALO - 2 + level] = p[level]


def tile_values(count_gz, groups, owners, t, out, counts):
    me = place("gx") * count_gz + place("gz")
    out[0] = jnp.zeros((ROWS, COLS), jnp.float32)
    out[1] = jnp.ones((ROWS, COLS), jnp.float32)

    def visit(x, owner, rank):
        j = me ^ owner
        out[0, pl.ds(x, 1), :] = t[j, pl.ds(2 * rank, 1), :]
        out[1, pl.ds(x, 1), :] = t[j, pl.ds(2 * rank + 1, 1), :]

    rank_rows(owners, counts, groups, visit)


def x_faces(count_gx, planes_in, z_e, z_o, tile, planes, *sends):
    def take(got, low):
        for dist in (1, 2, 3):
            planes[H0 + (HALO - dist if low else HALO + LEVELS - 1 + dist)] = got[dist - 1]
        for dist in (1, 2):
            off = HALO - 1 - dist if low else HALO - 2 + LEVELS + dist
            planes[A0 + off] = got[2 + dist]
            planes[N0 + off] = got[4 + dist]
            planes[S0 + off] = got[6 + dist]
        planes[P0 + (0 if low else NP - 1)] = got[9]
        planes[K_LO if low else K_HI] = got[10]
        planes[M_LO if low else M_HI] = got[11]

    even_z = is_even("gz")

    @pl.when(even_z)
    def _():
        take(z_e, False)
        take(z_o, True)

    @pl.when(jnp.logical_not(even_z))
    def _():
        take(z_e, True)
        take(z_o, False)

    planes[TP] = tile[0]
    planes[RT] = tile[1]

    def put(send, last):
        start = ROWS - HALO if last else 0
        for p in range(PLANES):
            send[p, pl.ds(0, HALO), :] = planes[p, pl.ds(start, HALO), :]

    even_x = is_even("gx")

    @pl.when(even_x)
    def _():
        put(sends[0], True)
        if count_gx > 2:
            put(sends[1], False)

    @pl.when(jnp.logical_not(even_x))
    def _():
        put(sends[0], False)
        if count_gx > 2:
            put(sends[1], True)


def y_faces(count_gx, *refs):
    planes = refs[0]
    if count_gx > 2:
        got_e, got_o = refs[1], refs[2]
    else:
        got_e, got_o = refs[1], None
    edge, strips, send_e, send_o = refs[-4:]

    def take(high, low):
        for p in range(PLANES):
            edge[p] = planes[p, ROWS - EDGE : ROWS]
            if high is not None:
                edge[p, pl.ds(0, HALO), :] = high[p, pl.ds(0, HALO), :]
            if low is not None:
                edge[p, pl.ds(EDGE - HALO, HALO), :] = low[p, pl.ds(0, HALO), :]

    even_x = is_even("gx")

    @pl.when(even_x)
    def _():
        take(got_e, got_o)

    @pl.when(jnp.logical_not(even_x))
    def _():
        take(got_o, got_e)

    lane_group = lax.broadcasted_iota(jnp.int32, (WIDE, COLS), 1) // SIDE

    def pack(t, carry):
        acc = jnp.zeros((WIDE, COLS), jnp.float32)
        for j in range(8):
            p = jnp.minimum(t * 8 + j, PLANES - 1)
            value = jnp.concatenate([planes[p], edge[p]], axis=0)
            acc = jnp.where(lane_group == j, pltpu.roll(value, SIDE * j + 8, 1), acc)
        full = jnp.concatenate([acc] + [acc[ROWS:WIDE]] * ((COLS - WIDE) // EDGE), axis=0)
        strips[pl.ds(pl.multiple_of(t * COLS, COLS), COLS), :] = full.T
        return carry

    lax.fori_loop(0, PACKS, pack, 0)

    def put(send, last):
        start = 5 if last else 8
        for p in range(PLANES):
            send[pl.ds(p * HALO, HALO), :] = strips[pl.ds(p * SIDE + start, HALO), :]
        rest = Y_SEND - PLANES * HALO
        if rest:
            send[pl.ds(PLANES * HALO, rest), :] = jnp.zeros((rest, COLS), jnp.float32)

    even_y = is_even("role")

    @pl.when(even_y)
    def _():
        put(send_e, True)
        put(send_o, False)

    @pl.when(jnp.logical_not(even_y))
    def _():
        put(send_e, False)
        put(send_o, True)


def uptake_of(tpot, roots, head, layers, base_exp, first):
    total = jnp.zeros_like(tpot)
    for layer in range(layers):
        total = total + jnp.where(roots > float(layer), math.exp(-layer / 4.0), 0.0)
    share = tpot * base_exp / total
    result = []
    for q in range(LAYERS_PER_BLOCK + 2):
        depth = (first + (q - 1)).astype(jnp.float32)
        weight = jnp.where(depth < roots, math.exp(-(q - 1) / 4.0) * share, 0.0)
        result.append(weight / (1.0 + head[q] * head[q] * (1.0 / 2.25)))
    return result


def sweeps(count_role, count_gx, count_gz, planes, edge, strips_in, y_e, y_o, out,
           strips, ha, hb, kc, mm, th, wd, sk, xmask,
           sa, sb, sc, ks, sm, sth, swd, ssk, turn):
    me_role, me_gx, me_gz = place("role"), place("gx"), place("gz")
    layers = LAYERS_PER_BLOCK * count_gz
    first = me_gz * LAYERS_PER_BLOCK
    f32 = jnp.float32
    z_top = jnp.where(me_gz == 0, 0.0, 1.0).astype(f32)
    z_bottom = jnp.where(me_gz == count_gz - 1, 0.0, 1.0).astype(f32)
    x_first = jnp.where(me_gx == 0, 0.0, 1.0).astype(f32)
    x_last = jnp.where(me_gx == count_gx - 1, 0.0, 1.0).astype(f32)
    y_first = jnp.where(me_role == 0, 0.0, 1.0).astype(f32)
    y_last = jnp.where(me_role == count_role - 1, 0.0, 1.0).astype(f32)
    exp_first = jnp.exp(jnp.zeros((8, COLS), f32) - me_gz.astype(f32))

    strips[...] = strips_in[...]

    def take(high, low):
        for p in range(PLANES):
            strips[pl.ds(p * SIDE, HALO), :] = high[pl.ds(p * HALO, HALO), :]
            strips[pl.ds(p * SIDE + SIDE - HALO, HALO), :] = low[pl.ds(p * HALO, HALO), :]

    even_y = is_even("role")

    @pl.when(even_y)
    def _():
        take(y_e, y_o)

    @pl.when(jnp.logical_not(even_y))
    def _():
        take(y_o, y_e)

    def wide(p):
        return jnp.concatenate([planes[p], edge[p]], axis=0)

    def put(ref, i, value):
        ref[i, 8 : 8 + WIDE] = value
        ref[i, 0:8] = value[ROWS:WIDE]
        ref[i, 8 + WIDE : 16 + WIDE] = value[0:8]

    row = lax.broadcasted_iota(jnp.int32, (WIDE, COLS), 0)
    xmask[0] = jnp.where(row == 0, x_first, 1.0)
    xmask[1] = jnp.where(row == ROWS - 1, x_last, 1.0)

    def fill(i, carry):
        put(ha, i, wide(H0 + i))
        return carry

    lax.fori_loop(0, NH, fill, 0)
    put(kc, 0, wide(K_LO))
    put(kc, NH - 1, wide(K_HI))

    def mean4(ref, i):
        return (ref[i, 8 : 8 + WIDE] + ref[i + 1, 8 : 8 + WIDE] + ref[i + 2, 8 : 8 + WIDE] + ref[i + 3, 8 : 8 + WIDE]) * 0.25

    heads = [wide(M_LO)] + [mean4(ha, HALO + 4 * q) for q in range(LAYERS_PER_BLOCK)] + [wide(M_HI)]
    base = jnp.concatenate([exp_first] * (WIDE // 8), axis=0)
    for q, value in enumerate(uptake_of(wide(TP), wide(RT), heads, layers, base, first)):
        sk[q] = value

    def strip(p, count=1):
        return strips[p * SIDE : (p + count) * SIDE, :]

    heads = [strip(M_LO)]
    for q in range(LAYERS_PER_BLOCK):
        at = H0 + HALO + 4 * q
        heads.append((strip(at) + strip(at + 1) + strip(at + 2) + strip(at + 3)) * 0.25)
    heads.append(strip(M_HI))
    base = jnp.concatenate([exp_first] * 2, axis=0)
    for q, value in enumerate(uptake_of(strip(TP), strip(RT), heads, layers, base, first)):
        ssk[q * SIDE : (q + 1) * SIDE, :] = value

    def first_curves(j, theta):
        i = j + 1
        half_n = wide(N0 + j)
        expo = expo_of(half_n)
        mm[j] = expo
        satur, cond = curves(ha[i, 8 : 8 + WIDE], wide(A0 + j), half_n, wide(S0 + j), expo)
        put(kc, i, cond)
        if theta:
            th[j - 1] = wide(P0 + j - 1) * satur

    def later_curves(src, j, water):
        i = j + 1
        satur, cond = curves(src[i, 8 : 8 + WIDE], wide(A0 + j), wide(N0 + j), wide(S0 + j), mm[j])
        put(kc, i, cond)
        if water:
            wd[j - 1] = wide(P0 + j - 1) * satur - th[j - 1]

    def stencil(src, i, sweep):
        here = pl.ds(8, WIDE)
        head, cond = src[i, here, :], kc[i, here, :]
        mask_up = jnp.where(i == HALO, z_top, 1.0)
        mask_down = jnp.where(i == HALO + LEVELS - 1, z_bottom, 1.0)
        kf_up = (cond + kc[i - 1, here, :]) * mask_up
        kf_down = (cond + kc[i + 1, here, :]) * mask_down
        kf_xm = (cond + kc[i, pl.ds(7, WIDE), :]) * xmask[0]
        kf_xp = (cond + kc[i, pl.ds(9, WIDE), :]) * xmask[1]
        kf_ym = cond + pltpu.roll(cond, 1, 1)
        kf_yp = cond + pltpu.roll(cond, COLS - 1, 1)
        flux = kf_up * (head - src[i - 1, here, :]) + kf_down * (head - src[i + 1, here, :])
        flux = flux + kf_xm * (head - src[i, pl.ds(7, WIDE), :]) + kf_xp * (head - src[i, pl.ds(9, WIDE), :])
        flux = flux + kf_ym * (head - pltpu.roll(head, 1, 1)) + kf_yp * (head - pltpu.roll(head, COLS - 1, 1))
        resid = flux + (kf_down - kf_up) + sk[(i + 1) // LEVELS_PER_LAYER]
        if sweep > 0:
            resid = resid + wd[i - 2]
        diag = 1.0 + (kf_up + kf_down + kf_xm + kf_xp + kf_ym + kf_yp)
        return head - omega(sweep) * resid / diag

    def loop(lo, hi, body):
        def step(i, carry):
            body(i)
            return carry

        lax.fori_loop(lo, hi, step, 0)

    first_curves(0, False)
    loop(1, NC - 1, lambda j: first_curves(j, True))
    first_curves(NC - 1, False)
    loop(1, NH - 1, lambda i: put(hb, i, stencil(ha, i, 0)))

    lane = lax.broadcasted_iota(jnp.int32, (SIDE, COLS), 1)
    srow = lax.broadcasted_iota(jnp.int32, (SIDE, COLS), 0)
    s_xm = jnp.where(lane == 0, x_first, 1.0)
    s_xp = jnp.where(lane == ROWS - 1, x_last, 1.0)
    side_mask = jnp.where(srow < 8, y_last, y_first)
    s_ym = jnp.where(srow % 8 == 0, side_mask, 1.0)
    s_yp = jnp.where(srow % 8 == 7, side_mask, 1.0)

    def tiled(mask, count):
        return jnp.concatenate([mask] * count, axis=0)

    def y_shift(value, by):
        parts = value.reshape(value.shape[0] // 8, 8, COLS)
        return pltpu.roll(parts, by, 1).reshape(value.shape)

    def rows_of(i, count):
        return slice(i * SIDE, (i + count) * SIDE)

    def strip_curves(src, lo, hi, sweep):
        i = lo
        while i < hi:
            count = min(5, hi - i)
            j = i - 1
            here = rows_of(i, count)
            half_n = strip(N0 + j, count)
            if sweep == 0:
                expo = expo_of(half_n)
                sm[rows_of(j, count), :] = expo
            else:
                expo = sm[rows_of(j, count), :]
            satur, cond = curves(src[here, :], strip(A0 + j, count), half_n, strip(S0 + j, count), expo)
            ks[here, :] = cond
            start, stop = max(i, 2), min(i + count, NH - 2)
            if stop > start:
                part = satur[(start - i) * SIDE : (stop - i) * SIDE]
                water = strip(P0 + start - 2, stop - start) * part
                at = rows_of(start - 2, stop - start)
                if sweep == 0:
                    sth[at, :] = water
                else:
                    swd[at, :] = water - sth[at, :]
            i += count

    def strip_stencil(src, dst, lo, hi, sweep):
        i = lo
        while i < hi:
            count = min(5, hi - i)
            here = rows_of(i, count)
            above, below = rows_of(i - 1, count), rows_of(i + 1, count)
            head, cond = src[here, :], ks[here, :]
            kf_up = cond + ks[above, :]
            kf_down = cond + ks[below, :]
            if i <= HALO < i + count:
                level = lax.broadcasted_iota(jnp.int32, kf_up.shape, 0) // SIDE
                kf_up = jnp.where(level == HALO - i, kf_up * z_top, kf_up)
            if i <= HALO + LEVELS - 1 < i + count:
                level = lax.broadcasted_iota(jnp.int32, kf_up.shape, 0) // SIDE
                kf_down = jnp.where(level == HALO + LEVELS - 1 - i, kf_down * z_bottom, kf_down)
            kf_xm = (cond + pltpu.roll(cond, 1, 1)) * tiled(s_xm, count)
            kf_xp = (cond + pltpu.roll(cond, COLS - 1, 1)) * tiled(s_xp, count)
            kf_ym = (cond + y_shift(cond, 1)) * tiled(s_ym, count)
            kf_yp = (cond + y_shift(cond, 7)) * tiled(s_yp, count)
            flux = kf_up * (head - src[above, :]) + kf_down * (head - src[below, :])
            flux = flux + kf_xm * (head - pltpu.roll(head, 1, 1)) + kf_xp * (head - pltpu.roll(head, COLS - 1, 1))
            flux = flux + kf_ym * (head - y_shift(head, 1)) + kf_yp * (head - y_shift(head, 7))
            sink = jnp.concatenate([ssk[rows_of((k + 1) // LEVELS_PER_LAYER, 1), :] for k in range(i, i + count)], axis=0)
            resid = flux + (kf_down - kf_up) + sink
            if sweep > 0:
                resid = resid + swd[rows_of(i - 2, count), :]
            diag = 1.0 + (kf_up + kf_down + kf_xm + kf_xp + kf_ym + kf_yp)
            dst[here, :] = head - omega(sweep) * resid / diag
            i += count

    ks[rows_of(0, 1), :] = strip(K_LO)
    ks[rows_of(NH - 1, 1), :] = strip(K_HI)
    strip_curves(strips, 1, NH - 1, 0)
    strip_stencil(strips, sa, 1, NH - 1, 0)
    strip_curves(sa, 1, NH - 1, 1)
    strip_stencil(sa, sb, 2, NH - 2, 1)
    strip_curves(sb, 2, NH - 2, 2)
    strip_stencil(sb, sc, 3, NH - 3, 2)

    lane_wide = lax.broadcasted_iota(jnp.int32, (WIDE, COLS), 1)
    low_rows = lax.broadcasted_iota(jnp.int32, (EDGE, COLS), 0) >= EDGE - HALO

    def turned(pieces):
        rows = sum(piece.shape[0] for piece in pieces)
        full = jnp.concatenate(pieces + [jnp.zeros((COLS - rows, COLS), f32)], axis=0).T
        last = jnp.where(low_rows, full[COLS - EDGE : COLS], full[ROWS:WIDE])
        return jnp.concatenate([full[0:ROWS], last], axis=0)

    turn[...] = turned([sa[i * SIDE + 7 : i * SIDE + 9, :] for i in range(1, NH - 1)])
    outer = (lane_wide == 0) | (lane_wide == COLS - 1)
    for i in range(1, NH - 1):
        moved = pltpu.roll(turn[...], (COLS - 1 - 2 * (i - 1)) % COLS, 1)
        put(hb, i, jnp.where(outer, moved, hb[i, 8 : 8 + WIDE]))

    loop(0, 1, lambda j: later_curves(hb, j, False))
    loop(1, NC - 1, lambda j: later_curves(hb, j, True))
    loop(NC - 1, NC, lambda j: later_curves(hb, j, False))
    loop(2, NH - 2, lambda i: put(ha, i, stencil(hb, i, 1)))
    loop(1, NC - 1, lambda j: later_curves(ha, j, True))

    turn[...] = turned([sc[i * SIDE + 6 : i * SIDE + 10, :] for i in range(HALO, HALO + LEVELS)])
    outer = ((lane_wide < 2) | (lane_wide >= COLS - 2))[0:ROWS]
    loop(HALO, HALO + LEVELS, lambda i: put(hb, i, stencil(ha, i, 2)))
    for level in range(LEVELS):
        moved = pltpu.roll(turn[0:ROWS], (COLS - 2 - 4 * level) % COLS, 1)
        out[level] = jnp.where(outer, moved, hb[HALO + level, 8 : 8 + ROWS])


def heat(count_gx, count_gz, y, temp, tr, air, rt, out, sat, head):
    me = place("gx") * count_gz + place("gz")
    layers = LAYERS_PER_BLOCK * count_gz
    for gx in range(count_gx):
        for gz in range(count_gz):
            j = me ^ (gx * count_gz + gz)
            for c in range(CAP):
                tile = y[j, c * 8 : c * 8 + 8]
                at = pl.ds(gz * LAYERS_PER_BLOCK, LAYERS_PER_BLOCK)
                sat[gx * CAP + c, at, :] = tile[0:LAYERS_PER_BLOCK]
                head[gx * CAP + c, at, :] = tile[LAYERS_PER_BLOCK : 2 * LAYERS_PER_BLOCK]
    layer = lax.broadcasted_iota(jnp.int32, (layers, COLS), 0)
    decay = jnp.exp(layer.astype(jnp.float32) * -0.25)
    for slot in range(count_gx * CAP):
        roots = jnp.broadcast_to(rt[pl.ds(slot, 1), :], (layers, COLS))
        weight = jnp.where(layer < roots, decay, 0.0)
        weight = weight / jnp.sum(weight, axis=0, keepdims=True)
        stress = 1.0 / (1.0 + head[slot] * head[slot] * (1.0 / 2.25))
        uptake = tr[pl.ds(slot, 1), :] * weight * stress
        kappa = 0.25 + 0.9 * sat[slot]
        top = jnp.broadcast_to(air[pl.ds(slot, 1), :], (layers, COLS))
        k_above = jnp.where(layer == 0, kappa, 0.5 * (kappa + pltpu.roll(kappa, 1, 0)))
        k_below = jnp.where(layer == layers - 1, 0.0, 0.5 * (kappa + pltpu.roll(kappa, layers - 1, 0)))
        old = temp[slot]
        new = old
        for _ in range(HEAT_STEPS):
            above = jnp.where(layer == 0, top, pltpu.roll(new, 1, 0))
            below = pltpu.roll(new, layers - 1, 0)
            new = new + 0.2 * (k_above * (above - new) + k_below * (below - new)) - 0.3 * uptake
        out[slot] = jnp.where(sat[slot] >= 0.0, new, old)


def call(body, outs, ins, scratch=(), aliases=None):
    return pl.pallas_call(
        body,
        out_shape=[jax.ShapeDtypeStruct(shape, jnp.float32) for shape in outs],
        in_specs=ins,
        out_specs=[VMEM] * len(outs),
        scratch_shapes=list(scratch),
        input_output_aliases=aliases or {},
        compiler_params=PARAMS,
    )


def local(h, a, n, s, p, tile_owner, land_temp, tr, air, rt):
    sizes = tuple(lax.axis_size(axis) for axis in AXES)
    count_role, count_gx, count_gz = sizes
    groups = count_gx * count_gz
    slots = count_gx * CAP
    f32 = jnp.float32

    def swap(value, axis, odd):
        return lax.ppermute(value, AXES, pairing(sizes, axis, odd))

    owners = lax.dynamic_slice(tile_owner, (place("gx") * ROWS, place("role")), (ROWS, 1))[:, 0]
    land_temp, tr, air, rt = land_temp[0, 0], tr[0, 0], air[0, 0], rt[0, 0]

    z_send_e, z_send_o = call(
        z_faces,
        [(Z_SEND, ROWS, COLS)] * 2,
        [ANY] * 5,
        [
            pltpu.VMEM((2, 4, ROWS, COLS), f32),
            pltpu.VMEM((2, 3, ROWS, COLS), f32),
            pltpu.VMEM((2, 3, ROWS, COLS), f32),
            pltpu.VMEM((2, 3, ROWS, COLS), f32),
            pltpu.VMEM((2, 1, ROWS, COLS), f32),
            pltpu.SemaphoreType.DMA((10,)),
        ],
    )(h, a, n, s, p)
    z_e = swap(z_send_e, "gz", False)
    z_o = swap(z_send_o, "gz", True) if count_gz > 2 else z_e

    y, t, planes = call(
        functools.partial(land_pack, count_gx, count_gz),
        [(groups, 8 * CAP, COLS), (count_gx, 8, COLS), (PLANES, ROWS, COLS)],
        [SMEM] + [VMEM] * 7,
        [
            pltpu.VMEM((2 * LAYERS_PER_BLOCK, ROWS, COLS), f32),
            pltpu.SMEM((groups,), jnp.int32),
            pltpu.SMEM((groups * CAP,), jnp.int32),
        ],
    )(owners, h, a, n, s, p, tr, rt)

    pieces = [y[j] for j in range(groups)]
    values = {j * count_gz: t[j] for j in range(count_gx)}
    bit = groups // 2
    while bit:
        axis, step = ("gx", bit // count_gz) if bit >= count_gz else ("gz", bit)
        moving = [j for j in range(groups) if j & bit]
        if axis == "gx":
            t_moving = [j for j in values if j & bit]
        else:
            t_moving = sorted(values)
        sent = jnp.concatenate([pieces[j] for j in moving] + [values[j] for j in t_moving], axis=0)
        got = lax.ppermute(sent, AXES, xor_pairs(sizes, axis, step))
        at = 0
        for j in moving:
            pieces[j] = got[at : at + 8 * CAP]
            at += 8 * CAP
        for j in t_moving:
            values[j | bit] = got[at : at + 8]
            at += 8
        bit //= 2
    y = jnp.stack(pieces)
    t = jnp.stack([values[j] for j in range(groups)])

    (tile,) = call(
        functools.partial(tile_values, count_gz, groups),
        [(2, ROWS, COLS)],
        [SMEM, VMEM],
        [pltpu.SMEM((groups,), jnp.int32)],
    )(owners, t)

    x_count = 1 if count_gx == 2 else 2
    planes, *x_sends = call(
        functools.partial(x_faces, count_gx),
        [(PLANES, ROWS, COLS)] + [(PLANES, 4, COLS)] * x_count,
        [VMEM] * 4,
        aliases={0: 0},
    )(planes, z_e, z_o, tile)
    x_got = [swap(value, "gx", bool(k)) for k, value in enumerate(x_sends)]

    edge, strips, y_send_e, y_send_o = call(
        functools.partial(y_faces, count_gx),
        [(PLANES, EDGE, COLS), (PACKS * COLS, COLS), (Y_SEND, COLS), (Y_SEND, COLS)],
        [VMEM] * (1 + x_count),
    )(planes, *x_got)
    y_e = swap(y_send_e, "role", False)
    y_o = swap(y_send_o, "role", True) if count_role > 2 else y_e

    (land_new,) = call(
        functools.partial(heat, count_gx, count_gz),
        [(slots, LAYERS_PER_BLOCK * count_gz, COLS)],
        [VMEM] * 5,
        [pltpu.VMEM((slots, LAYERS_PER_BLOCK * count_gz, COLS), f32)] * 2,
    )(y, land_temp, tr, air, rt)

    deep = WIDE + 16
    (head,) = call(
        functools.partial(sweeps, count_role, count_gx, count_gz),
        [(LEVELS, ROWS, COLS)],
        [VMEM] * 5,
        [
            pltpu.VMEM((PACKS * COLS, COLS), f32),
            pltpu.VMEM((NH, deep, COLS), f32),
            pltpu.VMEM((NH, deep, COLS), f32),
            pltpu.VMEM((NH, deep, COLS), f32),
            pltpu.VMEM((NC, WIDE, COLS), f32),
            pltpu.VMEM((NP, WIDE, COLS), f32),
            pltpu.VMEM((NP, WIDE, COLS), f32),
            pltpu.VMEM((LAYERS_PER_BLOCK + 2, WIDE, COLS), f32),
            pltpu.VMEM((2, WIDE, COLS), f32),
            pltpu.VMEM((NH * SIDE, COLS), f32),
            pltpu.VMEM((NH * SIDE, COLS), f32),
            pltpu.VMEM((NH * SIDE, COLS), f32),
            pltpu.VMEM((NH * SIDE, COLS), f32),
            pltpu.VMEM((NC * SIDE, COLS), f32),
            pltpu.VMEM((NP * SIDE, COLS), f32),
            pltpu.VMEM((NP * SIDE, COLS), f32),
            pltpu.VMEM(((LAYERS_PER_BLOCK + 2) * SIDE, COLS), f32),
            pltpu.VMEM((WIDE, COLS), f32),
        ],
    )(planes, edge, strips, y_e, y_o)
    return (head, land_new[None, None])


def solution(mesh):
    in_specs = (
        P("gz", "gx", "role"),
        P("gz", "gx", "role"),
        P("gz", "gx", "role"),
        P("gz", "gx", "role"),
        P("gz", "gx", "role"),
        P(),
        P("role", ("gx", "gz"), None, None, None),
        P("role", ("gx", "gz"), None, None),
        P("role", ("gx", "gz"), None, None),
        P("role", ("gx", "gz"), None, None),
    )
    out_specs = (P("gz", "gx", "role"), P("role", ("gx", "gz"), None, None, None))
    return jax.shard_map(local, mesh=mesh, in_specs=in_specs, out_specs=out_specs, check_vma=False)
```

time: 146 us -> 67.5 us (0.46)
  the two profiles are of different devices: /device:TPU:6 before, /device:TPU:2 now
where the time goes in v1:
time: 67.5 us; the launch traced here: 66.8 us
  waiting for transfers between devices  24.5 us (36%)
  Pallas kernels  21.9 us (32%)
  local copies, waits for them, and re-layouts  12 us (18%)
  starting transfers between devices  7.57 us (11%)
  between operations  0.95 us (1%)
    ppermute x3, waiting for transfers between devices, local(): got = lax.ppermute(sent, AXES, xor_pairs(sizes, axis, step))  16.1 us
    pallas_call x1, Pallas kernels, local(): call(functools.partial(sweeps, count_role, count_gx, count_gz), [(LEVELS,...  12.4 us
    unnamed x55, local copies, waits for them, and re-layouts  11.9 us
    ppermute x5, waiting for transfers between devices, swap(): return lax.ppermute(value, AXES, pairing(sizes, axis, odd))  8.39 us
    ppermute x5, starting transfers between devices, swap(): return lax.ppermute(value, AXES, pairing(sizes, axis, odd))  4.97 us
    pallas_call x1, Pallas kernels, local(): call(functools.partial(y_faces, count_gx), [(PLANES, EDGE, COLS), (PACKS...  3.33 us
    ppermute x3, starting transfers between devices, local(): got = lax.ppermute(sent, AXES, xor_pairs(sizes, axis, step))  2.59 us
    pallas_call x1, Pallas kernels, local(): call(functools.partial(land_pack, count_gx, count_gz), [(groups, 8 * CAP,...  2.39 us
  transfers between devices with their start and end apart: 8, of which 5 were waited for; matrix products, arithmetic and copies ran while one was open for 0% of the time, Pallas kernels for 5%

profile of v1, /device:TPU:2, one launch (start us, length us, event | category | flops | bytes accessed | tf_op | source)
XLA Modules:
  0.0 66.8 jit_solution(3304929521929667882)
XLA Ops:
  0.6 0.0 copy-start
  0.6 0.0 copy-start.12
  0.7 0.7 %copy.21 = f32[1,1,6,128]{3,2,1,0:T(8,128)S(1)} copy(f32[1,1,6,128]{3,1,2,0:T(1,128)} %param.17) | data formatting | bytes 6144
  1.4 0.7 %copy.20 = s32[1,1,6,128]{3,2,1,0:T(8,128)S(1)} copy(s32[1,1,6,128]{3,1,2,0:T(1,128)} %param.19) | data formatting | bytes 6144
  2.0 0.0 copy-done
  2.0 0.1 dynamic-slice_bitcast_fusion.owners
  2.1 0.0 copy-start.1
  2.1 1.0 %copy-done.1 = f32[16,64,128]{2,1,0:T(8,128)S(1)} copy-done((f32[16,64,128]{2,1,0:T(8,128)S(1)}, f32[16,64,128]{2,1,0:T(8,128)}, u32[]{:S(2)}) %copy-start.1) | copy-done | bytes 524312
  3.2 0.0 copy-start.3
  3.2 1.0 %copy-done.3 = f32[16,64,128]{2,1,0:T(8,128)S(1)} copy-done((f32[16,64,128]{2,1,0:T(8,128)S(1)}, f32[16,64,128]{2,1,0:T(8,128)}, u32[]{:S(2)}) %copy-start.3) | copy-done | bytes 524312
  4.2 0.0 copy-start.5
  4.2 1.0 %copy-done.5 = f32[16,64,128]{2,1,0:T(8,128)S(1)} copy-done((f32[16,64,128]{2,1,0:T(8,128)S(1)}, f32[16,64,128]{2,1,0:T(8,128)}, u32[]{:S(2)}) %copy-start.5) | copy-done | bytes 524312
  5.2 0.0 copy-start.7
  5.2 1.0 %copy-done.7 = f32[16,64,128]{2,1,0:T(8,128)S(1)} copy-done((f32[16,64,128]{2,1,0:T(8,128)S(1)}, f32[16,64,128]{2,1,0:T(8,128)}, u32[]{:S(2)}) %copy-start.7) | copy-done | bytes 524312
  6.3 0.0 copy-start.9
  6.3 1.0 %copy-done.9 = f32[16,64,128]{2,1,0:T(8,128)S(1)} copy-done((f32[16,64,128]{2,1,0:T(8,128)S(1)}, f32[16,64,128]{2,1,0:T(8,128)}, u32[]{:S(2)}) %copy-start.9) | copy-done | bytes 524312
  7.3 2.4 %shard_map.113 = (f32[8,24,128]{2,1,0:T(8,128)S(1)}, f32[2,8,128]{2,1,0:T(8,128)S(1)}, f32[106,64,128]{2,1,0:T(8,128)S(1)}) custom-call(s32[64]{0:T(128)S(1)} %dynamic-slice_bitcast_fusion.owners, f32[16,64,128]{2,1,0:T(8,128)S(1)} %copy-done.1, f32[16,64,128]{2,1,0:T(8,128)S(1)} %copy-done.3, f32[16,64,128]{2,1,0:T(8,128)S(1)} %copy-done.5, ...), custom_call_target="tpu_custom_call" | custom-call | tf_op jit(solution)/shard_map/pallas_call | solution.py:655
  9.8 0.1 collective-permute-start.2
  9.9 0.0 copy-start.2
  9.9 1.0 %copy-done.2 = f32[16,64,128]{2,1,0:T(8,128)S(1)} copy-done((f32[16,64,128]{2,1,0:T(8,128)S(1)}, f32[16,64,128]{2,1,0:T(8,128)}, u32[]{:S(2)}) %copy-start.2) | copy-done | bytes 524312
  10.9 0.0 copy-start.4
  10.9 1.0 %copy-done.4 = f32[16,64,128]{2,1,0:T(8,128)S(1)} copy-done((f32[16,64,128]{2,1,0:T(8,128)S(1)}, f32[16,64,128]{2,1,0:T(8,128)}, u32[]{:S(2)}) %copy-start.4) | copy-done | bytes 524312
  11.9 0.0 copy-start.6
  11.9 1.0 %copy-done.6 = f32[16,64,128]{2,1,0:T(8,128)S(1)} copy-done((f32[16,64,128]{2,1,0:T(8,128)S(1)}, f32[16,64,128]{2,1,0:T(8,128)}, u32[]{:S(2)}) %copy-start.6) | copy-done | bytes 524312
  13.0 0.0 copy-start.8
  13.0 1.0 %copy-done.8 = f32[16,64,128]{2,1,0:T(8,128)S(1)} copy-done((f32[16,64,128]{2,1,0:T(8,128)S(1)}, f32[16,64,128]{2,1,0:T(8,128)}, u32[]{:S(2)}) %copy-start.8) | copy-done | bytes 524312
  14.0 0.0 copy-start.10
  14.0 1.0 %copy-done.10 = f32[16,64,128]{2,1,0:T(8,128)S(1)} copy-done((f32[16,64,128]{2,1,0:T(8,128)S(1)}, f32[16,64,128]{2,1,0:T(8,128)}, u32[]{:S(2)}) %copy-start.10) | copy-done | bytes 524312
  15.1 1.4 %shard_map.114 = (f32[12,64,128]{2,1,0:T(8,128)S(1)}, f32[12,64,128]{2,1,0:T(8,128)S(1)}) custom-call(f32[16,64,128]{2,1,0:T(8,128)S(1)} %copy-done.2, f32[16,64,128]{2,1,0:T(8,128)S(1)} %copy-done.4, f32[16,64,128]{2,1,0:T(8,128)S(1)} %copy-done.6, f32[16,64,128]{2,1,0:T(8,128)S(1)} %copy-done.8, f32[16,64,128]{2,1,0:T(8,128)S(1)} %copy-done.10), custom_call_target="tpu_custom_call" | custom-call | tf_op jit(solution)/shard_map/pallas_call | solution.py:639
  16.4 1.6 %collective-permute-start = (f32[12,64,128]{2,1,0:T(8,128)S(1)}, f32[12,64,128]{2,1,0:T(8,128)S(1)}, u32[]{:S(2)}, u32[]{:S(2)}) collective-permute-start(f32[12,64,128]{2,1,0:T(8,128)S(1)} %get-tuple-element.14), channel_id=1, source_target_pairs={{0,1},{1,0},{2,3},{3,2},{4,5},{5,4},{6,7},{7,6},{8,9},{9,8},{10,11... | collective-permute-start | bytes 1179656 | tf_op jit(solution)/shard_map/ppermute | solution.py:634
  18.1 0.2 collective-permute-start.1
  18.3 0.0 collective-permute-done.2
  18.3 2.5 %collective-permute-start.3 = (f32[112,128]{1,0:T(8,128)S(1)}, f32[112,128]{1,0:T(8,128)S(1)}, u32[]{:S(2)}, u32[]{:S(2)}) collective-permute-start(f32[112,128]{1,0:T(8,128)S(1)} %constant_dynamic-update-slice_fusion.5), channel_id=1, source_target_pairs={{0,2},{1,3},{2,0},{3,1},{4,6},{5,7},{6,4},{7,5},{8,10},{9,11},{10,... | collective-permute-start | bytes 172040 | tf_op jit(solution)/shard_map/ppermute | solution.py:677
  20.8 11.8 %collective-permute-done.3 = f32[112,128]{1,0:T(8,128)S(1)} collective-permute-done((f32[112,128]{1,0:T(8,128)S(1)}, f32[112,128]{1,0:T(8,128)S(1)}, u32[]{:S(2)}, u32[]{:S(2)}) %collective-permute-start.3) | collective-permute-done | bytes 57376 | tf_op jit(solution)/shard_map/ppermute | solution.py:677
  32.7 0.1 collective-permute-start.4
  32.8 0.0 copy-done.12
  32.8 4.2 %collective-permute-done.4 = f32[128,128]{1,0:T(8,128)S(1)} collective-permute-done((f32[128,128]{1,0:T(8,128)S(1)}, f32[128,128]{1,0:T(8,128)S(1)}, u32[]{:S(2)}, u32[]{:S(2)}) %collective-permute-start.4) | collective-permute-done | bytes 65568 | tf_op jit(solution)/shard_map/ppermute | solution.py:677
  37.1 1.5 %shard_map.115.tile = f32[2,64,128]{2,1,0:T(8,128)S(1)} custom-call(s32[64]{0:T(128)S(1)} %dynamic-slice_bitcast_fusion.owners, f32[8,8,128]{2,1,0:T(8,128)S(1)} %constant_dynamic-update-slice_fusion.18.t), custom_call_target="tpu_custom_call" | custom-call | tf_op jit(solution)/shard_map/pallas_call | solution.py:689
  38.6 0.0 collective-permute-done.z_e
  38.6 0.0 collective-permute-done.1.z_o
  38.6 0.0 copy-start.11
  38.7 0.1 shard_map.116
  38.8 0.1 collective-permute-start.5
  38.9 1.4 %collective-permute-done.5.refs_1_ = f32[106,4,128]{2,1,0:T(4,128)S(1)} collective-permute-done((f32[106,4,128]{2,1,0:T(4,128)S(1)}, f32[106,4,128]{2,1,0:T(4,128)S(1)}, u32[]{:S(2)}, u32[]{:S(2)}) %collective-permute-start.5) | collective-permute-done | bytes 217120 | tf_op jit(solution)/shard_map/ppermute | solution.py:634
  40.3 3.3 %shard_map.117 = (f32[106,8,128]{2,1,0:T(8,128)S(1)}, f32[1792,128]{1,0:T(8,128)S(1)}, f32[320,128]{1,0:T(8,128)S(1)}, f32[320,128]{1,0:T(8,128)S(1)}) custom-call(f32[106,64,128]{2,1,0:T(8,128)S(1)} %get-tuple-element.18.refs_0_.planes, f32[106,4,128]{2,1,0:T(4,128)S(1)} %collective-permute-done.5.refs_1_), custom_call_target="tpu_custom_call" | custom-call | tf_op jit(solution)/shard_map/pallas_call | solution.py:705
  43.7 0.6 collective-permute-start.6
  44.3 2.4 %collective-permute-start.7 = (f32[320,128]{1,0:T(8,128)S(1)}, f32[320,128]{1,0:T(8,128)S(1)}, u32[]{:S(2)}, u32[]{:S(2)}) collective-permute-start(f32[320,128]{1,0:T(8,128)S(1)} %get-tuple-element.23), channel_id=1, source_target_pairs={{0,4},{1,5},{2,6},{3,7},{4,0},{5,1},{6,2},{7,3},{8,16},{9,17},{10,... | collective-permute-start | bytes 491528 | tf_op jit(solution)/shard_map/ppermute | solution.py:634
  46.7 0.0 copy-done.11
  46.7 0.8 %shard_map.119 = f32[6,16,128]{2,1,0:T(8,128)} custom-call(f32[8,24,128]{2,1,0:T(8,128)S(1)} %constant_dynamic-update-slice_fusion.26.y, f32[6,16,128]{2,1,0:T(8,128)S(1)} %bitcast.82, f32[6,128]{1,0:T(8,128)S(1)} %bitcast.84, f32[6,128]{1,0:T(8,128)S(1)} %bitcast.87, s32[6,128]{1,0:T(8,128)S(1)} %bitcast.86), custom_call_target="tpu_custom_call" | custom-call | tf_op jit(solution)/shard_map/pallas_call | solution.py:713
  47.5 2.5 %collective-permute-done.6.y_e = f32[320,128]{1,0:T(8,128)S(1)} collective-permute-done((f32[320,128]{1,0:T(8,128)S(1)}, f32[320,128]{1,0:T(8,128)S(1)}, u32[]{:S(2)}, u32[]{:S(2)}) %collective-permute-start.6) | collective-permute-done | bytes 163872 | tf_op jit(solution)/shard_map/ppermute | solution.py:634
  50.0 4.5 %collective-permute-done.7.y_o = f32[320,128]{1,0:T(8,128)S(1)} collective-permute-done((f32[320,128]{1,0:T(8,128)S(1)}, f32[320,128]{1,0:T(8,128)S(1)}, u32[]{:S(2)}, u32[]{:S(2)}) %collective-permute-start.7) | collective-permute-done | bytes 163872 | tf_op jit(solution)/shard_map/ppermute | solution.py:634
  54.5 12.4 %shard_map.118 = f32[16,64,128]{2,1,0:T(8,128)} custom-call(f32[106,64,128]{2,1,0:T(8,128)S(1)} %get-tuple-element.18.refs_0_.planes, f32[106,8,128]{2,1,0:T(8,128)S(1)} %get-tuple-element.20.edge, f32[1792,128]{1,0:T(8,128)S(1)} %get-tuple-element.21.strips_in, f32[320,128]{1,0:T(8,128)S(1)} %collective-permute-done.6.y_e, ...), custom_call_target="tpu_custom_call" | custom-call | tf_op jit(solution)/shard_map/pallas_call | solution.py:721
  (32 shorter events, 0.1 us)
Async XLA Ops:
  0.6 1.4 %copy-start = (s32[128,4]{0,1:T(4,128)S(1)}, s32[128,4]{0,1:T(4,128)}, u32[]{:S(2)}) copy-start(s32[128,4]{0,1:T(4,128)} %param.15) | copy-start | bytes 6148
  0.6 32.1 %copy-start.12 = (f32[1,1,6,128]{3,1,2,0:T(1,128)S(1)}, f32[1,1,6,128]{3,1,2,0:T(1,128)}, u32[]{:S(2)}) copy-start(f32[1,1,6,128]{3,1,2,0:T(1,128)} %param.18) | copy-start | bytes 9220
  2.1 1.0 %copy-start.1 = (f32[16,64,128]{2,1,0:T(8,128)S(1)}, f32[16,64,128]{2,1,0:T(8,128)}, u32[]{:S(2)}) copy-start(f32[16,64,128]{2,1,0:T(8,128)} %h.3) | copy-start | bytes 1572868
  3.2 1.0 %copy-start.3 = (f32[16,64,128]{2,1,0:T(8,128)S(1)}, f32[16,64,128]{2,1,0:T(8,128)}, u32[]{:S(2)}) copy-start(f32[16,64,128]{2,1,0:T(8,128)} %a.3) | copy-start | bytes 1572868
  4.2 1.0 %copy-start.5 = (f32[16,64,128]{2,1,0:T(8,128)S(1)}, f32[16,64,128]{2,1,0:T(8,128)}, u32[]{:S(2)}) copy-start(f32[16,64,128]{2,1,0:T(8,128)} %n.3) | copy-start | bytes 1572868
  5.2 1.0 %copy-start.7 = (f32[16,64,128]{2,1,0:T(8,128)S(1)}, f32[16,64,128]{2,1,0:T(8,128)}, u32[]{:S(2)}) copy-start(f32[16,64,128]{2,1,0:T(8,128)} %s.3) | copy-start | bytes 1572868
  6.3 1.0 %copy-start.9 = (f32[16,64,128]{2,1,0:T(8,128)S(1)}, f32[16,64,128]{2,1,0:T(8,128)}, u32[]{:S(2)}) copy-start(f32[16,64,128]{2,1,0:T(8,128)} %p.3) | copy-start | bytes 1572868
  9.8 8.5 %collective-permute-start.2 = (f32[104,128]{1,0:T(8,128)S(1)}, f32[104,128]{1,0:T(8,128)S(1)}, u32[]{:S(2)}, u32[]{:S(2)}) collective-permute-start(f32[104,128]{1,0:T(8,128)S(1)} %constant_dynamic-update-slice_fusion), channel_id=1, source_target_pairs={{0,4},{1,5},{2,6},{3,7},{4,0},{5,1},{6,2},{7,3},{8,12},{9,13},{10,... | collective-permute-start | bytes 159752 | tf_op jit(solution)/shard_map/ppermute | solution.py:677
  9.9 1.0 %copy-start.2 = (f32[16,64,128]{2,1,0:T(8,128)S(1)}, f32[16,64,128]{2,1,0:T(8,128)}, u32[]{:S(2)}) copy-start(f32[16,64,128]{2,1,0:T(8,128)} %h.3) | copy-start | bytes 1572868
  10.9 1.0 %copy-start.4 = (f32[16,64,128]{2,1,0:T(8,128)S(1)}, f32[16,64,128]{2,1,0:T(8,128)}, u32[]{:S(2)}) copy-start(f32[16,64,128]{2,1,0:T(8,128)} %a.3) | copy-start | bytes 1572868
  11.9 1.0 %copy-start.6 = (f32[16,64,128]{2,1,0:T(8,128)S(1)}, f32[16,64,128]{2,1,0:T(8,128)}, u32[]{:S(2)}) copy-start(f32[16,64,128]{2,1,0:T(8,128)} %n.3) | copy-start | bytes 1572868
  13.0 1.0 %copy-start.8 = (f32[16,64,128]{2,1,0:T(8,128)S(1)}, f32[16,64,128]{2,1,0:T(8,128)}, u32[]{:S(2)}) copy-start(f32[16,64,128]{2,1,0:T(8,128)} %s.3) | copy-start | bytes 1572868
  14.0 1.0 %copy-start.10 = (f32[16,64,128]{2,1,0:T(8,128)S(1)}, f32[16,64,128]{2,1,0:T(8,128)}, u32[]{:S(2)}) copy-start(f32[16,64,128]{2,1,0:T(8,128)} %p.3) | copy-start | bytes 1572868
  16.4 22.2 %collective-permute-start = (f32[12,64,128]{2,1,0:T(8,128)S(1)}, f32[12,64,128]{2,1,0:T(8,128)S(1)}, u32[]{:S(2)}, u32[]{:S(2)}) collective-permute-start(f32[12,64,128]{2,1,0:T(8,128)S(1)} %get-tuple-element.14), channel_id=1, source_target_pairs={{0,1},{1,0},{2,3},{3,2},{4,5},{5,4},{6,7},{7,6},{8,9},{9,8},{10,11... | collective-permute-start | bytes 1179656 | tf_op jit(solution)/shard_map/ppermute | solution.py:634
  18.1 20.6 %collective-permute-start.1 = (f32[12,64,128]{2,1,0:T(8,128)S(1)}, f32[12,64,128]{2,1,0:T(8,128)S(1)}, u32[]{:S(2)}, u32[]{:S(2)}) collective-permute-start(f32[12,64,128]{2,1,0:T(8,128)S(1)} %get-tuple-element.15), channel_id=1, source_target_pairs={{0,4},{1,2},{2,1},{3,7},{4,0},{5,6},{6,5},{7,3},{8,12},{9,10},{10,... | collective-permute-start | bytes 1179656 | tf_op jit(solution)/shard_map/ppermute | solution.py:634
  18.3 14.3 %collective-permute-start.3 = (f32[112,128]{1,0:T(8,128)S(1)}, f32[112,128]{1,0:T(8,128)S(1)}, u32[]{:S(2)}, u32[]{:S(2)}) collective-permute-start(f32[112,128]{1,0:T(8,128)S(1)} %constant_dynamic-update-slice_fusion.5), channel_id=1, source_target_pairs={{0,2},{1,3},{2,0},{3,1},{4,6},{5,7},{6,4},{7,5},{8,10},{9,11},{10,... | collective-permute-start | bytes 172040 | tf_op jit(solution)/shard_map/ppermute | solution.py:677
  32.7 4.3 %collective-permute-start.4 = (f32[128,128]{1,0:T(8,128)S(1)}, f32[128,128]{1,0:T(8,128)S(1)}, u32[]{:S(2)}, u32[]{:S(2)}) collective-permute-start(f32[128,128]{1,0:T(8,128)S(1)} %constant_dynamic-update-slice_fusion.10), channel_id=1, source_target_pairs={{0,1},{1,0},{2,3},{3,2},{4,5},{5,4},{6,7},{7,6},{8,9},{9,8},{10,11... | collective-permute-start | bytes 196616 | tf_op jit(solution)/shard_map/ppermute | solution.py:677
  38.6 8.1 %copy-start.11 = (f32[1,1,6,16,128]{4,3,2,1,0:T(8,128)S(1)}, f32[1,1,6,16,128]{4,3,2,1,0:T(8,128)}, u32[]{:S(2)}) copy-start(f32[1,1,6,16,128]{4,3,2,1,0:T(8,128)} %param.16) | copy-start | bytes 147460
  38.8 1.5 %collective-permute-start.5 = (f32[106,4,128]{2,1,0:T(4,128)S(1)}, f32[106,4,128]{2,1,0:T(4,128)S(1)}, u32[]{:S(2)}, u32[]{:S(2)}) collective-permute-start(f32[106,4,128]{2,1,0:T(4,128)S(1)} %get-tuple-element.19), channel_id=1, source_target_pairs={{0,4},{1,5},{2,6},{3,7},{4,0},{5,1},{6,2},{7,3},{8,12},{9,13},{10,... | collective-permute-start | bytes 651272 | tf_op jit(solution)/shard_map/ppermute | solution.py:634
  43.7 6.3 %collective-permute-start.6 = (f32[320,128]{1,0:T(8,128)S(1)}, f32[320,128]{1,0:T(8,128)S(1)}, u32[]{:S(2)}, u32[]{:S(2)}) collective-permute-start(f32[320,128]{1,0:T(8,128)S(1)} %get-tuple-element.22), channel_id=1, source_target_pairs={{0,8},{1,9},{2,10},{3,11},{4,12},{5,13},{6,14},{7,15},{8,0},{9,1},... | collective-permute-start | bytes 491528 | tf_op jit(solution)/shard_map/ppermute | solution.py:634
  44.3 10.2 %collective-permute-start.7 = (f32[320,128]{1,0:T(8,128)S(1)}, f32[320,128]{1,0:T(8,128)S(1)}, u32[]{:S(2)}, u32[]{:S(2)}) collective-permute-start(f32[320,128]{1,0:T(8,128)S(1)} %get-tuple-element.23), channel_id=1, source_target_pairs={{0,4},{1,5},{2,6},{3,7},{4,0},{5,1},{6,2},{7,3},{8,16},{9,17},{10,... | collective-permute-start | bytes 491528 | tf_op jit(solution)/shard_map/ppermute | solution.py:634

commit v2 on v1

--- a/solution.py
+++ b/solution.py
@@ -17,8 +17,8 @@
 AXES = ("role", "gx", "gz")
 VMEM = pl.BlockSpec(memory_space=pltpu.VMEM)
 SMEM = pl.BlockSpec(memory_space=pltpu.SMEM)
-ANY = pl.BlockSpec(memory_space=pl.ANY)
-PARAMS = pltpu.CompilerParams(vmem_limit_bytes=40 * 1024 * 1024)
+HBM = pl.BlockSpec(memory_space=pltpu.HBM)
+MIB = 1024 * 1024
 
 LEVELS = 16
 ROWS = 64
@@ -43,6 +43,7 @@
 PACKS = (PLANES + 7) // 8
 SIDE = 16
 Z_SEND = 12
+PIECE = 8 * CAP
 Y_SEND = (PLANES * HALO + 7) // 8 * 8
 
 
@@ -97,8 +98,18 @@
     return root * root, half_ks * root * (gap * gap)
 
 
+def inverse(value):
+    guess = pl.reciprocal(value, approx=True)
+    return guess * (2.0 - value * guess)
+
+
 def expo_of(half_n):
-    return 1.0 - 0.5 / half_n
+    return 1.0 - 0.5 * inverse(half_n)
+
+
+def relax(head, inflow, diag, sweep):
+    step = omega(sweep)
+    return (1.0 - step) * head + (step * (head + inflow)) * inverse(diag)
 
 
 def z_faces(h, a, n, s, p, out_e, out_o, hb, ab, nb, sb, pb, sem):
@@ -142,41 +153,46 @@
         put(out_o, 1)
 
 
-def rank_rows(owners, counts, groups, visit):
-    def clear(i, carry):
+def land_pack(count_gx, count_gz, owners, h_in, a_in, n_in, tr_in, rt_in, send, keep, hot,
+              means, counts, slots, h, a, n, tr, rt, sem):
+    groups = count_gx * count_gz
+    me_role, me_gx = place("role"), place("gx")
+    me = me_gx * count_gz + place("gz")
+    copies = []
+    for src, dst in ((h_in, h), (a_in, a), (n_in, n), (tr_in, tr), (rt_in, rt)):
+        copy = pltpu.make_async_copy(src, dst, sem.at[len(copies)])
+        copy.start()
+        copies.append(copy)
+
+    def clear_slot(i, carry):
+        slots[i] = -1
+        return carry
+
+    def clear_count(i, carry):
         counts[i] = 0
         return carry
 
+    lax.fori_loop(0, groups * CAP, clear_slot, 0)
+    lax.fori_loop(0, groups, clear_count, 0)
+    lane = lax.broadcasted_iota(jnp.int32, (1, groups * 8), 1)
+
     def step(x, carry):
-        owner = owners[x]
+        owner = owners[me_role, me_gx * ROWS + x]
+        safe = jnp.maximum(owner, 0)
+        rank = counts[safe]
+        at = jnp.where(owner >= 0, (me ^ owner) * 8 + 2 * rank, -1)
+        hot[pl.ds(x, 1), :] = jnp.where(lane == at, 1.0, 0.0)
 
         @pl.when(owner >= 0)
         def _():
-            rank = counts[owner]
             counts[owner] = rank + 1
-            visit(x, owner, rank)
+            slots[owner * CAP + rank] = x
 
         return carry
 
-    lax.fori_loop(0, groups, clear, 0)
     lax.fori_loop(0, ROWS, step, 0)
-
-
-def land_pack(count_gx, count_gz, owners, h, a, n, s, p, tr, rt, y, t, planes, means, counts, slots):
-    groups = count_gx * count_gz
-    me_gx = place("gx")
-    me = me_gx * count_gz + place("gz")
-
-    def clear(i, carry):
-        slots[i] = -1
-        return carry
-
-    lax.fori_loop(0, groups * CAP, clear, 0)
-
-    def visit(x, owner, rank):
-        slots[owner * CAP + rank] = x
-
-    rank_rows(owners, counts, groups, visit)
+    for copy in copies:
+        copy.wait()
     for layer in range(LAYERS_PER_BLOCK):
         saturs = []
         heads = []
@@ -190,87 +206,155 @@
             heads.append(head)
         means[layer] = (saturs[0] + saturs[1] + saturs[2] + saturs[3]) * 0.25
         means[LAYERS_PER_BLOCK + layer] = (heads[0] + heads[1] + heads[2] + heads[3]) * 0.25
+    half = groups // 2
     for j in range(groups):
+        out, k = (keep, j) if j < half else (send, j - half)
         for c in range(CAP):
             row = slots[(me ^ j) * CAP + c]
             safe = jnp.maximum(row, 0)
             for q in range(8):
                 value = means[q, pl.ds(safe, 1), :]
-                y[j, pl.ds(c * 8 + q, 1), :] = jnp.where(row >= 0, value, -1.0)
+                out[pl.ds(k * PIECE + c * 8 + q, 1), :] = jnp.where(row >= 0, value, -1.0)
+    blocks = count_gx // 2
     for j in range(count_gx):
         block = me_gx ^ j
-        t[j] = jnp.zeros((8, COLS), jnp.float32)
+        out, k = (keep, j) if j < blocks else (send, j - blocks)
+        base = half * PIECE + k * 8
+        out[pl.ds(base, 8), :] = jnp.zeros((8, COLS), jnp.float32)
         for c in range(CAP):
-            t[j, pl.ds(2 * c, 1), :] = tr[pl.ds(block * CAP + c, 1), :]
-            t[j, pl.ds(2 * c + 1, 1), :] = rt[pl.ds(block * CAP + c, 1), :].astype(jnp.float32)
-    for level in range(LEVELS):
-        planes[H0 + HALO + level] = h[level]
-        alpha = a[level]
-        planes[A0 + HALO - 1 + level] = alpha * alpha
-        planes[N0 + HALO - 1 + level] = 0.5 * n[level]
-        planes[S0 + HALO - 1 + level] = 0.5 * s[level]
-        planes[P0 + HALO - 2 + level] = p[level]
-
-
-def tile_values(count_gz, groups, owners, t, out, counts):
-    me = place("gx") * count_gz + place("gz")
-    out[0] = jnp.zeros((ROWS, COLS), jnp.float32)
-    out[1] = jnp.ones((ROWS, COLS), jnp.float32)
-
-    def visit(x, owner, rank):
-        j = me ^ owner
-        out[0, pl.ds(x, 1), :] = t[j, pl.ds(2 * rank, 1), :]
-        out[1, pl.ds(x, 1), :] = t[j, pl.ds(2 * rank + 1, 1), :]
-
-    rank_rows(owners, counts, groups, visit)
-
-
-def x_faces(count_gx, planes_in, z_e, z_o, tile, planes, *sends):
-    def take(got, low):
-        for dist in (1, 2, 3):
-            planes[H0 + (HALO - dist if low else HALO + LEVELS - 1 + dist)] = got[dist - 1]
-        for dist in (1, 2):
-            off = HALO - 1 - dist if low else HALO - 2 + LEVELS + dist
-            planes[A0 + off] = got[2 + dist]
-            planes[N0 + off] = got[4 + dist]
-            planes[S0 + off] = got[6 + dist]
-        planes[P0 + (0 if low else NP - 1)] = got[9]
-        planes[K_LO if low else K_HI] = got[10]
-        planes[M_LO if low else M_HI] = got[11]
-
-    even_z = is_even("gz")
-
-    @pl.when(even_z)
+            out[pl.ds(base + 2 * c, 1), :] = tr[block * CAP + c]
+            out[pl.ds(base + 2 * c + 1, 1), :] = rt[block * CAP + c].astype(jnp.float32)
+
+
+def land_sort(count_gx, count_gz, keep, got, *outs):
+    half, blocks = count_gx * count_gz // 2, count_gx // 2
+    for gx in range(count_gx):
+        src, k = (keep, gx) if gx < blocks else (got, gx - blocks)
+        for dist in range(count_gz):
+            at = (k * count_gz + dist) * PIECE
+            outs[dist][gx * PIECE : (gx + 1) * PIECE] = src[at : at + PIECE]
+            base = count_gx * PIECE + gx * 8
+            outs[dist][base : base + 8] = src[half * PIECE + k * 8 : half * PIECE + k * 8 + 8]
+
+
+def tile_values(count_gx, count_gz, hot, *refs):
+    parts, out = refs[:count_gz], refs[count_gz]
+    values = []
+    for gx in range(count_gx):
+        for dist in range(count_gz):
+            base = count_gx * PIECE + gx * 8
+            values.append(parts[dist][base : base + 8])
+    t = jnp.concatenate(values, axis=0)
+    out[0] = exact_dot(hot[...], t)
+    out[1] = jnp.maximum(exact_dot(hot[...], pltpu.roll(t, t.shape[0] - 1, 0)), 1.0)
+
+
+def exact_dot(hot, values):
+    total = None
+    rest = values
+    left = hot.astype(jnp.bfloat16)
+    for _ in range(3):
+        part = rest.astype(jnp.bfloat16)
+        rest = rest - part.astype(jnp.float32)
+        term = jnp.dot(left, part, preferred_element_type=jnp.float32)
+        total = term if total is None else total + term
+    return total
+
+
+def z_places(low):
+    places = [H0 + (HALO - dist if low else HALO + LEVELS - 1 + dist) for dist in (1, 2, 3)]
+    for first in (A0, N0, S0):
+        places += [first + (HALO - 1 - dist if low else HALO - 2 + LEVELS + dist) for dist in (1, 2)]
+    return places + [P0 + (0 if low else NP - 1), K_LO if low else K_HI, M_LO if low else M_HI]
+
+
+def by_parity(axis, action, first, second):
+    even = is_even(axis)
+
+    @pl.when(even)
     def _():
-        take(z_e, False)
-        take(z_o, True)
-
-    @pl.when(jnp.logical_not(even_z))
+        action(first, second)
+
+    @pl.when(jnp.logical_not(even))
     def _():
-        take(z_e, True)
-        take(z_o, False)
-
+        action(second, first)
+
+
+OWN = (H0 + HALO, A0 + HALO - 1, N0 + HALO - 1, S0 + HALO - 1, P0 + HALO - 2)
+
+
+def scaled(k, value):
+    return (value, value * value, 0.5 * value, 0.5 * value, value)[k]
+
+
+def own_edges(count_gx, *refs):
+    arrays, outs, buf, sem = refs[:5], refs[5:-2], refs[-2], refs[-1]
+    copies = []
+    for k, src in enumerate(arrays):
+        for side in range(2):
+            start = 0 if side == 0 else ROWS - 8
+            copy = pltpu.make_async_copy(src.at[:, pl.ds(start, 8), :], buf.at[side, k], sem.at[len(copies)])
+            copy.start()
+            copies.append(copy)
+    for copy in copies:
+        copy.wait()
+
+    def put(high, low):
+        for k, first in enumerate(OWN):
+            for level in range(LEVELS):
+                if high is not None:
+                    value = buf[1, k, level, pl.ds(8 - HALO, HALO), :]
+                    high[first + level, pl.ds(0, HALO), :] = scaled(k, value)
+                if low is not None:
+                    value = buf[0, k, level, pl.ds(0, HALO), :]
+                    low[first + level, pl.ds(0, HALO), :] = scaled(k, value)
+
+    by_parity("gx", put, outs[0], outs[1] if count_gx > 2 else None)
+
+
+def x_faces(count_gx, *refs):
+    z_e, z_o, tile = refs[:3]
+    sends = refs[-1:] if count_gx == 2 else refs[-2:]
+
+    def put_all(high, low):
+        def put(upper, lower):
+            for got, places in ((upper, z_places(False)), (lower, z_places(True))):
+                for k, p in enumerate(places):
+                    if high is not None:
+                        high[p, pl.ds(0, HALO), :] = got[k, pl.ds(ROWS - HALO, HALO), :]
+                    if low is not None:
+                        low[p, pl.ds(0, HALO), :] = got[k, pl.ds(0, HALO), :]
+
+        by_parity("gz", put, z_e, z_o)
+        for k in range(2):
+            if high is not None:
+                high[TP + k, pl.ds(0, HALO), :] = tile[k, pl.ds(ROWS - HALO, HALO), :]
+            if low is not None:
+                low[TP + k, pl.ds(0, HALO), :] = tile[k, pl.ds(0, HALO), :]
+
+    by_parity("gx", put_all, sends[0], sends[1] if count_gx > 2 else None)
+
+
+def all_planes(h, a, n, s, p, z_e, z_o, tile, planes, sem):
+    copies = []
+    for k, src in enumerate((h, a, n, s, p)):
+        copy = pltpu.make_async_copy(src, planes.at[pl.ds(OWN[k], LEVELS)], sem.at[k])
+        copy.start()
+        copies.append(copy)
+
+    def put(upper, lower):
+        for got, places in ((upper, z_places(False)), (lower, z_places(True))):
+            for k, p in enumerate(places):
+                planes[p] = got[k]
+
+    by_parity("gz", put, z_e, z_o)
     planes[TP] = tile[0]
     planes[RT] = tile[1]
-
-    def put(send, last):
-        start = ROWS - HALO if last else 0
-        for p in range(PLANES):
-            send[p, pl.ds(0, HALO), :] = planes[p, pl.ds(start, HALO), :]
-
-    even_x = is_even("gx")
-
-    @pl.when(even_x)
-    def _():
-        put(sends[0], True)
-        if count_gx > 2:
-            put(sends[1], False)
-
-    @pl.when(jnp.logical_not(even_x))
-    def _():
-        put(sends[0], False)
-        if count_gx > 2:
-            put(sends[1], True)
+    for copy in copies:
+        copy.wait()
+    for k in (1, 2, 3):
+        for level in range(LEVELS):
+            planes[OWN[k] + level] = scaled(k, planes[OWN[k] + level])
 
 
 def y_faces(count_gx, *refs):
@@ -348,7 +432,7 @@
 
 
 def sweeps(count_role, count_gx, count_gz, planes, edge, strips_in, y_e, y_o, out,
-           strips, ha, hb, kc, mm, th, wd, sk, xmask,
+           strips, ha, hb, kc, mm, th, wd, sk,
            sa, sb, sc, ks, sm, sth, swd, ssk, turn):
     me_role, me_gx, me_gz = place("role"), place("gx"), place("gz")
     layers = LAYERS_PER_BLOCK * count_gz
@@ -387,9 +471,9 @@
         ref[i, 0:8] = value[ROWS:WIDE]
         ref[i, 8 + WIDE : 16 + WIDE] = value[0:8]
 
-    row = lax.broadcasted_iota(jnp.int32, (WIDE, COLS), 0)
-    xmask[0] = jnp.where(row == 0, x_first, 1.0)
-    xmask[1] = jnp.where(row == ROWS - 1, x_last, 1.0)
+    row = lax.broadcasted_iota(jnp.int32, (8, COLS), 0)
+    x_low = jnp.where(row == 0, x_first, 1.0)
+    x_high = jnp.where(row == 7, x_last, 1.0)
 
     def fill(i, carry):
         put(ha, i, wide(H0 + i))
@@ -434,39 +518,54 @@
         satur, cond = curves(src[i, 8 : 8 + WIDE], wide(A0 + j), wide(N0 + j), wide(S0 + j), mm[j])
         put(kc, i, cond)
         if water:
-            wd[j - 1] = wide(P0 + j - 1) * satur - th[j - 1]
-
-    def stencil(src, i, sweep):
+            wd[j - 1] = wide(P0 + j - 1) * satur - th[j - 1] + sk[(i + 1) // LEVELS_PER_LAYER]
+
+    def stencil(src, i0, count, sweep, store):
         here = pl.ds(8, WIDE)
-        head, cond = src[i, here, :], kc[i, here, :]
-        mask_up = jnp.where(i == HALO, z_top, 1.0)
-        mask_down = jnp.where(i == HALO + LEVELS - 1, z_bottom, 1.0)
-        kf_up = (cond + kc[i - 1, here, :]) * mask_up
-        kf_down = (cond + kc[i + 1, here, :]) * mask_down
-        kf_xm = (cond + kc[i, pl.ds(7, WIDE), :]) * xmask[0]
-        kf_xp = (cond + kc[i, pl.ds(9, WIDE), :]) * xmask[1]
-        kf_ym = cond + pltpu.roll(cond, 1, 1)
-        kf_yp = cond + pltpu.roll(cond, COLS - 1, 1)
-        flux = kf_up * (head - src[i - 1, here, :]) + kf_down * (head - src[i + 1, here, :])
-        flux = flux + kf_xm * (head - src[i, pl.ds(7, WIDE), :]) + kf_xp * (head - src[i, pl.ds(9, WIDE), :])
-        flux = flux + kf_ym * (head - pltpu.roll(head, 1, 1)) + kf_yp * (head - pltpu.roll(head, COLS - 1, 1))
-        resid = flux + (kf_down - kf_up) + sk[(i + 1) // LEVELS_PER_LAYER]
-        if sweep > 0:
-            resid = resid + wd[i - 2]
-        diag = 1.0 + (kf_up + kf_down + kf_xm + kf_xp + kf_ym + kf_yp)
-        return head - omega(sweep) * resid / diag
-
-    def loop(lo, hi, body):
+        conds = [kc[i0 + g - 1, here, :] for g in range(count + 2)]
+        heads = [src[i0 + g - 1, here, :] for g in range(count + 2)]
+        faces = [conds[g] + conds[g + 1] for g in range(count + 1)]
+        faces[0] = faces[0] * jnp.where(i0 == HALO, z_top, jnp.where(i0 == HALO + LEVELS, z_bottom, 1.0))
+        end = i0 + count
+        faces[count] = faces[count] * jnp.where(
+            end == HALO, z_top, jnp.where(end == HALO + LEVELS, z_bottom, 1.0)
+        )
+        for g in range(count):
+            i = i0 + g
+            head, cond = heads[g + 1], conds[g + 1]
+            kf_up, kf_down = faces[g], faces[g + 1]
+            kf_xm = cond + kc[i, pl.ds(7, WIDE), :]
+            kf_xm = jnp.concatenate([kf_xm[0:8] * x_low, kf_xm[8:]], axis=0)
+            kf_xp = cond + kc[i, pl.ds(9, WIDE), :]
+            kf_xp = jnp.concatenate([kf_xp[: ROWS - 8], kf_xp[ROWS - 8 : ROWS] * x_high, kf_xp[ROWS:]], axis=0)
+            kf_ym = cond + pltpu.roll(cond, 1, 1)
+            kf_yp = cond + pltpu.roll(cond, COLS - 1, 1)
+            inflow = kf_up * (heads[g] + 1.0) + kf_down * (heads[g + 2] - 1.0)
+            inflow = inflow + (kf_xm * src[i, pl.ds(7, WIDE), :] + kf_xp * src[i, pl.ds(9, WIDE), :])
+            inflow = inflow + (kf_ym * pltpu.roll(head, 1, 1) + kf_yp * pltpu.roll(head, COLS - 1, 1))
+            lost = wd[i - 2] if sweep > 0 else sk[(i + 1) // LEVELS_PER_LAYER]
+            diag = (1.0 + kf_up) + (kf_down + kf_xm) + (kf_xp + kf_ym) + kf_yp
+            store(i, relax(head, inflow - lost, diag, sweep))
+
+    def loop(lo, hi, body, unroll=1):
         def step(i, carry):
             body(i)
             return carry
 
-        lax.fori_loop(lo, hi, step, 0)
+        lax.fori_loop(lo, hi, step, 0, unroll=unroll)
+
+    def levels_of(src, sweep, store):
+        extra = SWEEPS - 1 - sweep
+        if extra:
+            stencil(src, HALO - extra, extra, sweep, store)
+        loop(0, LEVELS // 4, lambda k: stencil(src, HALO + 4 * k, 4, sweep, store))
+        if extra:
+            stencil(src, HALO + LEVELS, extra, sweep, store)
 
     first_curves(0, False)
-    loop(1, NC - 1, lambda j: first_curves(j, True))
+    loop(1, NC - 1, lambda j: first_curves(j, True), 3)
     first_curves(NC - 1, False)
-    loop(1, NH - 1, lambda i: put(hb, i, stencil(ha, i, 0)))
+    levels_of(ha, 0, lambda i, value: put(hb, i, value))
 
     lane = lax.broadcasted_iota(jnp.int32, (SIDE, COLS), 1)
     srow = lax.broadcasted_iota(jnp.int32, (SIDE, COLS), 0)
@@ -530,15 +629,14 @@
             kf_xp = (cond + pltpu.roll(cond, COLS - 1, 1)) * tiled(s_xp, count)
             kf_ym = (cond + y_shift(cond, 1)) * tiled(s_ym, count)
             kf_yp = (cond + y_shift(cond, 7)) * tiled(s_yp, count)
-            flux = kf_up * (head - src[above, :]) + kf_down * (head - src[below, :])
-            flux = flux + kf_xm * (head - pltpu.roll(head, 1, 1)) + kf_xp * (head - pltpu.roll(head, COLS - 1, 1))
-            flux = flux + kf_ym * (head - y_shift(head, 1)) + kf_yp * (head - y_shift(head, 7))
-            sink = jnp.concatenate([ssk[rows_of((k + 1) // LEVELS_PER_LAYER, 1), :] for k in range(i, i + count)], axis=0)
-            resid = flux + (kf_down - kf_up) + sink
+            inflow = kf_up * (src[above, :] + 1.0) + kf_down * (src[below, :] - 1.0)
+            inflow = inflow + (kf_xm * pltpu.roll(head, 1, 1) + kf_xp * pltpu.roll(head, COLS - 1, 1))
+            inflow = inflow + (kf_ym * y_shift(head, 1) + kf_yp * y_shift(head, 7))
+            lost = jnp.concatenate([ssk[rows_of((k + 1) // LEVELS_PER_LAYER, 1), :] for k in range(i, i + count)], axis=0)
             if sweep > 0:
-                resid = resid + swd[rows_of(i - 2, count), :]
-            diag = 1.0 + (kf_up + kf_down + kf_xm + kf_xp + kf_ym + kf_yp)
-            dst[here, :] = head - omega(sweep) * resid / diag
+                lost = lost + swd[rows_of(i - 2, count), :]
+            diag = (1.0 + kf_up) + (kf_down + kf_xm) + (kf_xp + kf_ym) + kf_yp
+            dst[here, :] = relax(head, inflow - lost, diag, sweep)
             i += count
 
     ks[rows_of(0, 1), :] = strip(K_LO)
@@ -565,23 +663,39 @@
         moved = pltpu.roll(turn[...], (COLS - 1 - 2 * (i - 1)) % COLS, 1)
         put(hb, i, jnp.where(outer, moved, hb[i, 8 : 8 + WIDE]))
 
-    loop(0, 1, lambda j: later_curves(hb, j, False))
-    loop(1, NC - 1, lambda j: later_curves(hb, j, True))
-    loop(NC - 1, NC, lambda j: later_curves(hb, j, False))
-    loop(2, NH - 2, lambda i: put(ha, i, stencil(hb, i, 1)))
-    loop(1, NC - 1, lambda j: later_curves(ha, j, True))
+    later_curves(hb, 0, False)
+    loop(1, NC - 1, lambda j: later_curves(hb, j, True), 3)
+    later_curves(hb, NC - 1, False)
+    levels_of(hb, 1, lambda i, value: put(ha, i, value))
+    loop(1, NC - 1, lambda j: later_curves(ha, j, True), 3)
 
     turn[...] = turned([sc[i * SIDE + 6 : i * SIDE + 10, :] for i in range(HALO, HALO + LEVELS)])
     outer = ((lane_wide < 2) | (lane_wide >= COLS - 2))[0:ROWS]
-    loop(HALO, HALO + LEVELS, lambda i: put(hb, i, stencil(ha, i, 2)))
+    levels_of(ha, 2, lambda i, value: put(hb, i, value))
     for level in range(LEVELS):
         moved = pltpu.roll(turn[0:ROWS], (COLS - 2 - 4 * level) % COLS, 1)
         out[level] = jnp.where(outer, moved, hb[HALO + level, 8 : 8 + ROWS])
 
 
-def heat(count_gx, count_gz, y, temp, tr, air, rt, out, sat, head):
+def heat(count_gx, count_gz, *refs):
+    parts, refs = refs[:count_gz], refs[count_gz:]
+    temp_in, tr_in, air_in, rt_in, out, sat, head, temp, tr, air, rt, y, sem = refs
+    copies = []
+    for dist, part in enumerate(parts):
+        for gx in range(count_gx):
+            copy = pltpu.make_async_copy(
+                part.at[pl.ds(gx * PIECE, PIECE)], y.at[gx * count_gz + dist], sem.at[len(copies)]
+            )
+            copy.start()
+            copies.append(copy)
+    for src, dst in ((temp_in, temp), (tr_in, tr), (air_in, air), (rt_in, rt)):
+        copy = pltpu.make_async_copy(src, dst, sem.at[len(copies)])
+        copy.start()
+        copies.append(copy)
     me = place("gx") * count_gz + place("gz")
     layers = LAYERS_PER_BLOCK * count_gz
+    for copy in copies:
+        copy.wait()
     for gx in range(count_gx):
         for gz in range(count_gz):
             j = me ^ (gx * count_gz + gz)
@@ -593,13 +707,13 @@
     layer = lax.broadcasted_iota(jnp.int32, (layers, COLS), 0)
     decay = jnp.exp(layer.astype(jnp.float32) * -0.25)
     for slot in range(count_gx * CAP):
-        roots = jnp.broadcast_to(rt[pl.ds(slot, 1), :], (layers, COLS))
+        roots = jnp.broadcast_to(rt[slot], (layers, COLS))
         weight = jnp.where(layer < roots, decay, 0.0)
         weight = weight / jnp.sum(weight, axis=0, keepdims=True)
         stress = 1.0 / (1.0 + head[slot] * head[slot] * (1.0 / 2.25))
-        uptake = tr[pl.ds(slot, 1), :] * weight * stress
+        uptake = tr[slot] * weight * stress
         kappa = 0.25 + 0.9 * sat[slot]
-        top = jnp.broadcast_to(air[pl.ds(slot, 1), :], (layers, COLS))
+        top = jnp.broadcast_to(air[slot], (layers, COLS))
         k_above = jnp.where(layer == 0, kappa, 0.5 * (kappa + pltpu.roll(kappa, 1, 0)))
         k_below = jnp.where(layer == layers - 1, 0.0, 0.5 * (kappa + pltpu.roll(kappa, layers - 1, 0)))
         old = temp[slot]
@@ -611,114 +725,23 @@
         out[slot] = jnp.where(sat[slot] >= 0.0, new, old)
 
 
-def call(body, outs, ins, scratch=(), aliases=None):
+def call(body, outs, ins, scratch=(), aliases=None, limit=40 * MIB, kept=True, work=0):
     return pl.pallas_call(
         body,
-        out_shape=[jax.ShapeDtypeStruct(shape, jnp.float32) for shape in outs],
+        out_shape=[pltpu.VMEM(shape, jnp.float32) if kept else jax.ShapeDtypeStruct(shape, jnp.float32) for shape in outs],
         in_specs=ins,
         out_specs=[VMEM] * len(outs),
         scratch_shapes=list(scratch),
         input_output_aliases=aliases or {},
-        compiler_params=PARAMS,
+        compiler_params=pltpu.CompilerParams(vmem_limit_bytes=limit),
+        cost_estimate=pl.CostEstimate(flops=work, bytes_accessed=work, transcendentals=0) if work else None,
     )
 
 
-def local(h, a, n, s, p, tile_owner, land_temp, tr, air, rt):
-    sizes = tuple(lax.axis_size(axis) for axis in AXES)
-    count_role, count_gx, count_gz = sizes
-    groups = count_gx * count_gz
-    slots = count_gx * CAP
+def sweep_call(count_role, count_gx, count_gz):
     f32 = jnp.float32
-
-    def swap(value, axis, odd):
-        return lax.ppermute(value, AXES, pairing(sizes, axis, odd))
-
-    owners = lax.dynamic_slice(tile_owner, (place("gx") * ROWS, place("role")), (ROWS, 1))[:, 0]
-    land_temp, tr, air, rt = land_temp[0, 0], tr[0, 0], air[0, 0], rt[0, 0]
-
-    z_send_e, z_send_o = call(
-        z_faces,
-        [(Z_SEND, ROWS, COLS)] * 2,
-        [ANY] * 5,
-        [
-            pltpu.VMEM((2, 4, ROWS, COLS), f32),
-            pltpu.VMEM((2, 3, ROWS, COLS), f32),
-            pltpu.VMEM((2, 3, ROWS, COLS), f32),
-            pltpu.VMEM((2, 3, ROWS, COLS), f32),
-            pltpu.VMEM((2, 1, ROWS, COLS), f32),
-            pltpu.SemaphoreType.DMA((10,)),
-        ],
-    )(h, a, n, s, p)
-    z_e = swap(z_send_e, "gz", False)
-    z_o = swap(z_send_o, "gz", True) if count_gz > 2 else z_e
-
-    y, t, planes = call(
-        functools.partial(land_pack, count_gx, count_gz),
-        [(groups, 8 * CAP, COLS), (count_gx, 8, COLS), (PLANES, ROWS, COLS)],
-        [SMEM] + [VMEM] * 7,
-        [
-            pltpu.VMEM((2 * LAYERS_PER_BLOCK, ROWS, COLS), f32),
-            pltpu.SMEM((groups,), jnp.int32),
-            pltpu.SMEM((groups * CAP,), jnp.int32),
-        ],
-    )(owners, h, a, n, s, p, tr, rt)
-
-    pieces = [y[j] for j in range(groups)]
-    values = {j * count_gz: t[j] for j in range(count_gx)}
-    bit = groups // 2
-    while bit:
-        axis, step = ("gx", bit // count_gz) if bit >= count_gz else ("gz", bit)
-        moving = [j for j in range(groups) if j & bit]
-        if axis == "gx":
-            t_moving = [j for j in values if j & bit]
-        else:
-            t_moving = sorted(values)
-        sent = jnp.concatenate([pieces[j] for j in moving] + [values[j] for j in t_moving], axis=0)
-        got = lax.ppermute(sent, AXES, xor_pairs(sizes, axis, step))
-        at = 0
-        for j in moving:
-            pieces[j] = got[at : at + 8 * CAP]
-            at += 8 * CAP
-        for j in t_moving:
-            values[j | bit] = got[at : at + 8]
-            at += 8
-        bit //= 2
-    y = jnp.stack(pieces)
-    t = jnp.stack([values[j] for j in range(groups)])
-
-    (tile,) = call(
-        functools.partial(tile_values, count_gz, groups),
-        [(2, ROWS, COLS)],
-        [SMEM, VMEM],
-        [pltpu.SMEM((groups,), jnp.int32)],
-    )(owners, t)
-
-    x_count = 1 if count_gx == 2 else 2
-    planes, *x_sends = call(
-        functools.partial(x_faces, count_gx),
-        [(PLANES, ROWS, COLS)] + [(PLANES, 4, COLS)] * x_count,
-        [VMEM] * 4,
-        aliases={0: 0},
-    )(planes, z_e, z_o, tile)
-    x_got = [swap(value, "gx", bool(k)) for k, value in enumerate(x_sends)]
-
-    edge, strips, y_send_e, y_send_o = call(
-        functools.partial(y_faces, count_gx),
-        [(PLANES, EDGE, COLS), (PACKS * COLS, COLS), (Y_SEND, COLS), (Y_SEND, COLS)],
-        [VMEM] * (1 + x_count),
-    )(planes, *x_got)
-    y_e = swap(y_send_e, "role", False)
-    y_o = swap(y_send_o, "role", True) if count_role > 2 else y_e
-
-    (land_new,) = call(
-        functools.partial(heat, count_gx, count_gz),
-        [(slots, LAYERS_PER_BLOCK * count_gz, COLS)],
-        [VMEM] * 5,
-        [pltpu.VMEM((slots, LAYERS_PER_BLOCK * count_gz, COLS), f32)] * 2,
-    )(y, land_temp, tr, air, rt)
-
     deep = WIDE + 16
-    (head,) = call(
+    return call(
         functools.partial(sweeps, count_role, count_gx, count_gz),
         [(LEVELS, ROWS, COLS)],
         [VMEM] * 5,
@@ -731,7 +754,6 @@
             pltpu.VMEM((NP, WIDE, COLS), f32),
             pltpu.VMEM((NP, WIDE, COLS), f32),
             pltpu.VMEM((LAYERS_PER_BLOCK + 2, WIDE, COLS), f32),
-            pltpu.VMEM((2, WIDE, COLS), f32),
             pltpu.VMEM((NH * SIDE, COLS), f32),
             pltpu.VMEM((NH * SIDE, COLS), f32),
             pltpu.VMEM((NH * SIDE, COLS), f32),
@@ -742,7 +764,153 @@
             pltpu.VMEM(((LAYERS_PER_BLOCK + 2) * SIDE, COLS), f32),
             pltpu.VMEM((WIDE, COLS), f32),
         ],
-    )(planes, edge, strips, y_e, y_o)
+        kept=False,
+    )
+
+
+def local(h, a, n, s, p, tile_owner, land_temp, tr, air, rt):
+    sizes = tuple(lax.axis_size(axis) for axis in AXES)
+    count_role, count_gx, count_gz = sizes
+    groups = count_gx * count_gz
+    slots = count_gx * CAP
+    f32 = jnp.float32
+
+    def swap(value, axis, odd):
+        return lax.ppermute(value, AXES, pairing(sizes, axis, odd))
+
+    owners = tile_owner.T
+    land = (land_temp[0, 0], tr[0, 0, :, None], air[0, 0, :, None], rt[0, 0, :, None])
+    h, a, n, s, p = (pltpu.with_memory_space_constraint(x, pltpu.HBM) for x in (h, a, n, s, p))
+    land_temp, tr, air, rt = (pltpu.with_memory_space_constraint(x, pltpu.HBM) for x in land)
+
+    z_send_e, z_send_o = call(
+        z_faces,
+        [(Z_SEND, ROWS, COLS)] * 2,
+        [HBM] * 5,
+        [
+            pltpu.VMEM((2, 4, ROWS, COLS), f32),
+            pltpu.VMEM((2, 3, ROWS, COLS), f32),
+            pltpu.VMEM((2, 3, ROWS, COLS), f32),
+            pltpu.VMEM((2, 3, ROWS, COLS), f32),
+            pltpu.VMEM((2, 1, ROWS, COLS), f32),
+            pltpu.SemaphoreType.DMA((10,)),
+        ],
+    )(h, a, n, s, p)
+    z_e = swap(z_send_e, "gz", False)
+    z_o = swap(z_send_o, "gz", True) if count_gz > 2 else z_e
+
+    half = groups // 2
+    blocks = count_gx // 2
+    packed = half * 8 * CAP + blocks * 8
+    def land_stage():
+        send, keep, hot = call(
+            functools.partial(land_pack, count_gx, count_gz),
+            [(packed, COLS), (packed, COLS), (ROWS, groups * 8)],
+            [SMEM] + [HBM] * 5,
+            [
+                pltpu.VMEM((2 * LAYERS_PER_BLOCK, ROWS, COLS), f32),
+                pltpu.SMEM((groups,), jnp.int32),
+                pltpu.SMEM((groups * CAP,), jnp.int32),
+                pltpu.VMEM((LEVELS, ROWS, COLS), f32),
+                pltpu.VMEM((LEVELS, ROWS, COLS), f32),
+                pltpu.VMEM((LEVELS, ROWS, COLS), f32),
+                pltpu.VMEM((slots, 1, COLS), f32),
+                pltpu.VMEM((slots, 1, COLS), jnp.int32),
+                pltpu.SemaphoreType.DMA((5,)),
+            ],
+        )(owners, h, a, n, tr, rt)
+
+        got = lax.ppermute(send, AXES, xor_pairs(sizes, "gx", blocks))
+        bit = blocks // 2
+        if bit:
+            pieces = [part[j * PIECE : (j + 1) * PIECE] for part in (keep, got) for j in range(half)]
+            base = half * PIECE
+            values = [part[base + j * 8 : base + (j + 1) * 8] for part in (keep, got) for j in range(blocks)]
+            while bit:
+                moving = [j for j in range(groups) if (j // count_gz) & bit]
+                t_moving = [j for j in range(count_gx) if j & bit]
+                sent = jnp.concatenate([pieces[j] for j in moving] + [values[j] for j in t_moving], axis=0)
+                got = lax.ppermute(sent, AXES, xor_pairs(sizes, "gx", bit))
+                for k, j in enumerate(moving):
+                    pieces[j] = got[k * PIECE : (k + 1) * PIECE]
+                for k, j in enumerate(t_moving):
+                    base = len(moving) * PIECE + k * 8
+                    values[j] = got[base : base + 8]
+                bit //= 2
+            keep = jnp.concatenate(pieces[:half] + values[:blocks], axis=0)
+            got = jnp.concatenate(pieces[half:] + values[blocks:], axis=0)
+        parts = call(
+            functools.partial(land_sort, count_gx, count_gz),
+            [(count_gx * (PIECE + 8), COLS)] * count_gz,
+            [VMEM] * 2,
+        )(keep, got)
+        parts = [parts[0]] + [
+            lax.ppermute(parts[dist], AXES, xor_pairs(sizes, "gz", dist)) for dist in range(1, count_gz)
+        ]
+        (tile,) = call(
+            functools.partial(tile_values, count_gx, count_gz),
+            [(2, ROWS, COLS)],
+            [VMEM] * (1 + count_gz),
+        )(hot, *parts)
+        return [tile] + parts
+
+    def no_land_stage():
+        shapes = [(2, ROWS, COLS)] + [(count_gx * (PIECE + 8), COLS)] * count_gz
+        return [jnp.zeros(shape, f32) for shape in shapes]
+
+    ahead = lax.optimization_barrier(jnp.bool_(True))
+    tile, *parts = lax.cond(ahead, land_stage, no_land_stage)
+    parts = [pltpu.with_memory_space_constraint(x, pltpu.HBM) for x in parts]
+
+    x_count = 1 if count_gx == 2 else 2
+    x_shape = (PLANES, 4, COLS)
+    edges = call(
+        functools.partial(own_edges, count_gx),
+        [x_shape] * x_count,
+        [HBM] * 5,
+        [pltpu.VMEM((2, 5, LEVELS, 8, COLS), f32), pltpu.SemaphoreType.DMA((10,))],
+    )(h, a, n, s, p)
+    x_sends = call(
+        functools.partial(x_faces, count_gx),
+        [x_shape] * x_count,
+        [VMEM] * (3 + x_count),
+        aliases={3 + k: k for k in range(x_count)},
+    )(z_e, z_o, tile, *edges)
+    (planes,) = call(
+        all_planes,
+        [(PLANES, ROWS, COLS)],
+        [HBM] * 5 + [VMEM] * 3,
+        [pltpu.SemaphoreType.DMA((5,))],
+    )(h, a, n, s, p, z_e, z_o, tile)
+    x_got = [swap(value, "gx", bool(k)) for k, value in enumerate(x_sends)]
+
+    edge, strips, y_send_e, y_send_o = call(
+        functools.partial(y_faces, count_gx),
+        [(PLANES, EDGE, COLS), (PACKS * COLS, COLS), (Y_SEND, COLS), (Y_SEND, COLS)],
+        [VMEM] * (1 + x_count),
+    )(planes, *x_got)
+    y_e = swap(y_send_e, "role", False)
+    y_o = swap(y_send_o, "role", True) if count_role > 2 else y_e
+
+    land_shape = (slots, LAYERS_PER_BLOCK * count_gz, COLS)
+    (land_new,) = call(
+        functools.partial(heat, count_gx, count_gz),
+        [land_shape],
+        [HBM] * (count_gz + 4),
+        [
+            pltpu.VMEM(land_shape, f32),
+            pltpu.VMEM(land_shape, f32),
+            pltpu.VMEM(land_shape, f32),
+            pltpu.VMEM((slots, 1, COLS), f32),
+            pltpu.VMEM((slots, 1, COLS), f32),
+            pltpu.VMEM((slots, 1, COLS), jnp.int32),
+            pltpu.VMEM((groups, PIECE, COLS), f32),
+            pltpu.SemaphoreType.DMA((4 + groups,)),
+        ],
+        kept=False,
+    )(*parts, land_temp, tr, air, rt)
+
+    (head,) = sweep_call(count_role, count_gx, count_gz)(planes, edge, strips, y_e, y_o)
     return (head, land_new[None, None])
 
 

time: 67.5 us -> 45.3 us (0.67)
  waiting for transfers between devices: 24.5 us -> 10.8 us
  local copies, waits for them, and re-layouts: 12 us -> 0.01 us
  starting transfers between devices: 7.57 us -> 10.7 us
  Pallas kernels: 21.9 us -> 22.7 us
    unnamed x55 -> x2, local copies, waits for them, and re-layouts: 11.9 us -> 0.01 us
    ppermute x3 -> x4, waiting for transfers between devices: 16.1 us -> 4.49 us  [the longest x3 3.6 us: land_stage(): lax.ppermute(parts[dist], AXES, xor_pairs(sizes, 'gz', dist))]
    ppermute x3 -> x4, starting transfers between devices: 2.59 us -> 5.93 us  [the longest x3 5.36 us: land_stage(): lax.ppermute(parts[dist], AXES, xor_pairs(sizes, 'gz', dist))]
    ppermute x5, waiting for transfers between devices: 8.39 us -> 6.27 us  [swap(): return lax.ppermute(value, AXES, pairing(sizes, axis, odd))]
    pallas_call x6 -> x9, Pallas kernels: 18.5 us -> 19.3 us  [the longest x1 8.77 us: local(): sweep_call(count_role, count_gx, count_gz)(planes, edge, strips, y_e, y_o)]
  transfers between devices with their start and end apart: 8 -> 9, of which waited for: 5 -> 5; matrix products, arithmetic and copies ran while one was open for 0% -> 0% of each run, Pallas kernels for 5% -> 20%
where the time goes in v2:
time: 45.3 us; the launch traced here: 44.9 us
  Pallas kernels  22.7 us (50%)
  waiting for transfers between devices  10.8 us (24%)
  starting transfers between devices  10.7 us (24%)
  between operations  0.74 us (2%)
    pallas_call x1, Pallas kernels, local(): sweep_call(count_role, count_gx, count_gz)(planes, edge, strips, y_e, y_o)  8.77 us
    ppermute x5, waiting for transfers between devices, swap(): return lax.ppermute(value, AXES, pairing(sizes, axis, odd))  6.27 us
    ppermute x3, starting transfers between devices, land_stage(): lax.ppermute(parts[dist], AXES, xor_pairs(sizes, 'gz', dist))  5.36 us
    ppermute x5, starting transfers between devices, swap(): return lax.ppermute(value, AXES, pairing(sizes, axis, odd))  4.76 us
    ppermute x3, waiting for transfers between devices, land_stage(): lax.ppermute(parts[dist], AXES, xor_pairs(sizes, 'gz', dist))  3.6 us
    pallas_call x1, Pallas kernels, local(): call(functools.partial(y_faces, count_gx), [(PLANES, EDGE, COLS), (PACKS...  3.34 us
    pallas_call x1, Pallas kernels, land_stage(): call(functools.partial(land_pack, count_gx, count_gz), [(packed, COLS), (...  2.58 us
    pallas_call x1, Pallas kernels, local(): call(all_planes, [(PLANES, ROWS, COLS)], [HBM] * 5 + [VMEM] * 3, [pltpu.S...  1.82 us
  transfers between devices with their start and end apart: 9, of which 5 were waited for; matrix products, arithmetic and copies ran while one was open for 0% of the time, Pallas kernels for 20%

profile of v2, /device:TPU:2, one launch (start us, length us, event | category | flops | bytes accessed | tf_op | source)
XLA Modules:
  0.0 44.9 jit_solution(14395347048935902061)
XLA Ops:
  0.6 0.0 copy-start
  0.6 1.5 %shard_map.113 = (f32[12,64,128]{2,1,0:T(8,128)S(1)}, f32[12,64,128]{2,1,0:T(8,128)S(1)}) custom-call(f32[16,64,128]{2,1,0:T(8,128)} %refs_0_.1, f32[16,64,128]{2,1,0:T(8,128)} %refs_1_.1, f32[16,64,128]{2,1,0:T(8,128)} %refs_2_.1, f32[16,64,128]{2,1,0:T(8,128)} %refs_3_.1, f32[16,64,128]{2,1,0:T(8,128)} %refs_4_.1), custom_call_target="tpu_custom_call" | custom-call | tf_op jit(solution)/shard_map/pallas_call | solution.py:786
  2.1 1.6 %collective-permute-start.4 = (f32[12,64,128]{2,1,0:T(8,128)S(1)}, f32[12,64,128]{2,1,0:T(8,128)S(1)}, u32[]{:S(2)}, u32[]{:S(2)}) collective-permute-start(f32[12,64,128]{2,1,0:T(8,128)S(1)} %get-tuple-element.38), channel_id=1, source_target_pairs={{0,1},{1,0},{2,3},{3,2},{4,5},{5,4},{6,7},{7,6},{8,9},{9,8},{10,11... | collective-permute-start | bytes 1179656 | tf_op jit(solution)/shard_map/ppermute | solution.py:779
  3.7 0.0 collective-permute-start.5
  3.7 1.2 %shard_map.115.refs_3_ = f32[106,4,128]{2,1,0:T(4,128)S(1)} custom-call(f32[16,64,128]{2,1,0:T(8,128)} %refs_0_.1, f32[16,64,128]{2,1,0:T(8,128)} %refs_1_.1, f32[16,64,128]{2,1,0:T(8,128)} %refs_2_.1, f32[16,64,128]{2,1,0:T(8,128)} %refs_3_.1, f32[16,64,128]{2,1,0:T(8,128)} %refs_4_.1), custom_call_target="tpu_custom_call" | custom-call | tf_op jit(solution)/shard_map/pallas_call | solution.py:867
  5.0 0.0 copy-done
  5.0 14.6 %conditional.1 = (f32[2,64,128]{2,1,0:T(8,128)S(1)}, f32[64,128]{1,0:T(8,128)}, f32[64,128]{1,0:T(8,128)}, f32[64,128]{1,0:T(8,128)}, f32[64,128]{1,0:T(8,128)}) conditional(s32[]{:T(128)} %convert_element_type.3, () %tuple.16, (s32[4,128]{1,0:T(4,128)S(1)}, f32[16,64,128]{2,1,0:T(8,128)}, f32[16,64,128]{2,1,0:T(8,128)}, f32[16,64,128]{2,1,0:T(8,128)}, ...), branch_computations={%region_0.0_spmd, %region_1.0_spmd} | conditional | bytes 606408 | solution.py:862
  5.0 2.6 %branch_1_fun.3 = (f32[104,128]{1,0:T(8,128)S(1)}, f32[104,128]{1,0:T(8,128)S(1)}, f32[64,64]{1,0:T(8,128)S(1)}) custom-call(s32[4,128]{1,0:T(4,128)S(1)} %get-tuple-element.12.owners, f32[16,64,128]{2,1,0:T(8,128)} %get-tuple-element.13.h_in, f32[16,64,128]{2,1,0:T(8,128)} %get-tuple-element.14.a_in, f32[16,64,128]{2,1,0:T(8,128)} %get-tuple-element.15.n_in, ...), custom_call_target="tpu_custom_call" | custom-call | tf_op jit(solution)/shard_map/cond/branch_1_fun/pallas_call | solution.py:806
  7.6 0.6 %collective-permute-start = (f32[104,128]{1,0:T(8,128)S(1)}, f32[104,128]{1,0:T(8,128)S(1)}, u32[]{:S(2)}, u32[]{:S(2)}) collective-permute-start(f32[104,128]{1,0:T(8,128)S(1)} %get-tuple-element.20), channel_id=1, source_target_pairs={{0,4},{1,5},{2,6},{3,7},{4,0},{5,1},{6,2},{7,3},{8,12},{9,13},{10,... | collective-permute-start | bytes 159752 | tf_op jit(solution)/shard_map/cond/branch_1_fun/ppermute | solution.py:823
  8.2 0.9 %collective-permute-done.got = f32[104,128]{1,0:T(8,128)S(1)} collective-permute-done((f32[104,128]{1,0:T(8,128)S(1)}, f32[104,128]{1,0:T(8,128)S(1)}, u32[]{:S(2)}, u32[]{:S(2)}) %collective-permute-start) | collective-permute-done | bytes 53280 | tf_op jit(solution)/shard_map/cond/branch_1_fun/ppermute | solution.py:823
  9.1 0.6 %branch_1_fun.4 = (f32[64,128]{1,0:T(8,128)}, f32[64,128]{1,0:T(8,128)S(1)}, f32[64,128]{1,0:T(8,128)S(1)}, f32[64,128]{1,0:T(8,128)S(1)}) custom-call(f32[104,128]{1,0:T(8,128)S(1)} %get-tuple-element.19.keep, f32[104,128]{1,0:T(8,128)S(1)} %collective-permute-done.got), custom_call_target="tpu_custom_call" | custom-call | tf_op jit(solution)/shard_map/cond/branch_1_fun/pallas_call | solution.py:842
  9.7 3.0 %collective-permute-start.1 = (f32[64,128]{1,0:T(8,128)S(1)}, f32[64,128]{1,0:T(8,128)}, u32[]{:S(2)}, u32[]{:S(2)}) collective-permute-start(f32[64,128]{1,0:T(8,128)S(1)} %get-tuple-element.22), channel_id=1, source_target_pairs={{0,1},{1,0},{2,3},{3,2},{4,5},{5,4},{6,7},{7,6},{8,9},{9,8},{10,11... | collective-permute-start | bytes 98312 | tf_op jit(solution)/shard_map/cond/branch_1_fun/ppermute | solution.py:848
  12.7 0.0 collective-permute-start.2
  12.7 2.3 %collective-permute-start.3 = (f32[64,128]{1,0:T(8,128)S(1)}, f32[64,128]{1,0:T(8,128)}, u32[]{:S(2)}, u32[]{:S(2)}) collective-permute-start(f32[64,128]{1,0:T(8,128)S(1)} %get-tuple-element.24), channel_id=1, source_target_pairs={{0,3},{1,2},{2,1},{3,0},{4,7},{5,6},{6,5},{7,4},{8,11},{9,10},{10,... | collective-permute-start | bytes 98312 | tf_op jit(solution)/shard_map/cond/branch_1_fun/ppermute | solution.py:848
  15.0 0.0 collective-permute-done.1.refs_1_
  15.0 2.9 %collective-permute-done.2.refs_2_ = f32[64,128]{1,0:T(8,128)} collective-permute-done((f32[64,128]{1,0:T(8,128)S(1)}, f32[64,128]{1,0:T(8,128)}, u32[]{:S(2)}, u32[]{:S(2)}) %collective-permute-start.2) | collective-permute-done | bytes 32800 | tf_op jit(solution)/shard_map/cond/branch_1_fun/ppermute | solution.py:848
  18.0 0.7 %collective-permute-done.3.refs_3_ = f32[64,128]{1,0:T(8,128)} collective-permute-done((f32[64,128]{1,0:T(8,128)S(1)}, f32[64,128]{1,0:T(8,128)}, u32[]{:S(2)}, u32[]{:S(2)}) %collective-permute-start.3) | collective-permute-done | bytes 32800 | tf_op jit(solution)/shard_map/cond/branch_1_fun/ppermute | solution.py:848
  18.6 1.0 %branch_1_fun.5 = f32[2,64,128]{2,1,0:T(8,128)S(1)} custom-call(f32[64,64]{1,0:T(8,128)S(1)} %get-tuple-element.18.hot, f32[64,128]{1,0:T(8,128)} %get-tuple-element.55.refs_0_, f32[64,128]{1,0:T(8,128)} %collective-permute-done.1.refs_1_, f32[64,128]{1,0:T(8,128)} %collective-permute-done.2.refs_2_, f32[64,128]{1,0:T(8,128)} %collective-permute-done.3.refs_3_), custom_call_target="tpu_custom_call" | custom-call | tf_op jit(solution)/shard_map/cond/branch_1_fun/pallas_call | solution.py:850
  19.6 0.0 collective-permute-done.4.z_e.refs_0_
  19.6 0.0 collective-permute-done.5.z_o.refs_1_
  19.7 0.1 collective-permute-start.6
  19.8 1.8 %shard_map.114.refs_0_.planes = f32[106,64,128]{2,1,0:T(8,128)S(1)} custom-call(f32[16,64,128]{2,1,0:T(8,128)} %refs_0_.1, f32[16,64,128]{2,1,0:T(8,128)} %refs_1_.1, f32[16,64,128]{2,1,0:T(8,128)} %refs_2_.1, f32[16,64,128]{2,1,0:T(8,128)} %refs_3_.1, f32[16,64,128]{2,1,0:T(8,128)} %refs_4_.1, f32[12,64,128]{2,1,0:T(8,128)S(1)} %collective-permute-done.4.z_e.refs_0_, ...), custom_call_target="tpu_custom_call" | custom-call | tf_op jit(solution)/shard_map/pallas_call | solution.py:879
  21.6 0.0 collective-permute-done.6.refs_1_
  21.6 3.3 %shard_map.117 = (f32[106,8,128]{2,1,0:T(8,128)S(1)}, f32[1792,128]{1,0:T(8,128)S(1)}, f32[320,128]{1,0:T(8,128)S(1)}, f32[320,128]{1,0:T(8,128)S(1)}) custom-call(f32[106,64,128]{2,1,0:T(8,128)S(1)} %shard_map.114.refs_0_.planes, f32[106,4,128]{2,1,0:T(4,128)S(1)} %collective-permute-done.6.refs_1_), custom_call_target="tpu_custom_call" | custom-call | tf_op jit(solution)/shard_map/pallas_call | solution.py:887
  25.0 0.6 %collective-permute-start.7 = (f32[320,128]{1,0:T(8,128)S(1)}, f32[320,128]{1,0:T(8,128)S(1)}, u32[]{:S(2)}, u32[]{:S(2)}) collective-permute-start(f32[320,128]{1,0:T(8,128)S(1)} %get-tuple-element.43), channel_id=1, source_target_pairs={{0,8},{1,9},{2,10},{3,11},{4,12},{5,13},{6,14},{7,15},{8,0},{9,1},... | collective-permute-start | bytes 491528 | tf_op jit(solution)/shard_map/ppermute | solution.py:779
  25.6 2.4 %collective-permute-start.8 = (f32[320,128]{1,0:T(8,128)S(1)}, f32[320,128]{1,0:T(8,128)S(1)}, u32[]{:S(2)}, u32[]{:S(2)}) collective-permute-start(f32[320,128]{1,0:T(8,128)S(1)} %get-tuple-element.44), channel_id=1, source_target_pairs={{0,4},{1,5},{2,6},{3,7},{4,0},{5,1},{6,2},{7,3},{8,16},{9,17},{10,... | collective-permute-start | bytes 491528 | tf_op jit(solution)/shard_map/ppermute | solution.py:779
  28.0 1.8 %shard_map.119 = f32[6,16,128]{2,1,0:T(8,128)} custom-call(f32[64,128]{1,0:T(8,128)} %get-tuple-element.45.refs_0_, f32[64,128]{1,0:T(8,128)} %get-tuple-element.46.refs_1_, f32[64,128]{1,0:T(8,128)} %get-tuple-element.47.refs_2_, f32[64,128]{1,0:T(8,128)} %get-tuple-element.48.refs_3_, f32[6,16,128]{2,1,0:T(8,128)} %bitcast.6, f32[6,1,128]{2,1,0:T(1,128)} %bitcast.9, ...), custom_call_target="tpu_custom_call" | custom-call | tf_op jit(solution)/shard_map/pallas_call | solution.py:896
  29.8 1.8 %collective-permute-done.7.y_e = f32[320,128]{1,0:T(8,128)S(1)} collective-permute-done((f32[320,128]{1,0:T(8,128)S(1)}, f32[320,128]{1,0:T(8,128)S(1)}, u32[]{:S(2)}, u32[]{:S(2)}) %collective-permute-start.7) | collective-permute-done | bytes 163872 | tf_op jit(solution)/shard_map/ppermute | solution.py:779
  31.6 4.5 %collective-permute-done.8.y_o = f32[320,128]{1,0:T(8,128)S(1)} collective-permute-done((f32[320,128]{1,0:T(8,128)S(1)}, f32[320,128]{1,0:T(8,128)S(1)}, u32[]{:S(2)}, u32[]{:S(2)}) %collective-permute-start.8) | collective-permute-done | bytes 163872 | tf_op jit(solution)/shard_map/ppermute | solution.py:779
  36.1 8.8 %shard_map.118 = f32[16,64,128]{2,1,0:T(8,128)} custom-call(f32[106,64,128]{2,1,0:T(8,128)S(1)} %shard_map.114.refs_0_.planes, f32[106,8,128]{2,1,0:T(8,128)S(1)} %get-tuple-element.41.edge, f32[1792,128]{1,0:T(8,128)S(1)} %get-tuple-element.42.strips_in, f32[320,128]{1,0:T(8,128)S(1)} %collective-permute-done.7.y_e, f32[320,128]{1,0:T(8,128)S(1)} %collective-permute-done.8.y_o), custom_call_target="tpu_custom_call" | custom-call | tf_op jit(solution)/shard_map/pallas_call | solution.py:913
  (1 shorter events, 0.0 us)
Async XLA Ops:
  0.6 4.4 %copy-start = (s32[128,4]{0,1:T(4,128)S(1)}, s32[128,4]{0,1:T(4,128)}, u32[]{:S(2)}) copy-start(s32[128,4]{0,1:T(4,128)} %param.17) | copy-start | bytes 6148
  2.1 17.5 %collective-permute-start.4 = (f32[12,64,128]{2,1,0:T(8,128)S(1)}, f32[12,64,128]{2,1,0:T(8,128)S(1)}, u32[]{:S(2)}, u32[]{:S(2)}) collective-permute-start(f32[12,64,128]{2,1,0:T(8,128)S(1)} %get-tuple-element.38), channel_id=1, source_target_pairs={{0,1},{1,0},{2,3},{3,2},{4,5},{5,4},{6,7},{7,6},{8,9},{9,8},{10,11... | collective-permute-start | bytes 1179656 | tf_op jit(solution)/shard_map/ppermute | solution.py:779
  3.7 15.9 %collective-permute-start.5 = (f32[12,64,128]{2,1,0:T(8,128)S(1)}, f32[12,64,128]{2,1,0:T(8,128)S(1)}, u32[]{:S(2)}, u32[]{:S(2)}) collective-permute-start(f32[12,64,128]{2,1,0:T(8,128)S(1)} %get-tuple-element.39), channel_id=1, source_target_pairs={{0,4},{1,2},{2,1},{3,7},{4,0},{5,6},{6,5},{7,3},{8,12},{9,10},{10,... | collective-permute-start | bytes 1179656 | tf_op jit(solution)/shard_map/ppermute | solution.py:779
  7.6 1.5 %collective-permute-start = (f32[104,128]{1,0:T(8,128)S(1)}, f32[104,128]{1,0:T(8,128)S(1)}, u32[]{:S(2)}, u32[]{:S(2)}) collective-permute-start(f32[104,128]{1,0:T(8,128)S(1)} %get-tuple-element.20), channel_id=1, source_target_pairs={{0,4},{1,5},{2,6},{3,7},{4,0},{5,1},{6,2},{7,3},{8,12},{9,13},{10,... | collective-permute-start | bytes 159752 | tf_op jit(solution)/shard_map/cond/branch_1_fun/ppermute | solution.py:823
  9.7 5.4 %collective-permute-start.1 = (f32[64,128]{1,0:T(8,128)S(1)}, f32[64,128]{1,0:T(8,128)}, u32[]{:S(2)}, u32[]{:S(2)}) collective-permute-start(f32[64,128]{1,0:T(8,128)S(1)} %get-tuple-element.22), channel_id=1, source_target_pairs={{0,1},{1,0},{2,3},{3,2},{4,5},{5,4},{6,7},{7,6},{8,9},{9,8},{10,11... | collective-permute-start | bytes 98312 | tf_op jit(solution)/shard_map/cond/branch_1_fun/ppermute | solution.py:848
  12.7 5.3 %collective-permute-start.2 = (f32[64,128]{1,0:T(8,128)S(1)}, f32[64,128]{1,0:T(8,128)}, u32[]{:S(2)}, u32[]{:S(2)}) collective-permute-start(f32[64,128]{1,0:T(8,128)S(1)} %get-tuple-element.23), channel_id=1, source_target_pairs={{0,2},{1,3},{2,0},{3,1},{4,6},{5,7},{6,4},{7,5},{8,10},{9,11},{10,... | collective-permute-start | bytes 98312 | tf_op jit(solution)/shard_map/cond/branch_1_fun/ppermute | solution.py:848
  12.7 5.9 %collective-permute-start.3 = (f32[64,128]{1,0:T(8,128)S(1)}, f32[64,128]{1,0:T(8,128)}, u32[]{:S(2)}, u32[]{:S(2)}) collective-permute-start(f32[64,128]{1,0:T(8,128)S(1)} %get-tuple-element.24), channel_id=1, source_target_pairs={{0,3},{1,2},{2,1},{3,0},{4,7},{5,6},{6,5},{7,4},{8,11},{9,10},{10,... | collective-permute-start | bytes 98312 | tf_op jit(solution)/shard_map/cond/branch_1_fun/ppermute | solution.py:848
  19.7 1.9 %collective-permute-start.6 = (f32[106,4,128]{2,1,0:T(4,128)S(1)}, f32[106,4,128]{2,1,0:T(4,128)S(1)}, u32[]{:S(2)}, u32[]{:S(2)}) collective-permute-start(f32[106,4,128]{2,1,0:T(4,128)S(1)} %shard_map.116), channel_id=1, source_target_pairs={{0,4},{1,5},{2,6},{3,7},{4,0},{5,1},{6,2},{7,3},{8,12},{9,13},{10,... | collective-permute-start | bytes 651272 | tf_op jit(solution)/shard_map/ppermute | solution.py:779
  25.0 6.7 %collective-permute-start.7 = (f32[320,128]{1,0:T(8,128)S(1)}, f32[320,128]{1,0:T(8,128)S(1)}, u32[]{:S(2)}, u32[]{:S(2)}) collective-permute-start(f32[320,128]{1,0:T(8,128)S(1)} %get-tuple-element.43), channel_id=1, source_target_pairs={{0,8},{1,9},{2,10},{3,11},{4,12},{5,13},{6,14},{7,15},{8,0},{9,1},... | collective-permute-start | bytes 491528 | tf_op jit(solution)/shard_map/ppermute | solution.py:779
  25.6 10.5 %collective-permute-start.8 = (f32[320,128]{1,0:T(8,128)S(1)}, f32[320,128]{1,0:T(8,128)S(1)}, u32[]{:S(2)}, u32[]{:S(2)}) collective-permute-start(f32[320,128]{1,0:T(8,128)S(1)} %get-tuple-element.44), channel_id=1, source_target_pairs={{0,4},{1,5},{2,6},{3,7},{4,0},{5,1},{6,2},{7,3},{8,16},{9,17},{10,... | collective-permute-start | bytes 491528 | tf_op jit(solution)/shard_map/ppermute | solution.py:779

commit v3 on v2

--- a/solution.py
+++ b/solution.py
@@ -42,6 +42,7 @@
 PLANES = RT + 1
 PACKS = (PLANES + 7) // 8
 SIDE = 16
+NEAR = 4
 Z_SEND = 12
 PIECE = 8 * CAP
 Y_SEND = (PLANES * HALO + 7) // 8 * 8
@@ -431,37 +432,35 @@
     return result
 
 
-def sweeps(count_role, count_gx, count_gz, planes, edge, strips_in, y_e, y_o, out,
-           strips, ha, hb, kc, mm, th, wd, sk,
-           sa, sb, sc, ks, sm, sth, swd, ssk, turn):
-    me_role, me_gx, me_gz = place("role"), place("gx"), place("gz")
-    layers = LAYERS_PER_BLOCK * count_gz
-    first = me_gz * LAYERS_PER_BLOCK
-    f32 = jnp.float32
-    z_top = jnp.where(me_gz == 0, 0.0, 1.0).astype(f32)
-    z_bottom = jnp.where(me_gz == count_gz - 1, 0.0, 1.0).astype(f32)
-    x_first = jnp.where(me_gx == 0, 0.0, 1.0).astype(f32)
-    x_last = jnp.where(me_gx == count_gx - 1, 0.0, 1.0).astype(f32)
-    y_first = jnp.where(me_role == 0, 0.0, 1.0).astype(f32)
-    y_last = jnp.where(me_role == count_role - 1, 0.0, 1.0).astype(f32)
-    exp_first = jnp.exp(jnp.zeros((8, COLS), f32) - me_gz.astype(f32))
-
-    strips[...] = strips_in[...]
-
-    def take(high, low):
-        for p in range(PLANES):
-            strips[pl.ds(p * SIDE, HALO), :] = high[pl.ds(p * HALO, HALO), :]
-            strips[pl.ds(p * SIDE + SIDE - HALO, HALO), :] = low[pl.ds(p * HALO, HALO), :]
-
-    even_y = is_even("role")
-
-    @pl.when(even_y)
-    def _():
-        take(y_e, y_o)
-
-    @pl.when(jnp.logical_not(even_y))
-    def _():
-        take(y_o, y_e)
+def inner_lane(k):
+    return k // 9 * 18 + k % 9
+
+
+class Where:
+    def __init__(self, count_role, count_gx, count_gz):
+        me_role, me_gx, me_gz = place("role"), place("gx"), place("gz")
+        f32 = jnp.float32
+        self.layers = LAYERS_PER_BLOCK * count_gz
+        self.first = me_gz * LAYERS_PER_BLOCK
+        self.z_top = jnp.where(me_gz == 0, 0.0, 1.0).astype(f32)
+        self.z_bottom = jnp.where(me_gz == count_gz - 1, 0.0, 1.0).astype(f32)
+        self.x_first = jnp.where(me_gx == 0, 0.0, 1.0).astype(f32)
+        self.x_last = jnp.where(me_gx == count_gx - 1, 0.0, 1.0).astype(f32)
+        self.y_first = jnp.where(me_role == 0, 0.0, 1.0).astype(f32)
+        self.y_last = jnp.where(me_role == count_role - 1, 0.0, 1.0).astype(f32)
+        self.exp_first = jnp.exp(jnp.zeros((8, COLS), f32) - me_gz.astype(f32))
+
+
+def widened(value):
+    return jnp.concatenate([value] + [value[ROWS:WIDE]] * ((COLS - WIDE) // EDGE), axis=0)
+
+
+def main_region(count_role, count_gx, count_gz, planes, edge, *refs):
+    land_in, refs = refs[: count_gz + 4], refs[count_gz + 4 :]
+    out, inner, land_out, ha, hb, kc, mm, th, wd, sk = refs[:10]
+    heat_finish = heat(count_gx, count_gz, *land_in, land_out, *refs[10:])
+    spot = Where(count_role, count_gx, count_gz)
+    z_top, z_bottom = spot.z_top, spot.z_bottom
 
     def wide(p):
         return jnp.concatenate([planes[p], edge[p]], axis=0)
@@ -472,8 +471,8 @@
         ref[i, 8 + WIDE : 16 + WIDE] = value[0:8]
 
     row = lax.broadcasted_iota(jnp.int32, (8, COLS), 0)
-    x_low = jnp.where(row == 0, x_first, 1.0)
-    x_high = jnp.where(row == 7, x_last, 1.0)
+    x_low = jnp.where(row == 0, spot.x_first, 1.0)
+    x_high = jnp.where(row == 7, spot.x_last, 1.0)
 
     def fill(i, carry):
         put(ha, i, wide(H0 + i))
@@ -487,21 +486,9 @@
         return (ref[i, 8 : 8 + WIDE] + ref[i + 1, 8 : 8 + WIDE] + ref[i + 2, 8 : 8 + WIDE] + ref[i + 3, 8 : 8 + WIDE]) * 0.25
 
     heads = [wide(M_LO)] + [mean4(ha, HALO + 4 * q) for q in range(LAYERS_PER_BLOCK)] + [wide(M_HI)]
-    base = jnp.concatenate([exp_first] * (WIDE // 8), axis=0)
-    for q, value in enumerate(uptake_of(wide(TP), wide(RT), heads, layers, base, first)):
+    base = jnp.concatenate([spot.exp_first] * (WIDE // 8), axis=0)
+    for q, value in enumerate(uptake_of(wide(TP), wide(RT), heads, spot.layers, base, spot.first)):
         sk[q] = value
-
-    def strip(p, count=1):
-        return strips[p * SIDE : (p + count) * SIDE, :]
-
-    heads = [strip(M_LO)]
-    for q in range(LAYERS_PER_BLOCK):
-        at = H0 + HALO + 4 * q
-        heads.append((strip(at) + strip(at + 1) + strip(at + 2) + strip(at + 3)) * 0.25)
-    heads.append(strip(M_HI))
-    base = jnp.concatenate([exp_first] * 2, axis=0)
-    for q, value in enumerate(uptake_of(strip(TP), strip(RT), heads, layers, base, first)):
-        ssk[q * SIDE : (q + 1) * SIDE, :] = value
 
     def first_curves(j, theta):
         i = j + 1
@@ -567,11 +554,58 @@
     first_curves(NC - 1, False)
     levels_of(ha, 0, lambda i, value: put(hb, i, value))
 
+    lane_wide = lax.broadcasted_iota(jnp.int32, (WIDE, COLS), 1)
+    acc = jnp.zeros((WIDE, COLS), jnp.float32)
+    for k in range(NC):
+        lane = inner_lane(k)
+        pick = (lane_wide == lane) | (lane_wide == lane + 9)
+        acc = jnp.where(pick, pltpu.roll(hb[k + 1, 8 : 8 + WIDE], (lane - (COLS - 1 - NEAR)) % COLS, 1), acc)
+    inner[...] = widened(acc).T
+
+    later_curves(hb, 0, False)
+    loop(1, NC - 1, lambda j: later_curves(hb, j, True), 3)
+    later_curves(hb, NC - 1, False)
+    levels_of(hb, 1, lambda i, value: put(ha, i, value))
+    loop(1, NC - 1, lambda j: later_curves(ha, j, True), 3)
+
+    def keep(i, value):
+        out[i - HALO] = value[0:ROWS]
+
+    levels_of(ha, 2, keep)
+    heat_finish()
+
+
+def edge_strips(count_role, count_gx, count_gz, main, inner, strips_in, y_e, y_o, out,
+                strips, sa, sb, sc, ks, sm, sth, swd, ssk, turn, done, sem):
+    spot = Where(count_role, count_gx, count_gz)
+    z_top, z_bottom = spot.z_top, spot.z_bottom
+    f32 = jnp.float32
+    strips[...] = strips_in[...]
+
+    def take(high, low):
+        for p in range(PLANES):
+            strips[pl.ds(p * SIDE, HALO), :] = high[pl.ds(p * HALO, HALO), :]
+            strips[pl.ds(p * SIDE + SIDE - HALO, HALO), :] = low[pl.ds(p * HALO, HALO), :]
+
+    by_parity("role", take, y_e, y_o)
+
+    def strip(p, count=1):
+        return strips[p * SIDE : (p + count) * SIDE, :]
+
+    heads = [strip(M_LO)]
+    for q in range(LAYERS_PER_BLOCK):
+        at = H0 + HALO + 4 * q
+        heads.append((strip(at) + strip(at + 1) + strip(at + 2) + strip(at + 3)) * 0.25)
+    heads.append(strip(M_HI))
+    base = jnp.concatenate([spot.exp_first] * 2, axis=0)
+    for q, value in enumerate(uptake_of(strip(TP), strip(RT), heads, spot.layers, base, spot.first)):
+        ssk[q * SIDE : (q + 1) * SIDE, :] = value
+
     lane = lax.broadcasted_iota(jnp.int32, (SIDE, COLS), 1)
     srow = lax.broadcasted_iota(jnp.int32, (SIDE, COLS), 0)
-    s_xm = jnp.where(lane == 0, x_first, 1.0)
-    s_xp = jnp.where(lane == ROWS - 1, x_last, 1.0)
-    side_mask = jnp.where(srow < 8, y_last, y_first)
+    s_xm = jnp.where(lane == 0, spot.x_first, 1.0)
+    s_xp = jnp.where(lane == ROWS - 1, spot.x_last, 1.0)
+    side_mask = jnp.where(srow < 8, spot.y_last, spot.y_first)
     s_ym = jnp.where(srow % 8 == 0, side_mask, 1.0)
     s_yp = jnp.where(srow % 8 == 7, side_mask, 1.0)
 
@@ -643,38 +677,29 @@
     ks[rows_of(NH - 1, 1), :] = strip(K_HI)
     strip_curves(strips, 1, NH - 1, 0)
     strip_stencil(strips, sa, 1, NH - 1, 0)
+    for k in range(NC):
+        lane = inner_lane(k)
+        sa[pl.ds((k + 1) * SIDE + 3, 1), :] = inner[pl.ds(lane, 1), :]
+        sa[pl.ds((k + 1) * SIDE + 8 + NEAR, 1), :] = inner[pl.ds(lane + 9, 1), :]
     strip_curves(sa, 1, NH - 1, 1)
     strip_stencil(sa, sb, 2, NH - 2, 1)
     strip_curves(sb, 2, NH - 2, 2)
     strip_stencil(sb, sc, 3, NH - 3, 2)
 
-    lane_wide = lax.broadcasted_iota(jnp.int32, (WIDE, COLS), 1)
-    low_rows = lax.broadcasted_iota(jnp.int32, (EDGE, COLS), 0) >= EDGE - HALO
-
-    def turned(pieces):
-        rows = sum(piece.shape[0] for piece in pieces)
-        full = jnp.concatenate(pieces + [jnp.zeros((COLS - rows, COLS), f32)], axis=0).T
-        last = jnp.where(low_rows, full[COLS - EDGE : COLS], full[ROWS:WIDE])
-        return jnp.concatenate([full[0:ROWS], last], axis=0)
-
-    turn[...] = turned([sa[i * SIDE + 7 : i * SIDE + 9, :] for i in range(1, NH - 1)])
-    outer = (lane_wide == 0) | (lane_wide == COLS - 1)
-    for i in range(1, NH - 1):
-        moved = pltpu.roll(turn[...], (COLS - 1 - 2 * (i - 1)) % COLS, 1)
-        put(hb, i, jnp.where(outer, moved, hb[i, 8 : 8 + WIDE]))
-
-    later_curves(hb, 0, False)
-    loop(1, NC - 1, lambda j: later_curves(hb, j, True), 3)
-    later_curves(hb, NC - 1, False)
-    levels_of(hb, 1, lambda i, value: put(ha, i, value))
-    loop(1, NC - 1, lambda j: later_curves(ha, j, True), 3)
-
-    turn[...] = turned([sc[i * SIDE + 6 : i * SIDE + 10, :] for i in range(HALO, HALO + LEVELS)])
-    outer = ((lane_wide < 2) | (lane_wide >= COLS - 2))[0:ROWS]
-    levels_of(ha, 2, lambda i, value: put(hb, i, value))
+    pieces = [sc[i * SIDE + 8 - HALO : i * SIDE + 8 + HALO, :] for i in range(HALO, HALO + LEVELS)]
+    pieces.append(jnp.zeros((COLS - 2 * HALO * LEVELS, COLS), f32))
+    turn[...] = jnp.concatenate(pieces, axis=0).T[0:ROWS]
+    lane_rows = lax.broadcasted_iota(jnp.int32, (ROWS, COLS), 1)
+    outer = (lane_rows < HALO) | (lane_rows >= COLS - HALO)
+    copies = []
     for level in range(LEVELS):
-        moved = pltpu.roll(turn[0:ROWS], (COLS - 2 - 4 * level) % COLS, 1)
-        out[level] = jnp.where(outer, moved, hb[HALO + level, 8 : 8 + ROWS])
+        moved = pltpu.roll(turn[...], (COLS - HALO - 2 * HALO * level) % COLS, 1)
+        done[level] = jnp.where(outer, moved, main[level])
+        copy = pltpu.make_async_copy(done.at[level], out.at[level], sem.at[level])
+        copy.start()
+        copies.append(copy)
+    for copy in copies:
+        copy.wait()
 
 
 def heat(count_gx, count_gz, *refs):
@@ -692,37 +717,40 @@
         copy = pltpu.make_async_copy(src, dst, sem.at[len(copies)])
         copy.start()
         copies.append(copy)
-    me = place("gx") * count_gz + place("gz")
-    layers = LAYERS_PER_BLOCK * count_gz
-    for copy in copies:
-        copy.wait()
-    for gx in range(count_gx):
-        for gz in range(count_gz):
-            j = me ^ (gx * count_gz + gz)
-            for c in range(CAP):
-                tile = y[j, c * 8 : c * 8 + 8]
-                at = pl.ds(gz * LAYERS_PER_BLOCK, LAYERS_PER_BLOCK)
-                sat[gx * CAP + c, at, :] = tile[0:LAYERS_PER_BLOCK]
-                head[gx * CAP + c, at, :] = tile[LAYERS_PER_BLOCK : 2 * LAYERS_PER_BLOCK]
-    layer = lax.broadcasted_iota(jnp.int32, (layers, COLS), 0)
-    decay = jnp.exp(layer.astype(jnp.float32) * -0.25)
-    for slot in range(count_gx * CAP):
-        roots = jnp.broadcast_to(rt[slot], (layers, COLS))
-        weight = jnp.where(layer < roots, decay, 0.0)
-        weight = weight / jnp.sum(weight, axis=0, keepdims=True)
-        stress = 1.0 / (1.0 + head[slot] * head[slot] * (1.0 / 2.25))
-        uptake = tr[slot] * weight * stress
-        kappa = 0.25 + 0.9 * sat[slot]
-        top = jnp.broadcast_to(air[slot], (layers, COLS))
-        k_above = jnp.where(layer == 0, kappa, 0.5 * (kappa + pltpu.roll(kappa, 1, 0)))
-        k_below = jnp.where(layer == layers - 1, 0.0, 0.5 * (kappa + pltpu.roll(kappa, layers - 1, 0)))
-        old = temp[slot]
-        new = old
-        for _ in range(HEAT_STEPS):
-            above = jnp.where(layer == 0, top, pltpu.roll(new, 1, 0))
-            below = pltpu.roll(new, layers - 1, 0)
-            new = new + 0.2 * (k_above * (above - new) + k_below * (below - new)) - 0.3 * uptake
-        out[slot] = jnp.where(sat[slot] >= 0.0, new, old)
+    def finish():
+        me = place("gx") * count_gz + place("gz")
+        layers = LAYERS_PER_BLOCK * count_gz
+        for copy in copies:
+            copy.wait()
+        for gx in range(count_gx):
+            for gz in range(count_gz):
+                j = me ^ (gx * count_gz + gz)
+                for c in range(CAP):
+                    tile = y[j, c * 8 : c * 8 + 8]
+                    at = pl.ds(gz * LAYERS_PER_BLOCK, LAYERS_PER_BLOCK)
+                    sat[gx * CAP + c, at, :] = tile[0:LAYERS_PER_BLOCK]
+                    head[gx * CAP + c, at, :] = tile[LAYERS_PER_BLOCK : 2 * LAYERS_PER_BLOCK]
+        layer = lax.broadcasted_iota(jnp.int32, (layers, COLS), 0)
+        decay = jnp.exp(layer.astype(jnp.float32) * -0.25)
+        for slot in range(count_gx * CAP):
+            roots = jnp.broadcast_to(rt[slot], (layers, COLS))
+            weight = jnp.where(layer < roots, decay, 0.0)
+            weight = weight / jnp.sum(weight, axis=0, keepdims=True)
+            stress = 1.0 / (1.0 + head[slot] * head[slot] * (1.0 / 2.25))
+            uptake = tr[slot] * weight * stress
+            kappa = 0.25 + 0.9 * sat[slot]
+            top = jnp.broadcast_to(air[slot], (layers, COLS))
+            k_above = jnp.where(layer == 0, kappa, 0.5 * (kappa + pltpu.roll(kappa, 1, 0)))
+            k_below = jnp.where(layer == layers - 1, 0.0, 0.5 * (kappa + pltpu.roll(kappa, layers - 1, 0)))
+            old = temp[slot]
+            new = old
+            for _ in range(HEAT_STEPS):
+                above = jnp.where(layer == 0, top, pltpu.roll(new, 1, 0))
+                below = pltpu.roll(new, layers - 1, 0)
+                new = new + 0.2 * (k_above * (above - new) + k_below * (below - new)) - 0.3 * uptake
+            out[slot] = jnp.where(sat[slot] >= 0.0, new, old)
+
+    return finish
 
 
 def call(body, outs, ins, scratch=(), aliases=None, limit=40 * MIB, kept=True, work=0):
@@ -738,15 +766,22 @@
     )
 
 
-def sweep_call(count_role, count_gx, count_gz):
+def main_call(count_role, count_gx, count_gz):
     f32 = jnp.float32
     deep = WIDE + 16
-    return call(
-        functools.partial(sweeps, count_role, count_gx, count_gz),
-        [(LEVELS, ROWS, COLS)],
-        [VMEM] * 5,
-        [
-            pltpu.VMEM((PACKS * COLS, COLS), f32),
+    slots = count_gx * CAP
+    land_shape = (slots, LAYERS_PER_BLOCK * count_gz, COLS)
+    groups = count_gx * count_gz
+    return pl.pallas_call(
+        functools.partial(main_region, count_role, count_gx, count_gz),
+        out_shape=[
+            pltpu.VMEM((LEVELS, ROWS, COLS), f32),
+            pltpu.VMEM((COLS, COLS), f32),
+            jax.ShapeDtypeStruct(land_shape, f32),
+        ],
+        in_specs=[VMEM] * 2 + [HBM] * (count_gz + 4),
+        out_specs=[VMEM] * 3,
+        scratch_shapes=[
             pltpu.VMEM((NH, deep, COLS), f32),
             pltpu.VMEM((NH, deep, COLS), f32),
             pltpu.VMEM((NH, deep, COLS), f32),
@@ -754,6 +789,28 @@
             pltpu.VMEM((NP, WIDE, COLS), f32),
             pltpu.VMEM((NP, WIDE, COLS), f32),
             pltpu.VMEM((LAYERS_PER_BLOCK + 2, WIDE, COLS), f32),
+            pltpu.VMEM(land_shape, f32),
+            pltpu.VMEM(land_shape, f32),
+            pltpu.VMEM(land_shape, f32),
+            pltpu.VMEM((slots, 1, COLS), f32),
+            pltpu.VMEM((slots, 1, COLS), f32),
+            pltpu.VMEM((slots, 1, COLS), jnp.int32),
+            pltpu.VMEM((groups, PIECE, COLS), f32),
+            pltpu.SemaphoreType.DMA((4 + groups,)),
+        ],
+        compiler_params=pltpu.CompilerParams(vmem_limit_bytes=40 * MIB),
+    )
+
+
+def strip_call(count_role, count_gx, count_gz):
+    f32 = jnp.float32
+    return pl.pallas_call(
+        functools.partial(edge_strips, count_role, count_gx, count_gz),
+        out_shape=jax.ShapeDtypeStruct((LEVELS, ROWS, COLS), f32),
+        in_specs=[VMEM] * 5,
+        out_specs=HBM,
+        scratch_shapes=[
+            pltpu.VMEM((PACKS * COLS, COLS), f32),
             pltpu.VMEM((NH * SIDE, COLS), f32),
             pltpu.VMEM((NH * SIDE, COLS), f32),
             pltpu.VMEM((NH * SIDE, COLS), f32),
@@ -762,9 +819,11 @@
             pltpu.VMEM((NP * SIDE, COLS), f32),
             pltpu.VMEM((NP * SIDE, COLS), f32),
             pltpu.VMEM(((LAYERS_PER_BLOCK + 2) * SIDE, COLS), f32),
-            pltpu.VMEM((WIDE, COLS), f32),
+            pltpu.VMEM((ROWS, COLS), f32),
+            pltpu.VMEM((LEVELS, ROWS, COLS), f32),
+            pltpu.SemaphoreType.DMA((LEVELS,)),
         ],
-        kept=False,
+        compiler_params=pltpu.CompilerParams(vmem_limit_bytes=40 * MIB),
     )
 
 
@@ -892,25 +951,8 @@
     y_e = swap(y_send_e, "role", False)
     y_o = swap(y_send_o, "role", True) if count_role > 2 else y_e
 
-    land_shape = (slots, LAYERS_PER_BLOCK * count_gz, COLS)
-    (land_new,) = call(
-        functools.partial(heat, count_gx, count_gz),
-        [land_shape],
-        [HBM] * (count_gz + 4),
-        [
-            pltpu.VMEM(land_shape, f32),
-            pltpu.VMEM(land_shape, f32),
-            pltpu.VMEM(land_shape, f32),
-            pltpu.VMEM((slots, 1, COLS), f32),
-            pltpu.VMEM((slots, 1, COLS), f32),
-            pltpu.VMEM((slots, 1, COLS), jnp.int32),
-            pltpu.VMEM((groups, PIECE, COLS), f32),
-            pltpu.SemaphoreType.DMA((4 + groups,)),
-        ],
-        kept=False,
-    )(*parts, land_temp, tr, air, rt)
-
-    (head,) = sweep_call(count_role, count_gx, count_gz)(planes, edge, strips, y_e, y_o)
+    main, inner, land_new = main_call(*sizes)(planes, edge, *parts, land_temp, tr, air, rt)
+    head = strip_call(*sizes)(main, inner, strips, y_e, y_o)
     return (head, land_new[None, None])
 
 

time: 45.3 us -> 38.8 us (0.86)
  waiting for transfers between devices: 10.8 us -> 5.1 us
  Pallas kernels: 22.7 us -> 22 us
    ppermute x5, waiting for transfers between devices: 6.27 us -> 0.61 us  [swap(): return lax.ppermute(value, AXES, pairing(sizes, axis, odd))]
    pallas_call x2, Pallas kernels: 10.6 us -> 9.86 us  [the longest x1 7.47 us: local(): main_call(*sizes)(planes, edge, *parts, land_temp, tr, air, rt)]
  transfers between devices with their start and end apart: 9 -> 9, of which waited for: 5 -> 4; matrix products, arithmetic and copies ran while one was open for 0% -> 0% of each run, Pallas kernels for 20% -> 38%
where the time goes in v3:
time: 38.8 us; the launch traced here: 38.5 us
  Pallas kernels  22 us (57%)
  starting transfers between devices  10.7 us (28%)
  waiting for transfers between devices  5.1 us (13%)
  between operations  0.74 us (2%)
    pallas_call x1, Pallas kernels, local(): main_call(*sizes)(planes, edge, *parts, land_temp, tr, air, rt)  7.47 us
    ppermute x3, starting transfers between devices, land_stage(): lax.ppermute(parts[dist], AXES, xor_pairs(sizes, 'gz', dist))  5.36 us
    ppermute x5, starting transfers between devices, swap(): return lax.ppermute(value, AXES, pairing(sizes, axis, odd))  4.76 us
    ppermute x3, waiting for transfers between devices, land_stage(): lax.ppermute(parts[dist], AXES, xor_pairs(sizes, 'gz', dist))  3.6 us
    pallas_call x1, Pallas kernels, local(): call(functools.partial(y_faces, count_gx), [(PLANES, EDGE, COLS), (PACKS...  3.36 us
    pallas_call x1, Pallas kernels, land_stage(): call(functools.partial(land_pack, count_gx, count_gz), [(packed, COLS), (...  2.58 us
    pallas_call x1, Pallas kernels, local(): head = strip_call(*sizes)(main, inner, strips, y_e, y_o)  2.4 us
    pallas_call x1, Pallas kernels, local(): call(all_planes, [(PLANES, ROWS, COLS)], [HBM] * 5 + [VMEM] * 3, [pltpu.S...  1.82 us
  transfers between devices with their start and end apart: 9, of which 4 were waited for; matrix products, arithmetic and copies ran while one was open for 0% of the time, Pallas kernels for 38%

profile of v3, /device:TPU:2, one launch (start us, length us, event | category | flops | bytes accessed | tf_op | source)
XLA Modules:
  0.0 38.5 jit_solution(5269342890877781353)
XLA Ops:
  0.6 0.0 copy-start
  0.6 1.5 %shard_map.113 = (f32[12,64,128]{2,1,0:T(8,128)S(1)}, f32[12,64,128]{2,1,0:T(8,128)S(1)}) custom-call(f32[16,64,128]{2,1,0:T(8,128)} %refs_0_.1, f32[16,64,128]{2,1,0:T(8,128)} %refs_1_.1, f32[16,64,128]{2,1,0:T(8,128)} %refs_2_.1, f32[16,64,128]{2,1,0:T(8,128)} %refs_3_.1, f32[16,64,128]{2,1,0:T(8,128)} %refs_4_.1), custom_call_target="tpu_custom_call" | custom-call | tf_op jit(solution)/shard_map/pallas_call | solution.py:845
  2.1 1.6 %collective-permute-start.4 = (f32[12,64,128]{2,1,0:T(8,128)S(1)}, f32[12,64,128]{2,1,0:T(8,128)S(1)}, u32[]{:S(2)}, u32[]{:S(2)}) collective-permute-start(f32[12,64,128]{2,1,0:T(8,128)S(1)} %get-tuple-element.41), channel_id=1, source_target_pairs={{0,1},{1,0},{2,3},{3,2},{4,5},{5,4},{6,7},{7,6},{8,9},{9,8},{10,11... | collective-permute-start | bytes 1179656 | tf_op jit(solution)/shard_map/ppermute | solution.py:838
  3.7 0.0 collective-permute-start.5
  3.7 1.2 %shard_map.115.refs_3_ = f32[106,4,128]{2,1,0:T(4,128)S(1)} custom-call(f32[16,64,128]{2,1,0:T(8,128)} %refs_0_.1, f32[16,64,128]{2,1,0:T(8,128)} %refs_1_.1, f32[16,64,128]{2,1,0:T(8,128)} %refs_2_.1, f32[16,64,128]{2,1,0:T(8,128)} %refs_3_.1, f32[16,64,128]{2,1,0:T(8,128)} %refs_4_.1), custom_call_target="tpu_custom_call" | custom-call | tf_op jit(solution)/shard_map/pallas_call | solution.py:926
  5.0 0.0 copy-done
  5.0 14.6 %conditional.1 = (f32[2,64,128]{2,1,0:T(8,128)S(1)}, f32[64,128]{1,0:T(8,128)}, f32[64,128]{1,0:T(8,128)}, f32[64,128]{1,0:T(8,128)}, f32[64,128]{1,0:T(8,128)}) conditional(s32[]{:T(128)} %convert_element_type.3, () %tuple.16, (s32[4,128]{1,0:T(4,128)S(1)}, f32[16,64,128]{2,1,0:T(8,128)}, f32[16,64,128]{2,1,0:T(8,128)}, f32[16,64,128]{2,1,0:T(8,128)}, ...), branch_computations={%region_0.0_spmd, %region_1.0_spmd} | conditional | bytes 606408 | solution.py:921
  5.0 2.6 %branch_1_fun.3 = (f32[104,128]{1,0:T(8,128)S(1)}, f32[104,128]{1,0:T(8,128)S(1)}, f32[64,64]{1,0:T(8,128)S(1)}) custom-call(s32[4,128]{1,0:T(4,128)S(1)} %get-tuple-element.12.owners, f32[16,64,128]{2,1,0:T(8,128)} %get-tuple-element.13.h_in, f32[16,64,128]{2,1,0:T(8,128)} %get-tuple-element.14.a_in, f32[16,64,128]{2,1,0:T(8,128)} %get-tuple-element.15.n_in, ...), custom_call_target="tpu_custom_call" | custom-call | tf_op jit(solution)/shard_map/cond/branch_1_fun/pallas_call | solution.py:865
  7.6 0.6 %collective-permute-start = (f32[104,128]{1,0:T(8,128)S(1)}, f32[104,128]{1,0:T(8,128)S(1)}, u32[]{:S(2)}, u32[]{:S(2)}) collective-permute-start(f32[104,128]{1,0:T(8,128)S(1)} %get-tuple-element.20), channel_id=1, source_target_pairs={{0,4},{1,5},{2,6},{3,7},{4,0},{5,1},{6,2},{7,3},{8,12},{9,13},{10,... | collective-permute-start | bytes 159752 | tf_op jit(solution)/shard_map/cond/branch_1_fun/ppermute | solution.py:882
  8.2 0.9 %collective-permute-done.got = f32[104,128]{1,0:T(8,128)S(1)} collective-permute-done((f32[104,128]{1,0:T(8,128)S(1)}, f32[104,128]{1,0:T(8,128)S(1)}, u32[]{:S(2)}, u32[]{:S(2)}) %collective-permute-start) | collective-permute-done | bytes 53280 | tf_op jit(solution)/shard_map/cond/branch_1_fun/ppermute | solution.py:882
  9.1 0.6 %branch_1_fun.4 = (f32[64,128]{1,0:T(8,128)}, f32[64,128]{1,0:T(8,128)S(1)}, f32[64,128]{1,0:T(8,128)S(1)}, f32[64,128]{1,0:T(8,128)S(1)}) custom-call(f32[104,128]{1,0:T(8,128)S(1)} %get-tuple-element.19.keep, f32[104,128]{1,0:T(8,128)S(1)} %collective-permute-done.got), custom_call_target="tpu_custom_call" | custom-call | tf_op jit(solution)/shard_map/cond/branch_1_fun/pallas_call | solution.py:901
  9.7 3.0 %collective-permute-start.1 = (f32[64,128]{1,0:T(8,128)S(1)}, f32[64,128]{1,0:T(8,128)}, u32[]{:S(2)}, u32[]{:S(2)}) collective-permute-start(f32[64,128]{1,0:T(8,128)S(1)} %get-tuple-element.22), channel_id=1, source_target_pairs={{0,1},{1,0},{2,3},{3,2},{4,5},{5,4},{6,7},{7,6},{8,9},{9,8},{10,11... | collective-permute-start | bytes 98312 | tf_op jit(solution)/shard_map/cond/branch_1_fun/ppermute | solution.py:907
  12.7 0.0 collective-permute-start.2
  12.7 2.3 %collective-permute-start.3 = (f32[64,128]{1,0:T(8,128)S(1)}, f32[64,128]{1,0:T(8,128)}, u32[]{:S(2)}, u32[]{:S(2)}) collective-permute-start(f32[64,128]{1,0:T(8,128)S(1)} %get-tuple-element.24), channel_id=1, source_target_pairs={{0,3},{1,2},{2,1},{3,0},{4,7},{5,6},{6,5},{7,4},{8,11},{9,10},{10,... | collective-permute-start | bytes 98312 | tf_op jit(solution)/shard_map/cond/branch_1_fun/ppermute | solution.py:907
  15.0 0.0 collective-permute-done.1.refs_1_
  15.0 2.9 %collective-permute-done.2.refs_2_ = f32[64,128]{1,0:T(8,128)} collective-permute-done((f32[64,128]{1,0:T(8,128)S(1)}, f32[64,128]{1,0:T(8,128)}, u32[]{:S(2)}, u32[]{:S(2)}) %collective-permute-start.2) | collective-permute-done | bytes 32800 | tf_op jit(solution)/shard_map/cond/branch_1_fun/ppermute | solution.py:907
  18.0 0.7 %collective-permute-done.3.refs_3_ = f32[64,128]{1,0:T(8,128)} collective-permute-done((f32[64,128]{1,0:T(8,128)S(1)}, f32[64,128]{1,0:T(8,128)}, u32[]{:S(2)}, u32[]{:S(2)}) %collective-permute-start.3) | collective-permute-done | bytes 32800 | tf_op jit(solution)/shard_map/cond/branch_1_fun/ppermute | solution.py:907
  18.6 1.0 %branch_1_fun.5 = f32[2,64,128]{2,1,0:T(8,128)S(1)} custom-call(f32[64,64]{1,0:T(8,128)S(1)} %get-tuple-element.18.hot, f32[64,128]{1,0:T(8,128)} %get-tuple-element.61.refs_0_, f32[64,128]{1,0:T(8,128)} %collective-permute-done.1.refs_1_, f32[64,128]{1,0:T(8,128)} %collective-permute-done.2.refs_2_, f32[64,128]{1,0:T(8,128)} %collective-permute-done.3.refs_3_), custom_call_target="tpu_custom_call" | custom-call | tf_op jit(solution)/shard_map/cond/branch_1_fun/pallas_call | solution.py:909
  19.6 0.0 collective-permute-done.4.z_e.refs_0_
  19.6 0.0 collective-permute-done.5.z_o.refs_1_
  19.7 0.1 collective-permute-start.6
  19.8 1.8 %shard_map.114.refs_0_.planes = f32[106,64,128]{2,1,0:T(8,128)S(1)} custom-call(f32[16,64,128]{2,1,0:T(8,128)} %refs_0_.1, f32[16,64,128]{2,1,0:T(8,128)} %refs_1_.1, f32[16,64,128]{2,1,0:T(8,128)} %refs_2_.1, f32[16,64,128]{2,1,0:T(8,128)} %refs_3_.1, f32[16,64,128]{2,1,0:T(8,128)} %refs_4_.1, f32[12,64,128]{2,1,0:T(8,128)S(1)} %collective-permute-done.4.z_e.refs_0_, ...), custom_call_target="tpu_custom_call" | custom-call | tf_op jit(solution)/shard_map/pallas_call | solution.py:938
  21.6 0.0 collective-permute-done.6.refs_1_
  21.6 3.4 %shard_map.117 = (f32[106,8,128]{2,1,0:T(8,128)S(1)}, f32[1792,128]{1,0:T(8,128)S(1)}, f32[320,128]{1,0:T(8,128)S(1)}, f32[320,128]{1,0:T(8,128)S(1)}) custom-call(f32[106,64,128]{2,1,0:T(8,128)S(1)} %shard_map.114.refs_0_.planes, f32[106,4,128]{2,1,0:T(4,128)S(1)} %collective-permute-done.6.refs_1_), custom_call_target="tpu_custom_call" | custom-call | tf_op jit(solution)/shard_map/pallas_call | solution.py:946
  25.0 0.6 %collective-permute-start.7 = (f32[320,128]{1,0:T(8,128)S(1)}, f32[320,128]{1,0:T(8,128)S(1)}, u32[]{:S(2)}, u32[]{:S(2)}) collective-permute-start(f32[320,128]{1,0:T(8,128)S(1)} %get-tuple-element.52), channel_id=1, source_target_pairs={{0,8},{1,9},{2,10},{3,11},{4,12},{5,13},{6,14},{7,15},{8,0},{9,1},... | collective-permute-start | bytes 491528 | tf_op jit(solution)/shard_map/ppermute | solution.py:838
  25.6 2.4 %collective-permute-start.8 = (f32[320,128]{1,0:T(8,128)S(1)}, f32[320,128]{1,0:T(8,128)S(1)}, u32[]{:S(2)}, u32[]{:S(2)}) collective-permute-start(f32[320,128]{1,0:T(8,128)S(1)} %get-tuple-element.53), channel_id=1, source_target_pairs={{0,4},{1,5},{2,6},{3,7},{4,0},{5,1},{6,2},{7,3},{8,16},{9,17},{10,... | collective-permute-start | bytes 491528 | tf_op jit(solution)/shard_map/ppermute | solution.py:838
  28.0 7.5 %shard_map.118 = (f32[16,64,128]{2,1,0:T(8,128)S(1)}, f32[128,128]{1,0:T(8,128)S(1)}, f32[6,16,128]{2,1,0:T(8,128)}) custom-call(f32[106,64,128]{2,1,0:T(8,128)S(1)} %shard_map.114.refs_0_.planes, f32[106,8,128]{2,1,0:T(8,128)S(1)} %get-tuple-element.44.edge, f32[64,128]{1,0:T(8,128)} %get-tuple-element.45.refs_0_, f32[64,128]{1,0:T(8,128)} %get-tuple-element.46.refs_1_, ...), custom_call_target="tpu_custom_call" | custom-call | tf_op jit(solution)/shard_map/pallas_call | solution.py:954
  35.5 0.0 collective-permute-done.7.y_e
  35.5 0.6 %collective-permute-done.8.y_o = f32[320,128]{1,0:T(8,128)S(1)} collective-permute-done((f32[320,128]{1,0:T(8,128)S(1)}, f32[320,128]{1,0:T(8,128)S(1)}, u32[]{:S(2)}, u32[]{:S(2)}) %collective-permute-start.8) | collective-permute-done | bytes 163872 | tf_op jit(solution)/shard_map/ppermute | solution.py:838
  36.1 2.4 %shard_map.119 = f32[16,64,128]{2,1,0:T(8,128)} custom-call(f32[16,64,128]{2,1,0:T(8,128)S(1)} %get-tuple-element.49.main, f32[128,128]{1,0:T(8,128)S(1)} %get-tuple-element.50.inner, f32[1792,128]{1,0:T(8,128)S(1)} %get-tuple-element.51.strips_in, f32[320,128]{1,0:T(8,128)S(1)} %collective-permute-done.7.y_e, f32[320,128]{1,0:T(8,128)S(1)} %collective-permute-done.8.y_o), custom_call_target="tpu_custom_call" | custom-call | tf_op jit(solution)/shard_map/pallas_call | solution.py:955
  (1 shorter events, 0.0 us)
Async XLA Ops:
  0.6 4.4 %copy-start = (s32[128,4]{0,1:T(4,128)S(1)}, s32[128,4]{0,1:T(4,128)}, u32[]{:S(2)}) copy-start(s32[128,4]{0,1:T(4,128)} %param.17) | copy-start | bytes 6148
  2.1 17.5 %collective-permute-start.4 = (f32[12,64,128]{2,1,0:T(8,128)S(1)}, f32[12,64,128]{2,1,0:T(8,128)S(1)}, u32[]{:S(2)}, u32[]{:S(2)}) collective-permute-start(f32[12,64,128]{2,1,0:T(8,128)S(1)} %get-tuple-element.41), channel_id=1, source_target_pairs={{0,1},{1,0},{2,3},{3,2},{4,5},{5,4},{6,7},{7,6},{8,9},{9,8},{10,11... | collective-permute-start | bytes 1179656 | tf_op jit(solution)/shard_map/ppermute | solution.py:838
  3.7 15.9 %collective-permute-start.5 = (f32[12,64,128]{2,1,0:T(8,128)S(1)}, f32[12,64,128]{2,1,0:T(8,128)S(1)}, u32[]{:S(2)}, u32[]{:S(2)}) collective-permute-start(f32[12,64,128]{2,1,0:T(8,128)S(1)} %get-tuple-element.42), channel_id=1, source_target_pairs={{0,4},{1,2},{2,1},{3,7},{4,0},{5,6},{6,5},{7,3},{8,12},{9,10},{10,... | collective-permute-start | bytes 1179656 | tf_op jit(solution)/shard_map/ppermute | solution.py:838
  7.6 1.5 %collective-permute-start = (f32[104,128]{1,0:T(8,128)S(1)}, f32[104,128]{1,0:T(8,128)S(1)}, u32[]{:S(2)}, u32[]{:S(2)}) collective-permute-start(f32[104,128]{1,0:T(8,128)S(1)} %get-tuple-element.20), channel_id=1, source_target_pairs={{0,4},{1,5},{2,6},{3,7},{4,0},{5,1},{6,2},{7,3},{8,12},{9,13},{10,... | collective-permute-start | bytes 159752 | tf_op jit(solution)/shard_map/cond/branch_1_fun/ppermute | solution.py:882
  9.7 5.4 %collective-permute-start.1 = (f32[64,128]{1,0:T(8,128)S(1)}, f32[64,128]{1,0:T(8,128)}, u32[]{:S(2)}, u32[]{:S(2)}) collective-permute-start(f32[64,128]{1,0:T(8,128)S(1)} %get-tuple-element.22), channel_id=1, source_target_pairs={{0,1},{1,0},{2,3},{3,2},{4,5},{5,4},{6,7},{7,6},{8,9},{9,8},{10,11... | collective-permute-start | bytes 98312 | tf_op jit(solution)/shard_map/cond/branch_1_fun/ppermute | solution.py:907
  12.7 5.3 %collective-permute-start.2 = (f32[64,128]{1,0:T(8,128)S(1)}, f32[64,128]{1,0:T(8,128)}, u32[]{:S(2)}, u32[]{:S(2)}) collective-permute-start(f32[64,128]{1,0:T(8,128)S(1)} %get-tuple-element.23), channel_id=1, source_target_pairs={{0,2},{1,3},{2,0},{3,1},{4,6},{5,7},{6,4},{7,5},{8,10},{9,11},{10,... | collective-permute-start | bytes 98312 | tf_op jit(solution)/shard_map/cond/branch_1_fun/ppermute | solution.py:907
  12.7 5.9 %collective-permute-start.3 = (f32[64,128]{1,0:T(8,128)S(1)}, f32[64,128]{1,0:T(8,128)}, u32[]{:S(2)}, u32[]{:S(2)}) collective-permute-start(f32[64,128]{1,0:T(8,128)S(1)} %get-tuple-element.24), channel_id=1, source_target_pairs={{0,3},{1,2},{2,1},{3,0},{4,7},{5,6},{6,5},{7,4},{8,11},{9,10},{10,... | collective-permute-start | bytes 98312 | tf_op jit(solution)/shard_map/cond/branch_1_fun/ppermute | solution.py:907
  19.7 1.9 %collective-permute-start.6 = (f32[106,4,128]{2,1,0:T(4,128)S(1)}, f32[106,4,128]{2,1,0:T(4,128)S(1)}, u32[]{:S(2)}, u32[]{:S(2)}) collective-permute-start(f32[106,4,128]{2,1,0:T(4,128)S(1)} %shard_map.116), channel_id=1, source_target_pairs={{0,4},{1,5},{2,6},{3,7},{4,0},{5,1},{6,2},{7,3},{8,12},{9,13},{10,... | collective-permute-start | bytes 651272 | tf_op jit(solution)/shard_map/ppermute | solution.py:838
  25.0 10.5 %collective-permute-start.7 = (f32[320,128]{1,0:T(8,128)S(1)}, f32[320,128]{1,0:T(8,128)S(1)}, u32[]{:S(2)}, u32[]{:S(2)}) collective-permute-start(f32[320,128]{1,0:T(8,128)S(1)} %get-tuple-element.52), channel_id=1, source_target_pairs={{0,8},{1,9},{2,10},{3,11},{4,12},{5,13},{6,14},{7,15},{8,0},{9,1},... | collective-permute-start | bytes 491528 | tf_op jit(solution)/shard_map/ppermute | solution.py:838
  25.6 10.5 %collective-permute-start.8 = (f32[320,128]{1,0:T(8,128)S(1)}, f32[320,128]{1,0:T(8,128)S(1)}, u32[]{:S(2)}, u32[]{:S(2)}) collective-permute-start(f32[320,128]{1,0:T(8,128)S(1)} %get-tuple-element.53), channel_id=1, source_target_pairs={{0,4},{1,5},{2,6},{3,7},{4,0},{5,1},{6,2},{7,3},{8,16},{9,17},{10,... | collective-permute-start | bytes 491528 | tf_op jit(solution)/shard_map/ppermute | solution.py:838

commit v4 on v3

--- a/solution.py
+++ b/solution.py
@@ -18,6 +18,7 @@
 VMEM = pl.BlockSpec(memory_space=pltpu.VMEM)
 SMEM = pl.BlockSpec(memory_space=pltpu.SMEM)
 HBM = pl.BlockSpec(memory_space=pltpu.HBM)
+ANY = pl.BlockSpec(memory_space=pl.ANY)
 MIB = 1024 * 1024
 
 LEVELS = 16
@@ -160,10 +161,14 @@
     me_role, me_gx = place("role"), place("gx")
     me = me_gx * count_gz + place("gz")
     copies = []
-    for src, dst in ((h_in, h), (a_in, a), (n_in, n), (tr_in, tr), (rt_in, rt)):
-        copy = pltpu.make_async_copy(src, dst, sem.at[len(copies)])
+    for layer in range(LAYERS_PER_BLOCK):
+        some = pl.ds(layer * LEVELS_PER_LAYER, LEVELS_PER_LAYER)
+        for src, dst in ((h_in, h), (a_in, a), (n_in, n)):
+            copies.append(pltpu.make_async_copy(src.at[some], dst.at[some], sem.at[len(copies)]))
+    for src, dst in ((tr_in, tr), (rt_in, rt)):
+        copies.append(pltpu.make_async_copy(src, dst, sem.at[len(copies)]))
+    for copy in copies:
         copy.start()
-        copies.append(copy)
 
     def clear_slot(i, carry):
         slots[i] = -1
@@ -192,9 +197,9 @@
         return carry
 
     lax.fori_loop(0, ROWS, step, 0)
-    for copy in copies:
-        copy.wait()
     for layer in range(LAYERS_PER_BLOCK):
+        for copy in copies[3 * layer : 3 * layer + 3]:
+            copy.wait()
         saturs = []
         heads = []
         for level in range(layer * LEVELS_PER_LAYER, (layer + 1) * LEVELS_PER_LAYER):
@@ -207,6 +212,8 @@
             heads.append(head)
         means[layer] = (saturs[0] + saturs[1] + saturs[2] + saturs[3]) * 0.25
         means[LAYERS_PER_BLOCK + layer] = (heads[0] + heads[1] + heads[2] + heads[3]) * 0.25
+    for copy in copies[3 * LAYERS_PER_BLOCK :]:
+        copy.wait()
     half = groups // 2
     for j in range(groups):
         out, k = (keep, j) if j < half else (send, j - half)
@@ -239,12 +246,13 @@
 
 
 def tile_values(count_gx, count_gz, hot, *refs):
-    parts, out = refs[:count_gz], refs[count_gz]
+    parts, out, y = refs[:count_gz], refs[count_gz], refs[count_gz + 1]
     values = []
     for gx in range(count_gx):
         for dist in range(count_gz):
             base = count_gx * PIECE + gx * 8
             values.append(parts[dist][base : base + 8])
+            y[gx * count_gz + dist] = parts[dist][gx * PIECE : (gx + 1) * PIECE]
     t = jnp.concatenate(values, axis=0)
     out[0] = exact_dot(hot[...], t)
     out[1] = jnp.maximum(exact_dot(hot[...], pltpu.roll(t, t.shape[0] - 1, 0)), 1.0)
@@ -288,87 +296,77 @@
     return (value, value * value, 0.5 * value, 0.5 * value, value)[k]
 
 
-def own_edges(count_gx, *refs):
-    arrays, outs, buf, sem = refs[:5], refs[5:-2], refs[-2], refs[-1]
+def packed_tile(tile, rows_of, count):
+    lane_group = lax.broadcasted_iota(jnp.int32, (count, COLS), 1) // SIDE
+    acc = jnp.zeros((count, COLS), jnp.float32)
+    for j in range(8):
+        p = tile * 8 + j
+        value = rows_of(p) if p < PLANES else None
+        if value is not None:
+            acc = jnp.where(lane_group == j, pltpu.roll(value, SIDE * j + 8, 1), acc)
+    return acc
+
+
+OWN_AT = {first + level: k * LEVELS + level for k, first in enumerate(OWN) for level in range(LEVELS)}
+EXT_AT = {p: k for k, p in enumerate(p for p in range(PLANES) if p not in OWN_AT)}
+
+
+def own_planes(*refs):
+    arrays, own, sem = refs[:5], refs[5], refs[6]
     copies = []
     for k, src in enumerate(arrays):
-        for side in range(2):
-            start = 0 if side == 0 else ROWS - 8
-            copy = pltpu.make_async_copy(src.at[:, pl.ds(start, 8), :], buf.at[side, k], sem.at[len(copies)])
-            copy.start()
-            copies.append(copy)
-    for copy in copies:
-        copy.wait()
-
-    def put(high, low):
-        for k, first in enumerate(OWN):
-            for level in range(LEVELS):
-                if high is not None:
-                    value = buf[1, k, level, pl.ds(8 - HALO, HALO), :]
-                    high[first + level, pl.ds(0, HALO), :] = scaled(k, value)
-                if low is not None:
-                    value = buf[0, k, level, pl.ds(0, HALO), :]
-                    low[first + level, pl.ds(0, HALO), :] = scaled(k, value)
-
-    by_parity("gx", put, outs[0], outs[1] if count_gx > 2 else None)
-
-
-def x_faces(count_gx, *refs):
-    z_e, z_o, tile = refs[:3]
-    sends = refs[-1:] if count_gx == 2 else refs[-2:]
-
-    def put_all(high, low):
-        def put(upper, lower):
-            for got, places in ((upper, z_places(False)), (lower, z_places(True))):
-                for k, p in enumerate(places):
-                    if high is not None:
-                        high[p, pl.ds(0, HALO), :] = got[k, pl.ds(ROWS - HALO, HALO), :]
-                    if low is not None:
-                        low[p, pl.ds(0, HALO), :] = got[k, pl.ds(0, HALO), :]
-
-        by_parity("gz", put, z_e, z_o)
-        for k in range(2):
-            if high is not None:
-                high[TP + k, pl.ds(0, HALO), :] = tile[k, pl.ds(ROWS - HALO, HALO), :]
-            if low is not None:
-                low[TP + k, pl.ds(0, HALO), :] = tile[k, pl.ds(0, HALO), :]
-
-    by_parity("gx", put_all, sends[0], sends[1] if count_gx > 2 else None)
-
-
-def all_planes(h, a, n, s, p, z_e, z_o, tile, planes, sem):
-    copies = []
-    for k, src in enumerate((h, a, n, s, p)):
-        copy = pltpu.make_async_copy(src, planes.at[pl.ds(OWN[k], LEVELS)], sem.at[k])
+        copy = pltpu.make_async_copy(src, own.at[pl.ds(k * LEVELS, LEVELS)], sem.at[k])
         copy.start()
         copies.append(copy)
-
-    def put(upper, lower):
+    for k, copy in enumerate(copies):
+        copy.wait()
+        if 0 < k < 4:
+            for level in range(LEVELS):
+                own[k * LEVELS + level] = scaled(k, own[k * LEVELS + level])
+
+
+def own_part(*refs):
+    arrays, rim, pack, own, sem = refs[:5], refs[5], refs[6], refs[7], refs[8]
+    own_planes(*arrays, own, sem)
+    for k in range(len(OWN_AT)):
+        rim[k, 0:8] = own[k, 0:8]
+        rim[k, 8:16] = own[k, ROWS - 8 : ROWS]
+    for t in range(PACKS):
+        pack[t] = packed_tile(t, lambda p: own[OWN_AT[p]] if p in OWN_AT else None, ROWS)
+
+
+def x_faces(count_gx, rim, z_e, z_o, tile, ext, *sends):
+    def take(upper, lower):
         for got, places in ((upper, z_places(False)), (lower, z_places(True))):
             for k, p in enumerate(places):
-                planes[p] = got[k]
-
-    by_parity("gz", put, z_e, z_o)
-    planes[TP] = tile[0]
-    planes[RT] = tile[1]
-    for copy in copies:
-        copy.wait()
-    for k in (1, 2, 3):
-        for level in range(LEVELS):
-            planes[OWN[k] + level] = scaled(k, planes[OWN[k] + level])
+                ext[EXT_AT[p]] = got[k]
+
+    by_parity("gz", take, z_e, z_o)
+    ext[EXT_AT[TP]] = tile[0]
+    ext[EXT_AT[RT]] = tile[1]
+
+    def put(high, low):
+        for p in range(PLANES):
+            src, k, rows = (rim, OWN_AT[p], 16) if p in OWN_AT else (ext, EXT_AT[p], ROWS)
+            if high is not None:
+                high[p, pl.ds(0, HALO), :] = src[k, pl.ds(rows - HALO, HALO), :]
+            if low is not None:
+                low[p, pl.ds(0, HALO), :] = src[k, pl.ds(0, HALO), :]
+
+    by_parity("gx", put, sends[0], sends[1] if count_gx > 2 else None)
 
 
 def y_faces(count_gx, *refs):
-    planes = refs[0]
+    rim, own_pack, ext = refs[:3]
     if count_gx > 2:
-        got_e, got_o = refs[1], refs[2]
+        got_e, got_o = refs[4], refs[5]
     else:
-        got_e, got_o = refs[1], None
+        got_e, got_o = refs[4], None
     edge, strips, send_e, send_o = refs[-4:]
 
     def take(high, low):
         for p in range(PLANES):
-            edge[p] = planes[p, ROWS - EDGE : ROWS]
+            edge[p] = rim[OWN_AT[p], 8:16] if p in OWN_AT else ext[EXT_AT[p], ROWS - EDGE : ROWS]
             if high is not None:
                 edge[p, pl.ds(0, HALO), :] = high[p, pl.ds(0, HALO), :]
             if low is not None:
@@ -384,19 +382,16 @@
     def _():
         take(got_o, got_e)
 
-    lane_group = lax.broadcasted_iota(jnp.int32, (WIDE, COLS), 1) // SIDE
-
-    def pack(t, carry):
-        acc = jnp.zeros((WIDE, COLS), jnp.float32)
+    group = lax.broadcasted_iota(jnp.int32, (ROWS, COLS), 1) // SIDE
+    for t in range(PACKS):
+        rows = own_pack[t]
         for j in range(8):
-            p = jnp.minimum(t * 8 + j, PLANES - 1)
-            value = jnp.concatenate([planes[p], edge[p]], axis=0)
-            acc = jnp.where(lane_group == j, pltpu.roll(value, SIDE * j + 8, 1), acc)
-        full = jnp.concatenate([acc] + [acc[ROWS:WIDE]] * ((COLS - WIDE) // EDGE), axis=0)
-        strips[pl.ds(pl.multiple_of(t * COLS, COLS), COLS), :] = full.T
-        return carry
-
-    lax.fori_loop(0, PACKS, pack, 0)
+            p = t * 8 + j
+            if p in EXT_AT:
+                rows = jnp.where(group == j, pltpu.roll(ext[EXT_AT[p]], SIDE * j + 8, 1), rows)
+        last = packed_tile(t, lambda p: edge[p], EDGE)
+        full = widened(jnp.concatenate([rows, last], axis=0))
+        strips[t * COLS : (t + 1) * COLS, :] = full.T
 
     def put(send, last):
         start = 5 if last else 8
@@ -455,15 +450,24 @@
     return jnp.concatenate([value] + [value[ROWS:WIDE]] * ((COLS - WIDE) // EDGE), axis=0)
 
 
-def main_region(count_role, count_gx, count_gz, planes, edge, *refs):
-    land_in, refs = refs[: count_gz + 4], refs[count_gz + 4 :]
+def main_region(count_role, count_gx, count_gz, own, ext, edge, *refs):
+    land_in, refs = refs[:5], refs[5:]
     out, inner, land_out, ha, hb, kc, mm, th, wd, sk = refs[:10]
     heat_finish = heat(count_gx, count_gz, *land_in, land_out, *refs[10:])
     spot = Where(count_role, count_gx, count_gz)
     z_top, z_bottom = spot.z_top, spot.z_bottom
 
     def wide(p):
-        return jnp.concatenate([planes[p], edge[p]], axis=0)
+        rows = own[OWN_AT[p]] if p in OWN_AT else ext[EXT_AT[p]]
+        return jnp.concatenate([rows, edge[p]], axis=0)
+
+    def wide_own(k, level):
+        return jnp.concatenate([own[k * LEVELS + level], edge[OWN[k] + level]], axis=0)
+
+    def inputs(j):
+        if isinstance(j, int):
+            return [wide(A0 + j), wide(N0 + j), wide(S0 + j)] + ([wide(P0 + j - 1)] if 0 < j < NC - 1 else [])
+        return [wide_own(k, j - (HALO - 1)) for k in (1, 2, 3, 4)]
 
     def put(ref, i, value):
         ref[i, 8 : 8 + WIDE] = value
@@ -474,11 +478,14 @@
     x_low = jnp.where(row == 0, spot.x_first, 1.0)
     x_high = jnp.where(row == 7, spot.x_last, 1.0)
 
-    def fill(i, carry):
+    def fill(level, carry):
+        put(ha, HALO + level, wide_own(0, level))
+        return carry
+
+    lax.fori_loop(0, LEVELS, fill, 0, unroll=4)
+    for i in range(HALO):
         put(ha, i, wide(H0 + i))
-        return carry
-
-    lax.fori_loop(0, NH, fill, 0)
+        put(ha, HALO + LEVELS + i, wide(H0 + HALO + LEVELS + i))
     put(kc, 0, wide(K_LO))
     put(kc, NH - 1, wide(K_HI))
 
@@ -490,22 +497,30 @@
     for q, value in enumerate(uptake_of(wide(TP), wide(RT), heads, spot.layers, base, spot.first)):
         sk[q] = value
 
-    def first_curves(j, theta):
+    def first_curves(j):
         i = j + 1
-        half_n = wide(N0 + j)
+        alpha2, half_n, half_ks, *poros = inputs(j)
         expo = expo_of(half_n)
         mm[j] = expo
-        satur, cond = curves(ha[i, 8 : 8 + WIDE], wide(A0 + j), half_n, wide(S0 + j), expo)
+        satur, cond = curves(ha[i, 8 : 8 + WIDE], alpha2, half_n, half_ks, expo)
         put(kc, i, cond)
-        if theta:
-            th[j - 1] = wide(P0 + j - 1) * satur
-
-    def later_curves(src, j, water):
+        if poros:
+            th[j - 1] = poros[0] * satur
+
+    def later_curves(src, j):
         i = j + 1
-        satur, cond = curves(src[i, 8 : 8 + WIDE], wide(A0 + j), wide(N0 + j), wide(S0 + j), mm[j])
+        alpha2, half_n, half_ks, *poros = inputs(j)
+        satur, cond = curves(src[i, 8 : 8 + WIDE], alpha2, half_n, half_ks, mm[j])
         put(kc, i, cond)
-        if water:
-            wd[j - 1] = wide(P0 + j - 1) * satur - th[j - 1] + sk[(i + 1) // LEVELS_PER_LAYER]
+        if poros:
+            wd[j - 1] = poros[0] * satur - th[j - 1] + sk[(i + 1) // LEVELS_PER_LAYER]
+
+    def curves_of(body, extra):
+        for j in range(HALO - 1 - extra, HALO - 1):
+            body(j)
+        loop(HALO - 1, HALO - 1 + LEVELS, body, 4)
+        for j in range(HALO - 1 + LEVELS, HALO - 1 + LEVELS + extra):
+            body(j)
 
     def stencil(src, i0, count, sweep, store):
         here = pl.ds(8, WIDE)
@@ -549,9 +564,7 @@
         if extra:
             stencil(src, HALO + LEVELS, extra, sweep, store)
 
-    first_curves(0, False)
-    loop(1, NC - 1, lambda j: first_curves(j, True), 3)
-    first_curves(NC - 1, False)
+    curves_of(first_curves, 2)
     levels_of(ha, 0, lambda i, value: put(hb, i, value))
 
     lane_wide = lax.broadcasted_iota(jnp.int32, (WIDE, COLS), 1)
@@ -562,11 +575,9 @@
         acc = jnp.where(pick, pltpu.roll(hb[k + 1, 8 : 8 + WIDE], (lane - (COLS - 1 - NEAR)) % COLS, 1), acc)
     inner[...] = widened(acc).T
 
-    later_curves(hb, 0, False)
-    loop(1, NC - 1, lambda j: later_curves(hb, j, True), 3)
-    later_curves(hb, NC - 1, False)
+    curves_of(lambda j: later_curves(hb, j), 2)
     levels_of(hb, 1, lambda i, value: put(ha, i, value))
-    loop(1, NC - 1, lambda j: later_curves(ha, j, True), 3)
+    curves_of(lambda j: later_curves(ha, j), 1)
 
     def keep(i, value):
         out[i - HALO] = value[0:ROWS]
@@ -702,17 +713,8 @@
         copy.wait()
 
 
-def heat(count_gx, count_gz, *refs):
-    parts, refs = refs[:count_gz], refs[count_gz:]
-    temp_in, tr_in, air_in, rt_in, out, sat, head, temp, tr, air, rt, y, sem = refs
+def heat(count_gx, count_gz, y, temp_in, tr_in, air_in, rt_in, out, sat, head, temp, tr, air, rt, sem):
     copies = []
-    for dist, part in enumerate(parts):
-        for gx in range(count_gx):
-            copy = pltpu.make_async_copy(
-                part.at[pl.ds(gx * PIECE, PIECE)], y.at[gx * count_gz + dist], sem.at[len(copies)]
-            )
-            copy.start()
-            copies.append(copy)
     for src, dst in ((temp_in, temp), (tr_in, tr), (air_in, air), (rt_in, rt)):
         copy = pltpu.make_async_copy(src, dst, sem.at[len(copies)])
         copy.start()
@@ -753,7 +755,7 @@
     return finish
 
 
-def call(body, outs, ins, scratch=(), aliases=None, limit=40 * MIB, kept=True, work=0):
+def call(body, outs, ins, scratch=(), aliases=None, limit=16 * MIB, kept=True, work=0):
     return pl.pallas_call(
         body,
         out_shape=[pltpu.VMEM(shape, jnp.float32) if kept else jax.ShapeDtypeStruct(shape, jnp.float32) for shape in outs],
@@ -771,7 +773,6 @@
     deep = WIDE + 16
     slots = count_gx * CAP
     land_shape = (slots, LAYERS_PER_BLOCK * count_gz, COLS)
-    groups = count_gx * count_gz
     return pl.pallas_call(
         functools.partial(main_region, count_role, count_gx, count_gz),
         out_shape=[
@@ -779,7 +780,7 @@
             pltpu.VMEM((COLS, COLS), f32),
             jax.ShapeDtypeStruct(land_shape, f32),
         ],
-        in_specs=[VMEM] * 2 + [HBM] * (count_gz + 4),
+        in_specs=[VMEM] * 4 + [HBM] * 4,
         out_specs=[VMEM] * 3,
         scratch_shapes=[
             pltpu.VMEM((NH, deep, COLS), f32),
@@ -795,10 +796,9 @@
             pltpu.VMEM((slots, 1, COLS), f32),
             pltpu.VMEM((slots, 1, COLS), f32),
             pltpu.VMEM((slots, 1, COLS), jnp.int32),
-            pltpu.VMEM((groups, PIECE, COLS), f32),
-            pltpu.SemaphoreType.DMA((4 + groups,)),
+            pltpu.SemaphoreType.DMA((4,)),
         ],
-        compiler_params=pltpu.CompilerParams(vmem_limit_bytes=40 * MIB),
+        compiler_params=pltpu.CompilerParams(vmem_limit_bytes=16 * MIB),
     )
 
 
@@ -823,7 +823,7 @@
             pltpu.VMEM((LEVELS, ROWS, COLS), f32),
             pltpu.SemaphoreType.DMA((LEVELS,)),
         ],
-        compiler_params=pltpu.CompilerParams(vmem_limit_bytes=40 * MIB),
+        compiler_params=pltpu.CompilerParams(vmem_limit_bytes=16 * MIB),
     )
 
 
@@ -861,6 +861,10 @@
     half = groups // 2
     blocks = count_gx // 2
     packed = half * 8 * CAP + blocks * 8
+    x_count = 1 if count_gx == 2 else 2
+    x_shape = (PLANES, 4, COLS)
+    own_shapes = [(len(OWN_AT), 16, COLS), (PACKS, ROWS, COLS)]
+
     def land_stage():
         send, keep, hot = call(
             functools.partial(land_pack, count_gx, count_gz),
@@ -875,7 +879,7 @@
                 pltpu.VMEM((LEVELS, ROWS, COLS), f32),
                 pltpu.VMEM((slots, 1, COLS), f32),
                 pltpu.VMEM((slots, 1, COLS), jnp.int32),
-                pltpu.SemaphoreType.DMA((5,)),
+                pltpu.SemaphoreType.DMA((3 * LAYERS_PER_BLOCK + 2,)),
             ],
         )(owners, h, a, n, tr, rt)
 
@@ -898,6 +902,12 @@
                 bit //= 2
             keep = jnp.concatenate(pieces[:half] + values[:blocks], axis=0)
             got = jnp.concatenate(pieces[half:] + values[blocks:], axis=0)
+        rim, pack = call(
+            own_part,
+            own_shapes,
+            [HBM] * 5,
+            [pltpu.VMEM((len(OWN_AT), ROWS, COLS), f32), pltpu.SemaphoreType.DMA((5,))],
+        )(h, a, n, s, p)
         parts = call(
             functools.partial(land_sort, count_gx, count_gz),
             [(count_gx * (PIECE + 8), COLS)] * count_gz,
@@ -906,52 +916,42 @@
         parts = [parts[0]] + [
             lax.ppermute(parts[dist], AXES, xor_pairs(sizes, "gz", dist)) for dist in range(1, count_gz)
         ]
-        (tile,) = call(
+        tile, y = call(
             functools.partial(tile_values, count_gx, count_gz),
-            [(2, ROWS, COLS)],
+            [(2, ROWS, COLS), (groups, PIECE, COLS)],
             [VMEM] * (1 + count_gz),
         )(hot, *parts)
-        return [tile] + parts
+        return [rim, pack, tile, y]
 
     def no_land_stage():
-        shapes = [(2, ROWS, COLS)] + [(count_gx * (PIECE + 8), COLS)] * count_gz
+        shapes = own_shapes + [(2, ROWS, COLS), (groups, PIECE, COLS)]
         return [jnp.zeros(shape, f32) for shape in shapes]
 
     ahead = lax.optimization_barrier(jnp.bool_(True))
-    tile, *parts = lax.cond(ahead, land_stage, no_land_stage)
-    parts = [pltpu.with_memory_space_constraint(x, pltpu.HBM) for x in parts]
-
-    x_count = 1 if count_gx == 2 else 2
-    x_shape = (PLANES, 4, COLS)
-    edges = call(
-        functools.partial(own_edges, count_gx),
-        [x_shape] * x_count,
+    rim, pack, tile, y = lax.cond(ahead, land_stage, no_land_stage)
+
+    ext, *x_sends = call(
+        functools.partial(x_faces, count_gx),
+        [(len(EXT_AT), ROWS, COLS)] + [x_shape] * x_count,
+        [VMEM] * 4,
+    )(rim, z_e, z_o, tile)
+    (own,) = call(
+        own_planes,
+        [(len(OWN_AT), ROWS, COLS)],
         [HBM] * 5,
-        [pltpu.VMEM((2, 5, LEVELS, 8, COLS), f32), pltpu.SemaphoreType.DMA((10,))],
+        [pltpu.SemaphoreType.DMA((5,))],
     )(h, a, n, s, p)
-    x_sends = call(
-        functools.partial(x_faces, count_gx),
-        [x_shape] * x_count,
-        [VMEM] * (3 + x_count),
-        aliases={3 + k: k for k in range(x_count)},
-    )(z_e, z_o, tile, *edges)
-    (planes,) = call(
-        all_planes,
-        [(PLANES, ROWS, COLS)],
-        [HBM] * 5 + [VMEM] * 3,
-        [pltpu.SemaphoreType.DMA((5,))],
-    )(h, a, n, s, p, z_e, z_o, tile)
     x_got = [swap(value, "gx", bool(k)) for k, value in enumerate(x_sends)]
 
     edge, strips, y_send_e, y_send_o = call(
         functools.partial(y_faces, count_gx),
         [(PLANES, EDGE, COLS), (PACKS * COLS, COLS), (Y_SEND, COLS), (Y_SEND, COLS)],
-        [VMEM] * (1 + x_count),
-    )(planes, *x_got)
+        [VMEM] * 3 + [ANY] + [VMEM] * x_count,
+    )(rim, pack, ext, own, *x_got)
     y_e = swap(y_send_e, "role", False)
     y_o = swap(y_send_o, "role", True) if count_role > 2 else y_e
 
-    main, inner, land_new = main_call(*sizes)(planes, edge, *parts, land_temp, tr, air, rt)
+    main, inner, land_new = main_call(*sizes)(own, ext, edge, y, land_temp, tr, air, rt)
     head = strip_call(*sizes)(main, inner, strips, y_e, y_o)
     return (head, land_new[None, None])
 

time: 38.8 us -> 34.4 us (0.89)
  Pallas kernels: 22 us -> 19.1 us
  waiting for transfers between devices: 5.1 us -> 3.43 us
    pallas_call x1, Pallas kernels: 3.36 us -> 0.85 us  [local(): call(functools.partial(y_faces, count_gx), [(PLANES, EDGE, COLS), (PACKS...]
    ppermute x3, waiting for transfers between devices: 3.6 us -> 1.6 us  [land_stage(): lax.ppermute(parts[dist], AXES, xor_pairs(sizes, 'gz', dist))]
    pallas_call x4, Pallas kernels: 10.6 us -> 11.5 us  [the longest x1 7.13 us: local(): main_call(*sizes)(own, ext, edge, y, land_temp, tr, air, rt)]
    pallas_call x1, Pallas kernels: 0.97 us -> 0.17 us  [land_stage(): call(functools.partial(tile_values, count_gx, count_gz), [(2, ROWS, COLS)...]
    pallas_call x1, Pallas kernels: 0.62 us -> 0.01 us  [land_stage(): call(functools.partial(land_sort, count_gx, count_gz), [(count_gx * (PIEC...]
  transfers between devices with their start and end apart: 9 -> 9, of which waited for: 4 -> 3; matrix products, arithmetic and copies ran while one was open for 0% -> 0% of each run, Pallas kernels for 38% -> 42%
where the time goes in v4:
time: 34.4 us; the launch traced here: 34.1 us
  Pallas kernels  19.1 us (56%)
  starting transfers between devices  10.8 us (31%)
  waiting for transfers between devices  3.43 us (10%)
  between operations  0.73 us (2%)
    pallas_call x1, Pallas kernels, local(): main_call(*sizes)(own, ext, edge, y, land_temp, tr, air, rt)  7.13 us
    ppermute x3, starting transfers between devices, land_stage(): lax.ppermute(parts[dist], AXES, xor_pairs(sizes, 'gz', dist))  5.5 us
    ppermute x5, starting transfers between devices, swap(): return lax.ppermute(value, AXES, pairing(sizes, axis, odd))  4.76 us
    pallas_call x1, Pallas kernels, land_stage(): call(functools.partial(land_pack, count_gx, count_gz), [(packed, COLS), (...  2.77 us
    pallas_call x1, Pallas kernels, land_stage(): call(own_part, own_shapes, [HBM] * 5, [pltpu.VMEM((len(OWN_AT), ROWS, COL...  2.5 us
    pallas_call x1, Pallas kernels, local(): head = strip_call(*sizes)(main, inner, strips, y_e, y_o)  2.4 us
    pallas_call x1, Pallas kernels, local(): call(own_planes, [(len(OWN_AT), ROWS, COLS)], [HBM] * 5, [pltpu.Semaphore...  1.72 us
    ppermute x3, waiting for transfers between devices, land_stage(): lax.ppermute(parts[dist], AXES, xor_pairs(sizes, 'gz', dist))  1.6 us
  transfers between devices with their start and end apart: 9, of which 3 were waited for; matrix products, arithmetic and copies ran while one was open for 0% of the time, Pallas kernels for 42%

profile of v4, /device:TPU:2, one launch (start us, length us, event | category | flops | bytes accessed | tf_op | source)
XLA Modules:
  0.0 34.1 jit_solution(12482852563535296098)
XLA Ops:
  0.6 0.0 copy-start
  0.6 1.5 %shard_map.114 = (f32[12,64,128]{2,1,0:T(8,128)S(1)}, f32[12,64,128]{2,1,0:T(8,128)S(1)}) custom-call(f32[16,64,128]{2,1,0:T(8,128)} %h.1, f32[16,64,128]{2,1,0:T(8,128)} %a.1, f32[16,64,128]{2,1,0:T(8,128)} %n.1, f32[16,64,128]{2,1,0:T(8,128)} %s.1, f32[16,64,128]{2,1,0:T(8,128)} %p.1), custom_call_target="tpu_custom_call" | custom-call | tf_op jit(solution)/shard_map/pallas_call | solution.py:845
  2.1 1.6 %collective-permute-start.4 = (f32[12,64,128]{2,1,0:T(8,128)S(1)}, f32[12,64,128]{2,1,0:T(8,128)S(1)}, u32[]{:S(2)}, u32[]{:S(2)}) collective-permute-start(f32[12,64,128]{2,1,0:T(8,128)S(1)} %get-tuple-element.53), channel_id=1, source_target_pairs={{0,1},{1,0},{2,3},{3,2},{4,5},{5,4},{6,7},{7,6},{8,9},{9,8},{10,11... | collective-permute-start | bytes 1179656 | tf_op jit(solution)/shard_map/ppermute | solution.py:838
  3.7 0.0 collective-permute-start.5
  3.7 0.0 copy-done
  3.7 14.0 %conditional.1 = (f32[80,16,128]{2,1,0:T(8,128)S(1)}, f32[14,64,128]{2,1,0:T(8,128)S(1)}, f32[2,64,128]{2,1,0:T(8,128)S(1)}, f32[8,24,128]{2,1,0:T(8,128)S(1)}) conditional(s32[]{:T(128)} %convert_element_type.3, () %tuple.16, (f32[16,64,128]{2,1,0:T(8,128)}, f32[16,64,128]{2,1,0:T(8,128)}, f32[16,64,128]{2,1,0:T(8,128)}, f32[16,64,128]{2,1,0:T(8,128)}, ...), branch_computations={%region_0.0_spmd, %region_1.0_spmd} | conditional | bytes 1278000 | solution.py:931
  3.8 2.8 %branch_1_fun.5 = (f32[104,128]{1,0:T(8,128)S(1)}, f32[104,128]{1,0:T(8,128)S(1)}, f32[64,64]{1,0:T(8,128)S(1)}) custom-call(s32[4,128]{1,0:T(4,128)S(1)} %get-tuple-element.23.owners, f32[16,64,128]{2,1,0:T(8,128)} %get-tuple-element.16.refs_0_.h_in, f32[16,64,128]{2,1,0:T(8,128)} %get-tuple-element.17.refs_1_.a_in, ...), custom_call_target="tpu_custom_call" | custom-call | tf_op jit(solution)/shard_map/cond/branch_1_fun/pallas_call | solution.py:869
  6.5 0.6 %collective-permute-start = (f32[104,128]{1,0:T(8,128)S(1)}, f32[104,128]{1,0:T(8,128)S(1)}, u32[]{:S(2)}, u32[]{:S(2)}) collective-permute-start(f32[104,128]{1,0:T(8,128)S(1)} %get-tuple-element.28), channel_id=1, source_target_pairs={{0,4},{1,5},{2,6},{3,7},{4,0},{5,1},{6,2},{7,3},{8,12},{9,13},{10,... | collective-permute-start | bytes 159752 | tf_op jit(solution)/shard_map/cond/branch_1_fun/ppermute | solution.py:886
  7.1 0.9 %collective-permute-done.got = f32[104,128]{1,0:T(8,128)S(1)} collective-permute-done((f32[104,128]{1,0:T(8,128)S(1)}, f32[104,128]{1,0:T(8,128)S(1)}, u32[]{:S(2)}, u32[]{:S(2)}) %collective-permute-start) | collective-permute-done | bytes 53280 | tf_op jit(solution)/shard_map/cond/branch_1_fun/ppermute | solution.py:886
  8.0 3.1 %collective-permute-start.1 = (f32[64,128]{1,0:T(8,128)S(1)}, f32[64,128]{1,0:T(8,128)S(1)}, u32[]{:S(2)}, u32[]{:S(2)}) collective-permute-start(f32[64,128]{1,0:T(8,128)S(1)} %get-tuple-element.30), channel_id=1, source_target_pairs={{0,1},{1,0},{2,3},{3,2},{4,5},{5,4},{6,7},{7,6},{8,9},{9,8},{10,11... | collective-permute-start | bytes 98312 | tf_op jit(solution)/shard_map/cond/branch_1_fun/ppermute | solution.py:917
  11.1 0.0 collective-permute-start.2
  11.1 2.4 %collective-permute-start.3 = (f32[64,128]{1,0:T(8,128)S(1)}, f32[64,128]{1,0:T(8,128)S(1)}, u32[]{:S(2)}, u32[]{:S(2)}) collective-permute-start(f32[64,128]{1,0:T(8,128)S(1)} %get-tuple-element.32), channel_id=1, source_target_pairs={{0,3},{1,2},{2,1},{3,0},{4,7},{5,6},{6,5},{7,4},{8,11},{9,10},{10,... | collective-permute-start | bytes 98312 | tf_op jit(solution)/shard_map/cond/branch_1_fun/ppermute | solution.py:917
  13.5 2.5 %branch_1_fun.4 = (f32[80,16,128]{2,1,0:T(8,128)S(1)}, f32[14,64,128]{2,1,0:T(8,128)S(1)}) custom-call(f32[16,64,128]{2,1,0:T(8,128)} %get-tuple-element.16.refs_0_.h_in, f32[16,64,128]{2,1,0:T(8,128)} %get-tuple-element.17.refs_1_.a_in, f32[16,64,128]{2,1,0:T(8,128)} %get-tuple-element.18.refs_2_.n_in, f32[16,64,128]{2,1,0:T(8,128)} %get-tuple-element.19.refs_3_, ...), custom_call_target="tpu_custom_call" | custom-call | tf_op jit(solution)/shard_map/cond/branch_1_fun/pallas_call | solution.py:905
  16.0 0.0 collective-permute-done.1.refs_1_
  16.0 1.6 %collective-permute-done.2.refs_2_ = f32[64,128]{1,0:T(8,128)S(1)} collective-permute-done((f32[64,128]{1,0:T(8,128)S(1)}, f32[64,128]{1,0:T(8,128)S(1)}, u32[]{:S(2)}, u32[]{:S(2)}) %collective-permute-start.2) | collective-permute-done | bytes 32800 | tf_op jit(solution)/shard_map/cond/branch_1_fun/ppermute | solution.py:917
  17.6 0.0 collective-permute-done.3.refs_3_
  17.6 0.2 branch_1_fun.7
  17.8 0.0 collective-permute-done.4.z_e
  17.8 0.0 collective-permute-done.5.z_o
  17.8 0.1 shard_map.115
  17.9 0.1 collective-permute-start.6
  18.0 1.7 %shard_map.113.refs_3_.own = f32[80,64,128]{2,1,0:T(8,128)S(1)} custom-call(f32[16,64,128]{2,1,0:T(8,128)} %h.1, f32[16,64,128]{2,1,0:T(8,128)} %a.1, f32[16,64,128]{2,1,0:T(8,128)} %n.1, f32[16,64,128]{2,1,0:T(8,128)} %s.1, f32[16,64,128]{2,1,0:T(8,128)} %p.1), custom_call_target="tpu_custom_call" | custom-call | tf_op jit(solution)/shard_map/pallas_call | solution.py:938
  19.8 0.0 collective-permute-done.6.refs_4_
  19.8 0.8 %shard_map.116 = (f32[106,8,128]{2,1,0:T(8,128)S(1)}, f32[1792,128]{1,0:T(8,128)S(1)}, f32[320,128]{1,0:T(8,128)S(1)}, f32[320,128]{1,0:T(8,128)S(1)}) custom-call(f32[80,16,128]{2,1,0:T(8,128)S(1)} %get-tuple-element.52.rim.refs_0_, f32[14,64,128]{2,1,0:T(8,128)S(1)} %get-tuple-element.57.refs_1_, f32[26,64,128]{2,1,0:T(8,128)S(1)} %get-tuple-element.56.refs_2_.ext, ...), custom_call_target="tpu_custom_call" | custom-call | tf_op jit(solution)/shard_map/pallas_call | solution.py:946
  20.6 0.6 %collective-permute-start.7 = (f32[320,128]{1,0:T(8,128)S(1)}, f32[320,128]{1,0:T(8,128)S(1)}, u32[]{:S(2)}, u32[]{:S(2)}) collective-permute-start(f32[320,128]{1,0:T(8,128)S(1)} %get-tuple-element.64), channel_id=1, source_target_pairs={{0,8},{1,9},{2,10},{3,11},{4,12},{5,13},{6,14},{7,15},{8,0},{9,1},... | collective-permute-start | bytes 491528 | tf_op jit(solution)/shard_map/ppermute | solution.py:838
  21.2 2.5 %collective-permute-start.8 = (f32[320,128]{1,0:T(8,128)S(1)}, f32[320,128]{1,0:T(8,128)S(1)}, u32[]{:S(2)}, u32[]{:S(2)}) collective-permute-start(f32[320,128]{1,0:T(8,128)S(1)} %get-tuple-element.65), channel_id=1, source_target_pairs={{0,4},{1,5},{2,6},{3,7},{4,0},{5,1},{6,2},{7,3},{8,16},{9,17},{10,... | collective-permute-start | bytes 491528 | tf_op jit(solution)/shard_map/ppermute | solution.py:838
  23.7 7.1 %shard_map.117 = (f32[16,64,128]{2,1,0:T(8,128)S(1)}, f32[128,128]{1,0:T(8,128)S(1)}, f32[6,16,128]{2,1,0:T(8,128)}) custom-call(f32[80,64,128]{2,1,0:T(8,128)S(1)} %shard_map.113.refs_3_.own, f32[26,64,128]{2,1,0:T(8,128)S(1)} %get-tuple-element.56.refs_2_.ext, f32[106,8,128]{2,1,0:T(8,128)S(1)} %get-tuple-element.59.edge, ...), custom_call_target="tpu_custom_call" | custom-call | tf_op jit(solution)/shard_map/pallas_call | solution.py:954
  30.8 0.0 collective-permute-done.7.y_e
  30.8 0.9 %collective-permute-done.8.y_o = f32[320,128]{1,0:T(8,128)S(1)} collective-permute-done((f32[320,128]{1,0:T(8,128)S(1)}, f32[320,128]{1,0:T(8,128)S(1)}, u32[]{:S(2)}, u32[]{:S(2)}) %collective-permute-start.8) | collective-permute-done | bytes 163872 | tf_op jit(solution)/shard_map/ppermute | solution.py:838
  31.8 2.4 %shard_map.118 = f32[16,64,128]{2,1,0:T(8,128)} custom-call(f32[16,64,128]{2,1,0:T(8,128)S(1)} %get-tuple-element.61.main, f32[128,128]{1,0:T(8,128)S(1)} %get-tuple-element.62.inner, f32[1792,128]{1,0:T(8,128)S(1)} %get-tuple-element.63.strips_in, f32[320,128]{1,0:T(8,128)S(1)} %collective-permute-done.7.y_e, f32[320,128]{1,0:T(8,128)S(1)} %collective-permute-done.8.y_o), custom_call_target="tpu_custom_call" | custom-call | tf_op jit(solution)/shard_map/pallas_call | solution.py:955
  (1 shorter events, 0.0 us)
Async XLA Ops:
  0.6 3.1 %copy-start = (s32[128,4]{0,1:T(4,128)S(1)}, s32[128,4]{0,1:T(4,128)}, u32[]{:S(2)}) copy-start(s32[128,4]{0,1:T(4,128)} %param.17) | copy-start | bytes 6148
  2.1 15.7 %collective-permute-start.4 = (f32[12,64,128]{2,1,0:T(8,128)S(1)}, f32[12,64,128]{2,1,0:T(8,128)S(1)}, u32[]{:S(2)}, u32[]{:S(2)}) collective-permute-start(f32[12,64,128]{2,1,0:T(8,128)S(1)} %get-tuple-element.53), channel_id=1, source_target_pairs={{0,1},{1,0},{2,3},{3,2},{4,5},{5,4},{6,7},{7,6},{8,9},{9,8},{10,11... | collective-permute-start | bytes 1179656 | tf_op jit(solution)/shard_map/ppermute | solution.py:838
  3.7 14.1 %collective-permute-start.5 = (f32[12,64,128]{2,1,0:T(8,128)S(1)}, f32[12,64,128]{2,1,0:T(8,128)S(1)}, u32[]{:S(2)}, u32[]{:S(2)}) collective-permute-start(f32[12,64,128]{2,1,0:T(8,128)S(1)} %get-tuple-element.54), channel_id=1, source_target_pairs={{0,4},{1,2},{2,1},{3,7},{4,0},{5,6},{6,5},{7,3},{8,12},{9,10},{10,... | collective-permute-start | bytes 1179656 | tf_op jit(solution)/shard_map/ppermute | solution.py:838
  6.5 1.5 %collective-permute-start = (f32[104,128]{1,0:T(8,128)S(1)}, f32[104,128]{1,0:T(8,128)S(1)}, u32[]{:S(2)}, u32[]{:S(2)}) collective-permute-start(f32[104,128]{1,0:T(8,128)S(1)} %get-tuple-element.28), channel_id=1, source_target_pairs={{0,4},{1,5},{2,6},{3,7},{4,0},{5,1},{6,2},{7,3},{8,12},{9,13},{10,... | collective-permute-start | bytes 159752 | tf_op jit(solution)/shard_map/cond/branch_1_fun/ppermute | solution.py:886
  8.0 8.0 %collective-permute-start.1 = (f32[64,128]{1,0:T(8,128)S(1)}, f32[64,128]{1,0:T(8,128)S(1)}, u32[]{:S(2)}, u32[]{:S(2)}) collective-permute-start(f32[64,128]{1,0:T(8,128)S(1)} %get-tuple-element.30), channel_id=1, source_target_pairs={{0,1},{1,0},{2,3},{3,2},{4,5},{5,4},{6,7},{7,6},{8,9},{9,8},{10,11... | collective-permute-start | bytes 98312 | tf_op jit(solution)/shard_map/cond/branch_1_fun/ppermute | solution.py:917
  11.1 6.6 %collective-permute-start.2 = (f32[64,128]{1,0:T(8,128)S(1)}, f32[64,128]{1,0:T(8,128)S(1)}, u32[]{:S(2)}, u32[]{:S(2)}) collective-permute-start(f32[64,128]{1,0:T(8,128)S(1)} %get-tuple-element.31), channel_id=1, source_target_pairs={{0,2},{1,3},{2,0},{3,1},{4,6},{5,7},{6,4},{7,5},{8,10},{9,11},{10,... | collective-permute-start | bytes 98312 | tf_op jit(solution)/shard_map/cond/branch_1_fun/ppermute | solution.py:917
  11.1 6.5 %collective-permute-start.3 = (f32[64,128]{1,0:T(8,128)S(1)}, f32[64,128]{1,0:T(8,128)S(1)}, u32[]{:S(2)}, u32[]{:S(2)}) collective-permute-start(f32[64,128]{1,0:T(8,128)S(1)} %get-tuple-element.32), channel_id=1, source_target_pairs={{0,3},{1,2},{2,1},{3,0},{4,7},{5,6},{6,5},{7,4},{8,11},{9,10},{10,... | collective-permute-start | bytes 98312 | tf_op jit(solution)/shard_map/cond/branch_1_fun/ppermute | solution.py:917
  17.9 1.8 %collective-permute-start.6 = (f32[106,4,128]{2,1,0:T(4,128)S(1)}, f32[106,4,128]{2,1,0:T(4,128)S(1)}, u32[]{:S(2)}, u32[]{:S(2)}) collective-permute-start(f32[106,4,128]{2,1,0:T(4,128)S(1)} %get-tuple-element.58), channel_id=1, source_target_pairs={{0,4},{1,5},{2,6},{3,7},{4,0},{5,1},{6,2},{7,3},{8,12},{9,13},{10,... | collective-permute-start | bytes 651272 | tf_op jit(solution)/shard_map/ppermute | solution.py:838
  20.6 10.2 %collective-permute-start.7 = (f32[320,128]{1,0:T(8,128)S(1)}, f32[320,128]{1,0:T(8,128)S(1)}, u32[]{:S(2)}, u32[]{:S(2)}) collective-permute-start(f32[320,128]{1,0:T(8,128)S(1)} %get-tuple-element.64), channel_id=1, source_target_pairs={{0,8},{1,9},{2,10},{3,11},{4,12},{5,13},{6,14},{7,15},{8,0},{9,1},... | collective-permute-start | bytes 491528 | tf_op jit(solution)/shard_map/ppermute | solution.py:838
  21.2 10.6 %collective-permute-start.8 = (f32[320,128]{1,0:T(8,128)S(1)}, f32[320,128]{1,0:T(8,128)S(1)}, u32[]{:S(2)}, u32[]{:S(2)}) collective-permute-start(f32[320,128]{1,0:T(8,128)S(1)} %get-tuple-element.65), channel_id=1, source_target_pairs={{0,4},{1,5},{2,6},{3,7},{4,0},{5,1},{6,2},{7,3},{8,16},{9,17},{10,... | collective-permute-start | bytes 491528 | tf_op jit(solution)/shard_map/ppermute | solution.py:838

commit v5 on v4

--- a/solution.py
+++ b/solution.py
@@ -46,7 +46,21 @@
 NEAR = 4
 Z_SEND = 12
 PIECE = 8 * CAP
-Y_SEND = (PLANES * HALO + 7) // 8 * 8
+
+
+def columns_sent(p):
+    for first, count, reach in ((H0, NH, HALO), (A0, NC, HALO), (N0, NC, HALO), (S0, NC, HALO), (P0, NP, 1)):
+        if first <= p < first + count:
+            out = (count - LEVELS) // 2
+            level = p - first - out
+            away = max(0, -level, level - LEVELS + 1)
+            return max(0, reach - away)
+    return {M_LO: 1, M_HI: 1, TP: 2, RT: 2}.get(p, 0)
+
+
+Y_ROWS = 256
+Y_EXTRA = Y_ROWS // (ROWS // EDGE)
+Y_SEND = Y_ROWS // 2 + Y_EXTRA
 
 
 def omega(sweep):
@@ -92,11 +106,19 @@
     return pairs
 
 
+LOG2E = math.log2(math.e)
+HALF_LOG2E = 0.5 * LOG2E
+
+
+def saturation_of(head, alpha2, half_n, expo):
+    logx = half_n * jnp.log(alpha2 * (head * head + 0.01))
+    softer = LOG2E * jnp.log(1.0 + jnp.exp2(logx))
+    return logx, softer, jnp.exp2(-0.5 * expo * softer)
+
+
 def curves(head, alpha2, half_n, half_ks, expo):
-    logx = half_n * jnp.log(alpha2 * (head * head + 0.01))
-    softer = jnp.log(1.0 + jnp.exp(logx))
-    root = jnp.exp(-0.5 * expo * softer)
-    gap = 1.0 - jnp.exp(expo * (logx - softer))
+    logx, softer, root = saturation_of(head, alpha2, half_n, expo)
+    gap = 1.0 - jnp.exp2(expo * (logx - softer))
     return root * root, half_ks * root * (gap * gap)
 
 
@@ -106,7 +128,7 @@
 
 
 def expo_of(half_n):
-    return 1.0 - 0.5 * inverse(half_n)
+    return 1.0 - HALF_LOG2E * inverse(half_n)
 
 
 def relax(head, inflow, diag, sweep):
@@ -134,11 +156,11 @@
         for dist in (1, 2):
             alpha = level(ab, 3, dist)
             out[2 + dist] = alpha * alpha
-            out[4 + dist] = 0.5 * level(nb, 3, dist)
+            out[4 + dist] = HALF_LOG2E * level(nb, 3, dist)
             out[6 + dist] = 0.5 * level(sb, 3, dist)
         out[9] = level(pb, 1, 1)
         alpha = level(ab, 3, 3)
-        half_n = 0.5 * level(nb, 3, 3)
+        half_n = HALF_LOG2E * level(nb, 3, 3)
         out[10] = curves(level(hb, 4, 3), alpha * alpha, half_n, 0.5 * level(sb, 3, 3), expo_of(half_n))[1]
         out[11] = (hb[side, 0] + hb[side, 1] + hb[side, 2] + hb[side, 3]) * 0.25
 
@@ -205,10 +227,9 @@
         for level in range(layer * LEVELS_PER_LAYER, (layer + 1) * LEVELS_PER_LAYER):
             head = h[level]
             alpha = a[level]
-            half_n = 0.5 * n[level]
-            logx = half_n * jnp.log(alpha * alpha * (head * head + 0.01))
-            softer = jnp.log(1.0 + jnp.exp(logx))
-            saturs.append(jnp.exp(-expo_of(half_n) * softer))
+            half_n = HALF_LOG2E * n[level]
+            root = saturation_of(head, alpha * alpha, half_n, expo_of(half_n))[2]
+            saturs.append(root * root)
             heads.append(head)
         means[layer] = (saturs[0] + saturs[1] + saturs[2] + saturs[3]) * 0.25
         means[LAYERS_PER_BLOCK + layer] = (heads[0] + heads[1] + heads[2] + heads[3]) * 0.25
@@ -293,7 +314,7 @@
 
 
 def scaled(k, value):
-    return (value, value * value, 0.5 * value, 0.5 * value, value)[k]
+    return (value, value * value, HALF_LOG2E * value, 0.5 * value, value)[k]
 
 
 def packed_tile(tile, rows_of, count):
@@ -335,6 +356,36 @@
         pack[t] = packed_tile(t, lambda p: own[OWN_AT[p]] if p in OWN_AT else None, ROWS)
 
 
+def own_curves(*refs):
+    arrays, (params, ha, kc, mm, th, sem) = refs[:4], refs[4:]
+    step = 4
+    copies = []
+    for first in range(0, LEVELS, step):
+        for k, src in enumerate(arrays):
+            if k == 0:
+                dst = ha.at[pl.ds(HALO + first, step), pl.ds(8, ROWS), :]
+            else:
+                dst = params.at[pl.ds((k - 1) * LEVELS + first, step)]
+            copies.append(pltpu.make_async_copy(src.at[pl.ds(first, step)], dst, sem.at[len(copies)]))
+    for copy in copies:
+        copy.start()
+    for first in range(0, LEVELS, step):
+        for copy in copies[first // step * 4 : first // step * 4 + 4]:
+            copy.wait()
+        for level in range(first, first + step):
+            i = HALO + level
+            alpha2, half_n, half_ks = (scaled(k, params[(k - 1) * LEVELS + level]) for k in (1, 2, 3))
+            params[level] = alpha2
+            params[LEVELS + level] = half_n
+            params[2 * LEVELS + level] = half_ks
+            head = ha[i, 8 : 8 + ROWS]
+            expo = expo_of(half_n)
+            satur, cond = curves(head, alpha2, half_n, half_ks, expo)
+            kc[i, 8 : 8 + ROWS] = cond
+            mm[i - 1, 0:ROWS] = expo
+            th[i - 2, 0:ROWS] = satur
+
+
 def x_faces(count_gx, rim, z_e, z_o, tile, ext, *sends):
     def take(upper, lower):
         for got, places in ((upper, z_places(False)), (lower, z_places(True))):
@@ -362,7 +413,7 @@
         got_e, got_o = refs[4], refs[5]
     else:
         got_e, got_o = refs[4], None
-    edge, strips, send_e, send_o = refs[-4:]
+    edge, strips, send_e, send_o, lines = refs[-5:]
 
     def take(high, low):
         for p in range(PLANES):
@@ -393,25 +444,27 @@
         full = widened(jnp.concatenate([rows, last], axis=0))
         strips[t * COLS : (t + 1) * COLS, :] = full.T
 
-    def put(send, last):
-        start = 5 if last else 8
-        for p in range(PLANES):
-            send[pl.ds(p * HALO, HALO), :] = strips[pl.ds(p * SIDE + start, HALO), :]
-        rest = Y_SEND - PLANES * HALO
-        if rest:
-            send[pl.ds(PLANES * HALO, rest), :] = jnp.zeros((rest, COLS), jnp.float32)
-
-    even_y = is_even("role")
-
-    @pl.when(even_y)
-    def _():
-        put(send_e, True)
-        put(send_o, False)
-
-    @pl.when(jnp.logical_not(even_y))
-    def _():
-        put(send_e, False)
-        put(send_o, True)
+    lane = lax.broadcasted_iota(jnp.int32, (Y_ROWS // 2, COLS), 1)
+
+    def put(high, low):
+        for send, last in ((high, True), (low, False)):
+            at = 0
+            for p in range(PLANES):
+                count = columns_sent(p)
+                if count:
+                    start = p * SIDE + (8 - count if last else 8)
+                    lines[pl.ds(at, count), :] = strips[pl.ds(start, count), :]
+                    at += count
+            lines[pl.ds(at, Y_ROWS - at), :] = jnp.zeros((Y_ROWS - at, COLS), jnp.float32)
+            first, second = lines[0 : Y_ROWS // 2], lines[Y_ROWS // 2 : Y_ROWS]
+            send[0 : Y_ROWS // 2] = jnp.where(lane < ROWS, first, pltpu.roll(second, ROWS, 1))
+            extra = jnp.zeros((Y_EXTRA, COLS), jnp.float32)
+            for g in range(Y_ROWS // Y_EXTRA):
+                part = pltpu.roll(lines[g * Y_EXTRA : (g + 1) * Y_EXTRA], (EDGE * g - ROWS) % COLS, 1)
+                extra = jnp.where(lane[0:Y_EXTRA] // EDGE == g, part, extra)
+            send[Y_ROWS // 2 : Y_SEND] = extra
+
+    by_parity("role", put, send_e, send_o)
 
 
 def uptake_of(tpot, roots, head, layers, base_exp, first):
@@ -450,19 +503,21 @@
     return jnp.concatenate([value] + [value[ROWS:WIDE]] * ((COLS - WIDE) // EDGE), axis=0)
 
 
-def main_region(count_role, count_gx, count_gz, own, ext, edge, *refs):
-    land_in, refs = refs[:5], refs[5:]
-    out, inner, land_out, ha, hb, kc, mm, th, wd, sk = refs[:10]
-    heat_finish = heat(count_gx, count_gz, *land_in, land_out, *refs[10:])
+def main_region(count_role, count_gx, count_gz, params, ext, edge, *refs):
+    land_in, poro_in, refs = refs[:5], refs[5], refs[10:]
+    out, inner, land_out, ha, kc, mm, th, hb, wd, sk, poro, poro_sem = refs[:12]
+    heat_finish = heat(count_gx, count_gz, *land_in, land_out, *refs[12:])
+    poro_copy = pltpu.make_async_copy(poro_in, poro, poro_sem)
+    poro_copy.start()
     spot = Where(count_role, count_gx, count_gz)
     z_top, z_bottom = spot.z_top, spot.z_bottom
 
     def wide(p):
-        rows = own[OWN_AT[p]] if p in OWN_AT else ext[EXT_AT[p]]
-        return jnp.concatenate([rows, edge[p]], axis=0)
+        return jnp.concatenate([ext[EXT_AT[p]], edge[p]], axis=0)
 
     def wide_own(k, level):
-        return jnp.concatenate([own[k * LEVELS + level], edge[OWN[k] + level]], axis=0)
+        rows = poro[level] if k == 4 else params[(k - 1) * LEVELS + level]
+        return jnp.concatenate([rows, edge[OWN[k] + level]], axis=0)
 
     def inputs(j):
         if isinstance(j, int):
@@ -478,11 +533,13 @@
     x_low = jnp.where(row == 0, spot.x_first, 1.0)
     x_high = jnp.where(row == 7, spot.x_last, 1.0)
 
-    def fill(level, carry):
-        put(ha, HALO + level, wide_own(0, level))
-        return carry
-
-    lax.fori_loop(0, LEVELS, fill, 0, unroll=4)
+    def put_edge(ref, i, value):
+        ref[i, 8 + ROWS : 8 + WIDE] = value
+        ref[i, 0:8] = value
+        ref[i, 8 + WIDE : 16 + WIDE] = ref[i, 8:16]
+
+    for level in range(LEVELS):
+        put_edge(ha, HALO + level, edge[OWN[0] + level])
     for i in range(HALO):
         put(ha, i, wide(H0 + i))
         put(ha, HALO + LEVELS + i, wide(H0 + HALO + LEVELS + i))
@@ -505,7 +562,7 @@
         satur, cond = curves(ha[i, 8 : 8 + WIDE], alpha2, half_n, half_ks, expo)
         put(kc, i, cond)
         if poros:
-            th[j - 1] = poros[0] * satur
+            th[j - 1] = satur
 
     def later_curves(src, j):
         i = j + 1
@@ -513,7 +570,7 @@
         satur, cond = curves(src[i, 8 : 8 + WIDE], alpha2, half_n, half_ks, mm[j])
         put(kc, i, cond)
         if poros:
-            wd[j - 1] = poros[0] * satur - th[j - 1] + sk[(i + 1) // LEVELS_PER_LAYER]
+            wd[j - 1] = poros[0] * (satur - th[j - 1]) + sk[(i + 1) // LEVELS_PER_LAYER]
 
     def curves_of(body, extra):
         for j in range(HALO - 1 - extra, HALO - 1):
@@ -523,7 +580,8 @@
             body(j)
 
     def stencil(src, i0, count, sweep, store):
-        here = pl.ds(8, WIDE)
+        size = WIDE if sweep < SWEEPS - 1 else ROWS
+        here = pl.ds(8, size)
         conds = [kc[i0 + g - 1, here, :] for g in range(count + 2)]
         heads = [src[i0 + g - 1, here, :] for g in range(count + 2)]
         faces = [conds[g] + conds[g + 1] for g in range(count + 1)]
@@ -536,16 +594,17 @@
             i = i0 + g
             head, cond = heads[g + 1], conds[g + 1]
             kf_up, kf_down = faces[g], faces[g + 1]
-            kf_xm = cond + kc[i, pl.ds(7, WIDE), :]
+            kf_xm = cond + kc[i, pl.ds(7, size), :]
             kf_xm = jnp.concatenate([kf_xm[0:8] * x_low, kf_xm[8:]], axis=0)
-            kf_xp = cond + kc[i, pl.ds(9, WIDE), :]
-            kf_xp = jnp.concatenate([kf_xp[: ROWS - 8], kf_xp[ROWS - 8 : ROWS] * x_high, kf_xp[ROWS:]], axis=0)
+            kf_xp = cond + kc[i, pl.ds(9, size), :]
+            parts = [kf_xp[: ROWS - 8], kf_xp[ROWS - 8 : ROWS] * x_high] + ([kf_xp[ROWS:]] if size > ROWS else [])
+            kf_xp = jnp.concatenate(parts, axis=0)
             kf_ym = cond + pltpu.roll(cond, 1, 1)
             kf_yp = cond + pltpu.roll(cond, COLS - 1, 1)
             inflow = kf_up * (heads[g] + 1.0) + kf_down * (heads[g + 2] - 1.0)
-            inflow = inflow + (kf_xm * src[i, pl.ds(7, WIDE), :] + kf_xp * src[i, pl.ds(9, WIDE), :])
+            inflow = inflow + (kf_xm * src[i, pl.ds(7, size), :] + kf_xp * src[i, pl.ds(9, size), :])
             inflow = inflow + (kf_ym * pltpu.roll(head, 1, 1) + kf_yp * pltpu.roll(head, COLS - 1, 1))
-            lost = wd[i - 2] if sweep > 0 else sk[(i + 1) // LEVELS_PER_LAYER]
+            lost = wd[i - 2, 0:size, :] if sweep > 0 else sk[(i + 1) // LEVELS_PER_LAYER]
             diag = (1.0 + kf_up) + (kf_down + kf_xm) + (kf_xp + kf_ym) + kf_yp
             store(i, relax(head, inflow - lost, diag, sweep))
 
@@ -560,12 +619,25 @@
         extra = SWEEPS - 1 - sweep
         if extra:
             stencil(src, HALO - extra, extra, sweep, store)
-        loop(0, LEVELS // 4, lambda k: stencil(src, HALO + 4 * k, 4, sweep, store))
+        loop(0, LEVELS // 8, lambda k: stencil(src, HALO + 8 * k, 8, sweep, store))
         if extra:
             stencil(src, HALO + LEVELS, extra, sweep, store)
 
-    curves_of(first_curves, 2)
+    def edges(k):
+        return edge[OWN[k] : OWN[k] + LEVELS].reshape(LEVELS * EDGE, COLS)
+
+    half_n = edges(2)
+    expo = expo_of(half_n)
+    satur, cond = curves(edges(0), edges(1), half_n, edges(3), expo)
+    for level in range(LEVELS):
+        rows = slice(level * EDGE, (level + 1) * EDGE)
+        put_edge(kc, HALO + level, cond[rows])
+        mm[HALO - 1 + level, ROWS:WIDE] = expo[rows]
+        th[HALO - 2 + level, ROWS:WIDE] = satur[rows]
+    for j in (0, 1, NC - 2, NC - 1):
+        first_curves(j)
     levels_of(ha, 0, lambda i, value: put(hb, i, value))
+    land_sent = heat_finish()
 
     lane_wide = lax.broadcasted_iota(jnp.int32, (WIDE, COLS), 1)
     acc = jnp.zeros((WIDE, COLS), jnp.float32)
@@ -575,28 +647,45 @@
         acc = jnp.where(pick, pltpu.roll(hb[k + 1, 8 : 8 + WIDE], (lane - (COLS - 1 - NEAR)) % COLS, 1), acc)
     inner[...] = widened(acc).T
 
+    poro_copy.wait()
     curves_of(lambda j: later_curves(hb, j), 2)
     levels_of(hb, 1, lambda i, value: put(ha, i, value))
     curves_of(lambda j: later_curves(ha, j), 1)
 
     def keep(i, value):
-        out[i - HALO] = value[0:ROWS]
+        out[i - HALO] = value
 
     levels_of(ha, 2, keep)
-    heat_finish()
+    land_sent.wait()
 
 
 def edge_strips(count_role, count_gx, count_gz, main, inner, strips_in, y_e, y_o, out,
-                strips, sa, sb, sc, ks, sm, sth, swd, ssk, turn, done, sem):
+                strips, sa, sb, sc, ks, sm, sth, swd, ssk, turn, done, lines, sem):
     spot = Where(count_role, count_gx, count_gz)
     z_top, z_bottom = spot.z_top, spot.z_bottom
     f32 = jnp.float32
     strips[...] = strips_in[...]
 
+    line = lax.broadcasted_iota(jnp.int32, (Y_EXTRA, COLS), 1)
+
     def take(high, low):
-        for p in range(PLANES):
-            strips[pl.ds(p * SIDE, HALO), :] = high[pl.ds(p * HALO, HALO), :]
-            strips[pl.ds(p * SIDE + SIDE - HALO, HALO), :] = low[pl.ds(p * HALO, HALO), :]
+        for got, last in ((high, False), (low, True)):
+            extra = got[Y_ROWS // 2 : Y_SEND]
+            for g in range(Y_ROWS // Y_EXTRA):
+                first = g * Y_EXTRA % (Y_ROWS // 2)
+                rows = got[first : first + Y_EXTRA]
+                if g * Y_EXTRA >= Y_ROWS // 2:
+                    rows = pltpu.roll(rows, ROWS, 1)
+                rows = jnp.where(line < ROWS, rows, pltpu.roll(extra, (ROWS - EDGE * g) % COLS, 1))
+                rows = jnp.where(line < COLS - EDGE, rows, pltpu.roll(extra, (COLS - EDGE - EDGE * g) % COLS, 1))
+                lines[g * Y_EXTRA : (g + 1) * Y_EXTRA] = rows
+            at = 0
+            for p in range(PLANES):
+                count = columns_sent(p)
+                if count:
+                    start = p * SIDE + (SIDE - count if last else 0)
+                    strips[pl.ds(start, count), :] = lines[pl.ds(at, count), :]
+                    at += count
 
     by_parity("role", take, y_e, y_o)
 
@@ -647,12 +736,11 @@
             start, stop = max(i, 2), min(i + count, NH - 2)
             if stop > start:
                 part = satur[(start - i) * SIDE : (stop - i) * SIDE]
-                water = strip(P0 + start - 2, stop - start) * part
                 at = rows_of(start - 2, stop - start)
                 if sweep == 0:
-                    sth[at, :] = water
+                    sth[at, :] = part
                 else:
-                    swd[at, :] = water - sth[at, :]
+                    swd[at, :] = strip(P0 + start - 2, stop - start) * (part - sth[at, :])
             i += count
 
     def strip_stencil(src, dst, lo, hi, sweep):
@@ -695,25 +783,28 @@
     strip_curves(sa, 1, NH - 1, 1)
     strip_stencil(sa, sb, 2, NH - 2, 1)
     strip_curves(sb, 2, NH - 2, 2)
-    strip_stencil(sb, sc, 3, NH - 3, 2)
-
-    pieces = [sc[i * SIDE + 8 - HALO : i * SIDE + 8 + HALO, :] for i in range(HALO, HALO + LEVELS)]
-    pieces.append(jnp.zeros((COLS - 2 * HALO * LEVELS, COLS), f32))
-    turn[...] = jnp.concatenate(pieces, axis=0).T[0:ROWS]
+
     lane_rows = lax.broadcasted_iota(jnp.int32, (ROWS, COLS), 1)
     outer = (lane_rows < HALO) | (lane_rows >= COLS - HALO)
     copies = []
-    for level in range(LEVELS):
-        moved = pltpu.roll(turn[...], (COLS - HALO - 2 * HALO * level) % COLS, 1)
-        done[level] = jnp.where(outer, moved, main[level])
-        copy = pltpu.make_async_copy(done.at[level], out.at[level], sem.at[level])
-        copy.start()
-        copies.append(copy)
+    half = LEVELS // 2
+    for first in (0, half):
+        strip_stencil(sb, sc, HALO + first, HALO + first + half, 2)
+        pieces = [sc[i * SIDE + 8 - HALO : i * SIDE + 8 + HALO, :] for i in range(HALO + first, HALO + first + half)]
+        pieces.append(jnp.zeros((COLS - 2 * HALO * half, COLS), f32))
+        turn[...] = jnp.concatenate(pieces, axis=0).T[0:ROWS]
+        for k in range(half):
+            moved = pltpu.roll(turn[...], (COLS - HALO - 2 * HALO * k) % COLS, 1)
+            level = first + k
+            done[level] = jnp.where(outer, moved, main[level])
+            copy = pltpu.make_async_copy(done.at[level], out.at[level], sem.at[level])
+            copy.start()
+            copies.append(copy)
     for copy in copies:
         copy.wait()
 
 
-def heat(count_gx, count_gz, y, temp_in, tr_in, air_in, rt_in, out, sat, head, temp, tr, air, rt, sem):
+def heat(count_gx, count_gz, y, temp_in, tr_in, air_in, rt_in, land_out, out, sat, head, temp, tr, air, rt, sem, out_sem):
     copies = []
     for src, dst in ((temp_in, temp), (tr_in, tr), (air_in, air), (rt_in, rt)):
         copy = pltpu.make_async_copy(src, dst, sem.at[len(copies)])
@@ -751,6 +842,9 @@
                 below = pltpu.roll(new, layers - 1, 0)
                 new = new + 0.2 * (k_above * (above - new) + k_below * (below - new)) - 0.3 * uptake
             out[slot] = jnp.where(sat[slot] >= 0.0, new, old)
+        sent = pltpu.make_async_copy(out, land_out, out_sem)
+        sent.start()
+        return sent
 
     return finish
 
@@ -768,9 +862,12 @@
     )
 
 
+DEEP = WIDE + 16
+START_SHAPES = [(NH, DEEP, COLS), (NH, DEEP, COLS), (NC, WIDE, COLS), (NP, WIDE, COLS)]
+
+
 def main_call(count_role, count_gx, count_gz):
     f32 = jnp.float32
-    deep = WIDE + 16
     slots = count_gx * CAP
     land_shape = (slots, LAYERS_PER_BLOCK * count_gz, COLS)
     return pl.pallas_call(
@@ -779,17 +876,18 @@
             pltpu.VMEM((LEVELS, ROWS, COLS), f32),
             pltpu.VMEM((COLS, COLS), f32),
             jax.ShapeDtypeStruct(land_shape, f32),
-        ],
-        in_specs=[VMEM] * 4 + [HBM] * 4,
-        out_specs=[VMEM] * 3,
+        ]
+        + [pltpu.VMEM(shape, f32) for shape in START_SHAPES],
+        in_specs=[VMEM] * 4 + [HBM] * 5 + [VMEM] * 4,
+        out_specs=[VMEM] * 2 + [HBM] + [VMEM] * 4,
+        input_output_aliases={9 + k: 3 + k for k in range(4)},
         scratch_shapes=[
-            pltpu.VMEM((NH, deep, COLS), f32),
-            pltpu.VMEM((NH, deep, COLS), f32),
-            pltpu.VMEM((NH, deep, COLS), f32),
-            pltpu.VMEM((NC, WIDE, COLS), f32),
-            pltpu.VMEM((NP, WIDE, COLS), f32),
+            pltpu.VMEM((NH, DEEP, COLS), f32),
             pltpu.VMEM((NP, WIDE, COLS), f32),
             pltpu.VMEM((LAYERS_PER_BLOCK + 2, WIDE, COLS), f32),
+            pltpu.VMEM((LEVELS, ROWS, COLS), f32),
+            pltpu.SemaphoreType.DMA(()),
+            pltpu.VMEM(land_shape, f32),
             pltpu.VMEM(land_shape, f32),
             pltpu.VMEM(land_shape, f32),
             pltpu.VMEM(land_shape, f32),
@@ -797,6 +895,7 @@
             pltpu.VMEM((slots, 1, COLS), f32),
             pltpu.VMEM((slots, 1, COLS), jnp.int32),
             pltpu.SemaphoreType.DMA((4,)),
+            pltpu.SemaphoreType.DMA(()),
         ],
         compiler_params=pltpu.CompilerParams(vmem_limit_bytes=16 * MIB),
     )
@@ -821,6 +920,7 @@
             pltpu.VMEM(((LAYERS_PER_BLOCK + 2) * SIDE, COLS), f32),
             pltpu.VMEM((ROWS, COLS), f32),
             pltpu.VMEM((LEVELS, ROWS, COLS), f32),
+            pltpu.VMEM((Y_ROWS, COLS), f32),
             pltpu.SemaphoreType.DMA((LEVELS,)),
         ],
         compiler_params=pltpu.CompilerParams(vmem_limit_bytes=16 * MIB),
@@ -935,23 +1035,24 @@
         [(len(EXT_AT), ROWS, COLS)] + [x_shape] * x_count,
         [VMEM] * 4,
     )(rim, z_e, z_o, tile)
-    (own,) = call(
-        own_planes,
-        [(len(OWN_AT), ROWS, COLS)],
-        [HBM] * 5,
-        [pltpu.SemaphoreType.DMA((5,))],
-    )(h, a, n, s, p)
+    params, *start = call(
+        own_curves,
+        [(3 * LEVELS, ROWS, COLS)] + START_SHAPES,
+        [HBM] * 4,
+        [pltpu.SemaphoreType.DMA((LEVELS,))],
+    )(h, a, n, s)
     x_got = [swap(value, "gx", bool(k)) for k, value in enumerate(x_sends)]
 
     edge, strips, y_send_e, y_send_o = call(
         functools.partial(y_faces, count_gx),
         [(PLANES, EDGE, COLS), (PACKS * COLS, COLS), (Y_SEND, COLS), (Y_SEND, COLS)],
         [VMEM] * 3 + [ANY] + [VMEM] * x_count,
-    )(rim, pack, ext, own, *x_got)
+        [pltpu.VMEM((Y_ROWS, COLS), f32)],
+    )(rim, pack, ext, params, *x_got)
     y_e = swap(y_send_e, "role", False)
     y_o = swap(y_send_o, "role", True) if count_role > 2 else y_e
 
-    main, inner, land_new = main_call(*sizes)(own, ext, edge, y, land_temp, tr, air, rt)
+    main, inner, land_new, *_ = main_call(*sizes)(params, ext, edge, y, land_temp, tr, air, rt, p, *start)
     head = strip_call(*sizes)(main, inner, strips, y_e, y_o)
     return (head, land_new[None, None])
 

time: 34.4 us -> 32.5 us (0.945)
  Pallas kernels: 19.1 us -> 18 us
  waiting for transfers between devices: 3.43 us -> 2.51 us
    pallas_call x2, Pallas kernels: 8.85 us -> 7.51 us  [the longest x1 5.63 us: local(): main_call(*sizes)(params, ext, edge, y, land_temp, tr, air, rt, p, *start)]
    ppermute x5, waiting for transfers between devices: 0.94 us -> 0.01 us  [swap(): return lax.ppermute(value, AXES, pairing(sizes, axis, odd))]
  transfers between devices with their start and end apart: 9 -> 9, of which waited for: 3 -> 2; matrix products, arithmetic and copies ran while one was open for 0% -> 0% of each run, Pallas kernels for 42% -> 40%
where the time goes in v5:
time: 32.5 us; the launch traced here: 32.1 us
  Pallas kernels  18 us (55%)
  starting transfers between devices  10.8 us (33%)
  waiting for transfers between devices  2.51 us (8%)
  between operations  0.74 us (2%)
    pallas_call x1, Pallas kernels, local(): main_call(*sizes)(params, ext, edge, y, land_temp, tr, air, rt, p, *start)  5.63 us
    ppermute x3, starting transfers between devices, land_stage(): lax.ppermute(parts[dist], AXES, xor_pairs(sizes, 'gz', dist))  5.5 us
    ppermute x5, starting transfers between devices, swap(): return lax.ppermute(value, AXES, pairing(sizes, axis, odd))  4.76 us
    pallas_call x1, Pallas kernels, land_stage(): call(functools.partial(land_pack, count_gx, count_gz), [(packed, COLS), (...  2.76 us
    pallas_call x1, Pallas kernels, local(): head = strip_call(*sizes)(main, inner, strips, y_e, y_o)  2.53 us
    pallas_call x1, Pallas kernels, land_stage(): call(own_part, own_shapes, [HBM] * 5, [pltpu.VMEM((len(OWN_AT), ROWS, COL...  2.5 us
    pallas_call x1, Pallas kernels, local(): call(own_curves, [(3 * LEVELS, ROWS, COLS)] + START_SHAPES, [HBM] * 4, [p...  1.88 us
    ppermute x3, waiting for transfers between devices, land_stage(): lax.ppermute(parts[dist], AXES, xor_pairs(sizes, 'gz', dist))  1.61 us
  transfers between devices with their start and end apart: 9, of which 2 were waited for; matrix products, arithmetic and copies ran while one was open for 0% of the time, Pallas kernels for 40%

profile of v5, /device:TPU:2, one launch (start us, length us, event | category | flops | bytes accessed | tf_op | source)
XLA Modules:
  0.0 32.1 jit_solution(10296487188145126555)
XLA Ops:
  0.6 0.0 copy-start
  0.6 1.5 %shard_map.114 = (f32[12,64,128]{2,1,0:T(8,128)S(1)}, f32[12,64,128]{2,1,0:T(8,128)S(1)}) custom-call(f32[16,64,128]{2,1,0:T(8,128)} %h.1, f32[16,64,128]{2,1,0:T(8,128)} %a.1, f32[16,64,128]{2,1,0:T(8,128)} %n.1, f32[16,64,128]{2,1,0:T(8,128)} %s.1, f32[16,64,128]{2,1,0:T(8,128)} %refs_5_.1), custom_call_target="tpu_custom_call" | custom-call | tf_op jit(solution)/shard_map/pallas_call | solution.py:945
  2.1 1.6 %collective-permute-start.4 = (f32[12,64,128]{2,1,0:T(8,128)S(1)}, f32[12,64,128]{2,1,0:T(8,128)S(1)}, u32[]{:S(2)}, u32[]{:S(2)}) collective-permute-start(f32[12,64,128]{2,1,0:T(8,128)S(1)} %get-tuple-element.59), channel_id=1, source_target_pairs={{0,1},{1,0},{2,3},{3,2},{4,5},{5,4},{6,7},{7,6},{8,9},{9,8},{10,11... | collective-permute-start | bytes 1179656 | tf_op jit(solution)/shard_map/ppermute | solution.py:938
  3.7 0.0 collective-permute-start.5
  3.7 0.0 copy-done
  3.7 14.0 %conditional.1 = (f32[80,16,128]{2,1,0:T(8,128)S(1)}, f32[14,64,128]{2,1,0:T(8,128)S(1)}, f32[2,64,128]{2,1,0:T(8,128)S(1)}, f32[8,24,128]{2,1,0:T(8,128)S(1)}) conditional(s32[]{:T(128)} %convert_element_type.3, () %tuple.16, (f32[16,64,128]{2,1,0:T(8,128)}, f32[16,64,128]{2,1,0:T(8,128)}, f32[16,64,128]{2,1,0:T(8,128)}, f32[16,64,128]{2,1,0:T(8,128)}, ...), branch_computations={%region_0.0_spmd, %region_1.0_spmd} | conditional | bytes 1278000 | solution.py:1031
  3.7 2.8 %branch_1_fun.5 = (f32[104,128]{1,0:T(8,128)S(1)}, f32[104,128]{1,0:T(8,128)S(1)}, f32[64,64]{1,0:T(8,128)S(1)}) custom-call(s32[4,128]{1,0:T(4,128)S(1)} %get-tuple-element.23.owners, f32[16,64,128]{2,1,0:T(8,128)} %get-tuple-element.16.refs_0_.h_in, f32[16,64,128]{2,1,0:T(8,128)} %get-tuple-element.17.refs_1_.a_in, ...), custom_call_target="tpu_custom_call" | custom-call | tf_op jit(solution)/shard_map/cond/branch_1_fun/pallas_call | solution.py:969
  6.5 0.6 %collective-permute-start = (f32[104,128]{1,0:T(8,128)S(1)}, f32[104,128]{1,0:T(8,128)S(1)}, u32[]{:S(2)}, u32[]{:S(2)}) collective-permute-start(f32[104,128]{1,0:T(8,128)S(1)} %get-tuple-element.28), channel_id=1, source_target_pairs={{0,4},{1,5},{2,6},{3,7},{4,0},{5,1},{6,2},{7,3},{8,12},{9,13},{10,... | collective-permute-start | bytes 159752 | tf_op jit(solution)/shard_map/cond/branch_1_fun/ppermute | solution.py:986
  7.1 0.9 %collective-permute-done.got = f32[104,128]{1,0:T(8,128)S(1)} collective-permute-done((f32[104,128]{1,0:T(8,128)S(1)}, f32[104,128]{1,0:T(8,128)S(1)}, u32[]{:S(2)}, u32[]{:S(2)}) %collective-permute-start) | collective-permute-done | bytes 53280 | tf_op jit(solution)/shard_map/cond/branch_1_fun/ppermute | solution.py:986
  8.0 3.1 %collective-permute-start.1 = (f32[64,128]{1,0:T(8,128)S(1)}, f32[64,128]{1,0:T(8,128)S(1)}, u32[]{:S(2)}, u32[]{:S(2)}) collective-permute-start(f32[64,128]{1,0:T(8,128)S(1)} %get-tuple-element.30), channel_id=1, source_target_pairs={{0,1},{1,0},{2,3},{3,2},{4,5},{5,4},{6,7},{7,6},{8,9},{9,8},{10,11... | collective-permute-start | bytes 98312 | tf_op jit(solution)/shard_map/cond/branch_1_fun/ppermute | solution.py:1017
  11.0 0.0 collective-permute-start.2
  11.1 2.4 %collective-permute-start.3 = (f32[64,128]{1,0:T(8,128)S(1)}, f32[64,128]{1,0:T(8,128)S(1)}, u32[]{:S(2)}, u32[]{:S(2)}) collective-permute-start(f32[64,128]{1,0:T(8,128)S(1)} %get-tuple-element.32), channel_id=1, source_target_pairs={{0,3},{1,2},{2,1},{3,0},{4,7},{5,6},{6,5},{7,4},{8,11},{9,10},{10,... | collective-permute-start | bytes 98312 | tf_op jit(solution)/shard_map/cond/branch_1_fun/ppermute | solution.py:1017
  13.5 2.5 %branch_1_fun.4 = (f32[80,16,128]{2,1,0:T(8,128)S(1)}, f32[14,64,128]{2,1,0:T(8,128)S(1)}) custom-call(f32[16,64,128]{2,1,0:T(8,128)} %get-tuple-element.16.refs_0_.h_in, f32[16,64,128]{2,1,0:T(8,128)} %get-tuple-element.17.refs_1_.a_in, f32[16,64,128]{2,1,0:T(8,128)} %get-tuple-element.18.refs_2_.n_in, f32[16,64,128]{2,1,0:T(8,128)} %get-tuple-element.19.refs_3_, ...), custom_call_target="tpu_custom_call" | custom-call | tf_op jit(solution)/shard_map/cond/branch_1_fun/pallas_call | solution.py:1005
  16.0 0.0 collective-permute-done.1.refs_1_
  16.0 1.6 %collective-permute-done.2.refs_2_ = f32[64,128]{1,0:T(8,128)S(1)} collective-permute-done((f32[64,128]{1,0:T(8,128)S(1)}, f32[64,128]{1,0:T(8,128)S(1)}, u32[]{:S(2)}, u32[]{:S(2)}) %collective-permute-start.2) | collective-permute-done | bytes 32800 | tf_op jit(solution)/shard_map/cond/branch_1_fun/ppermute | solution.py:1017
  17.6 0.0 collective-permute-done.3.refs_3_
  17.6 0.2 branch_1_fun.7
  17.8 0.0 collective-permute-done.4.z_e
  17.8 0.0 collective-permute-done.5.z_o
  17.8 0.1 shard_map.115
  17.9 0.1 collective-permute-start.6
  18.0 1.9 %shard_map.113 = (f32[48,64,128]{2,1,0:T(8,128)S(1)}, f32[22,88,128]{2,1,0:T(8,128)S(1)}, f32[22,88,128]{2,1,0:T(8,128)S(1)}, f32[20,72,128]{2,1,0:T(8,128)S(1)}, f32[18,72,128]{2,1,0:T(8,128)S(1)}) custom-call(f32[16,64,128]{2,1,0:T(8,128)} %h.1, f32[16,64,128]{2,1,0:T(8,128)} %a.1, f32[16,64,128]{2,1,0:T(8,128)} %n.1, f32[16,64,128]{2,1,0:T(8,128)} %s.1), custom_call_target="tpu_custom_call" | custom-call | tf_op jit(solution)/shard_map/pallas_call | solution.py:1038
  19.9 0.0 collective-permute-done.6.refs_4_
  19.9 1.0 %shard_map.116 = (f32[106,8,128]{2,1,0:T(8,128)S(1)}, f32[1792,128]{1,0:T(8,128)S(1)}, f32[160,128]{1,0:T(8,128)S(1)}, f32[160,128]{1,0:T(8,128)S(1)}) custom-call(f32[80,16,128]{2,1,0:T(8,128)S(1)} %get-tuple-element.58.rim.refs_0_, f32[14,64,128]{2,1,0:T(8,128)S(1)} %get-tuple-element.63.refs_1_, f32[26,64,128]{2,1,0:T(8,128)S(1)} %get-tuple-element.62.refs_2_.ext, ...), custom_call_target="tpu_custom_call" | custom-call | tf_op jit(solution)/shard_map/pallas_call | solution.py:1046
  20.9 0.6 %collective-permute-start.7 = (f32[160,128]{1,0:T(8,128)S(1)}, f32[160,128]{1,0:T(8,128)S(1)}, u32[]{:S(2)}, u32[]{:S(2)}) collective-permute-start(f32[160,128]{1,0:T(8,128)S(1)} %get-tuple-element.74), channel_id=1, source_target_pairs={{0,8},{1,9},{2,10},{3,11},{4,12},{5,13},{6,14},{7,15},{8,0},{9,1},... | collective-permute-start | bytes 245768 | tf_op jit(solution)/shard_map/ppermute | solution.py:938
  21.5 2.5 %collective-permute-start.8 = (f32[160,128]{1,0:T(8,128)S(1)}, f32[160,128]{1,0:T(8,128)S(1)}, u32[]{:S(2)}, u32[]{:S(2)}) collective-permute-start(f32[160,128]{1,0:T(8,128)S(1)} %get-tuple-element.75), channel_id=1, source_target_pairs={{0,4},{1,5},{2,6},{3,7},{4,0},{5,1},{6,2},{7,3},{8,16},{9,17},{10,... | collective-permute-start | bytes 245768 | tf_op jit(solution)/shard_map/ppermute | solution.py:938
  24.0 5.6 %shard_map.117 = (f32[16,64,128]{2,1,0:T(8,128)S(1)}, f32[128,128]{1,0:T(8,128)S(1)}, f32[6,16,128]{2,1,0:T(8,128)}, f32[22,88,128]{2,1,0:T(8,128)S(1)}, f32[22,...) custom-call(f32[48,64,128]{2,1,0:T(8,128)S(1)} %get-tuple-element.57, ...), custom_call_target="tpu_custom_call", output_to_operand_aliasing={{3}: (9, {}), {4}: (10, {}), {5}: (11, {}), {6}: (12, {})} | custom-call | tf_op jit(solution)/shard_map/pallas_call | solution.py:1055
  29.6 0.0 collective-permute-done.7.y_e
  29.6 0.0 collective-permute-done.8.y_o
  29.6 2.5 %shard_map.118 = f32[16,64,128]{2,1,0:T(8,128)} custom-call(f32[16,64,128]{2,1,0:T(8,128)S(1)} %get-tuple-element.71.main, f32[128,128]{1,0:T(8,128)S(1)} %get-tuple-element.72.inner, f32[1792,128]{1,0:T(8,128)S(1)} %get-tuple-element.73.strips_in, f32[160,128]{1,0:T(8,128)S(1)} %collective-permute-done.7.y_e, f32[160,128]{1,0:T(8,128)S(1)} %collective-permute-done.8.y_o), custom_call_target="tpu_custom_call" | custom-call | tf_op jit(solution)/shard_map/pallas_call | solution.py:1056
  (1 shorter events, 0.0 us)
Async XLA Ops:
  0.6 3.1 %copy-start = (s32[128,4]{0,1:T(4,128)S(1)}, s32[128,4]{0,1:T(4,128)}, u32[]{:S(2)}) copy-start(s32[128,4]{0,1:T(4,128)} %param.17) | copy-start | bytes 6148
  2.1 15.7 %collective-permute-start.4 = (f32[12,64,128]{2,1,0:T(8,128)S(1)}, f32[12,64,128]{2,1,0:T(8,128)S(1)}, u32[]{:S(2)}, u32[]{:S(2)}) collective-permute-start(f32[12,64,128]{2,1,0:T(8,128)S(1)} %get-tuple-element.59), channel_id=1, source_target_pairs={{0,1},{1,0},{2,3},{3,2},{4,5},{5,4},{6,7},{7,6},{8,9},{9,8},{10,11... | collective-permute-start | bytes 1179656 | tf_op jit(solution)/shard_map/ppermute | solution.py:938
  3.7 14.1 %collective-permute-start.5 = (f32[12,64,128]{2,1,0:T(8,128)S(1)}, f32[12,64,128]{2,1,0:T(8,128)S(1)}, u32[]{:S(2)}, u32[]{:S(2)}) collective-permute-start(f32[12,64,128]{2,1,0:T(8,128)S(1)} %get-tuple-element.60), channel_id=1, source_target_pairs={{0,4},{1,2},{2,1},{3,7},{4,0},{5,6},{6,5},{7,3},{8,12},{9,10},{10,... | collective-permute-start | bytes 1179656 | tf_op jit(solution)/shard_map/ppermute | solution.py:938
  6.5 1.5 %collective-permute-start = (f32[104,128]{1,0:T(8,128)S(1)}, f32[104,128]{1,0:T(8,128)S(1)}, u32[]{:S(2)}, u32[]{:S(2)}) collective-permute-start(f32[104,128]{1,0:T(8,128)S(1)} %get-tuple-element.28), channel_id=1, source_target_pairs={{0,4},{1,5},{2,6},{3,7},{4,0},{5,1},{6,2},{7,3},{8,12},{9,13},{10,... | collective-permute-start | bytes 159752 | tf_op jit(solution)/shard_map/cond/branch_1_fun/ppermute | solution.py:986
  8.0 8.0 %collective-permute-start.1 = (f32[64,128]{1,0:T(8,128)S(1)}, f32[64,128]{1,0:T(8,128)S(1)}, u32[]{:S(2)}, u32[]{:S(2)}) collective-permute-start(f32[64,128]{1,0:T(8,128)S(1)} %get-tuple-element.30), channel_id=1, source_target_pairs={{0,1},{1,0},{2,3},{3,2},{4,5},{5,4},{6,7},{7,6},{8,9},{9,8},{10,11... | collective-permute-start | bytes 98312 | tf_op jit(solution)/shard_map/cond/branch_1_fun/ppermute | solution.py:1017
  11.0 6.6 %collective-permute-start.2 = (f32[64,128]{1,0:T(8,128)S(1)}, f32[64,128]{1,0:T(8,128)S(1)}, u32[]{:S(2)}, u32[]{:S(2)}) collective-permute-start(f32[64,128]{1,0:T(8,128)S(1)} %get-tuple-element.31), channel_id=1, source_target_pairs={{0,2},{1,3},{2,0},{3,1},{4,6},{5,7},{6,4},{7,5},{8,10},{9,11},{10,... | collective-permute-start | bytes 98312 | tf_op jit(solution)/shard_map/cond/branch_1_fun/ppermute | solution.py:1017
  11.1 6.5 %collective-permute-start.3 = (f32[64,128]{1,0:T(8,128)S(1)}, f32[64,128]{1,0:T(8,128)S(1)}, u32[]{:S(2)}, u32[]{:S(2)}) collective-permute-start(f32[64,128]{1,0:T(8,128)S(1)} %get-tuple-element.32), channel_id=1, source_target_pairs={{0,3},{1,2},{2,1},{3,0},{4,7},{5,6},{6,5},{7,4},{8,11},{9,10},{10,... | collective-permute-start | bytes 98312 | tf_op jit(solution)/shard_map/cond/branch_1_fun/ppermute | solution.py:1017
  17.9 2.0 %collective-permute-start.6 = (f32[106,4,128]{2,1,0:T(4,128)S(1)}, f32[106,4,128]{2,1,0:T(4,128)S(1)}, u32[]{:S(2)}, u32[]{:S(2)}) collective-permute-start(f32[106,4,128]{2,1,0:T(4,128)S(1)} %get-tuple-element.64), channel_id=1, source_target_pairs={{0,4},{1,5},{2,6},{3,7},{4,0},{5,1},{6,2},{7,3},{8,12},{9,13},{10,... | collective-permute-start | bytes 651272 | tf_op jit(solution)/shard_map/ppermute | solution.py:938
  20.9 8.7 %collective-permute-start.7 = (f32[160,128]{1,0:T(8,128)S(1)}, f32[160,128]{1,0:T(8,128)S(1)}, u32[]{:S(2)}, u32[]{:S(2)}) collective-permute-start(f32[160,128]{1,0:T(8,128)S(1)} %get-tuple-element.74), channel_id=1, source_target_pairs={{0,8},{1,9},{2,10},{3,11},{4,12},{5,13},{6,14},{7,15},{8,0},{9,1},... | collective-permute-start | bytes 245768 | tf_op jit(solution)/shard_map/ppermute | solution.py:938
  21.5 8.1 %collective-permute-start.8 = (f32[160,128]{1,0:T(8,128)S(1)}, f32[160,128]{1,0:T(8,128)S(1)}, u32[]{:S(2)}, u32[]{:S(2)}) collective-permute-start(f32[160,128]{1,0:T(8,128)S(1)} %get-tuple-element.75), channel_id=1, source_target_pairs={{0,4},{1,5},{2,6},{3,7},{4,0},{5,1},{6,2},{7,3},{8,16},{9,17},{10,... | collective-permute-start | bytes 245768 | tf_op jit(solution)/shard_map/ppermute | solution.py:938

commit v6 on v5

--- a/solution.py
+++ b/solution.py
@@ -16,7 +16,6 @@
 HALO = SWEEPS
 AXES = ("role", "gx", "gz")
 VMEM = pl.BlockSpec(memory_space=pltpu.VMEM)
-SMEM = pl.BlockSpec(memory_space=pltpu.SMEM)
 HBM = pl.BlockSpec(memory_space=pltpu.HBM)
 ANY = pl.BlockSpec(memory_space=pl.ANY)
 MIB = 1024 * 1024
@@ -138,50 +137,50 @@
 
 def z_faces(h, a, n, s, p, out_e, out_o, hb, ab, nb, sb, pb, sem):
     copies = []
-    for side in range(2):
-        for src, dst, count in ((h, hb, 4), (a, ab, 3), (n, nb, 3), (s, sb, 3), (p, pb, 1)):
+    for src, dst, count in ((h, hb, 4), (a, ab, 3), (n, nb, 3), (s, sb, 3), (p, pb, 1)):
+        for side in range(2):
             start = 0 if side == 0 else LEVELS - count
             copy = pltpu.make_async_copy(src.at[pl.ds(start, count)], dst.at[side], sem.at[len(copies)])
             copy.start()
             copies.append(copy)
-    for copy in copies:
-        copy.wait()
-
-    def put(out, side):
-        def level(buf, count, dist):
-            return buf[side, dist - 1 if side == 0 else count - dist]
-
+    def level(buf, side, count, dist):
+        return buf[side, dist - 1 if side == 0 else count - dist]
+
+    def put_heads(out, side):
         for dist in (1, 2, 3):
-            out[dist - 1] = level(hb, 4, dist)
+            out[dist - 1] = level(hb, side, 4, dist)
+        out[11] = (hb[side, 0] + hb[side, 1] + hb[side, 2] + hb[side, 3]) * 0.25
+
+    def put_rest(out, side):
         for dist in (1, 2):
-            alpha = level(ab, 3, dist)
+            alpha = level(ab, side, 3, dist)
             out[2 + dist] = alpha * alpha
-            out[4 + dist] = HALF_LOG2E * level(nb, 3, dist)
-            out[6 + dist] = 0.5 * level(sb, 3, dist)
-        out[9] = level(pb, 1, 1)
-        alpha = level(ab, 3, 3)
-        half_n = HALF_LOG2E * level(nb, 3, 3)
-        out[10] = curves(level(hb, 4, 3), alpha * alpha, half_n, 0.5 * level(sb, 3, 3), expo_of(half_n))[1]
-        out[11] = (hb[side, 0] + hb[side, 1] + hb[side, 2] + hb[side, 3]) * 0.25
-
-    even = is_even("gz")
-
-    @pl.when(even)
-    def _():
-        put(out_e, 1)
-        put(out_o, 0)
-
-    @pl.when(jnp.logical_not(even))
-    def _():
-        put(out_e, 0)
-        put(out_o, 1)
-
-
-def land_pack(count_gx, count_gz, owners, h_in, a_in, n_in, tr_in, rt_in, send, keep, hot,
-              means, counts, slots, h, a, n, tr, rt, sem):
+            out[4 + dist] = HALF_LOG2E * level(nb, side, 3, dist)
+            out[6 + dist] = 0.5 * level(sb, side, 3, dist)
+        out[9] = level(pb, side, 1, 1)
+        alpha = level(ab, side, 3, 3)
+        half_n = HALF_LOG2E * level(nb, side, 3, 3)
+        half_ks = 0.5 * level(sb, side, 3, 3)
+        out[10] = curves(level(hb, side, 4, 3), alpha * alpha, half_n, half_ks, expo_of(half_n))[1]
+
+    for waited, put in ((copies[:2], put_heads), (copies[2:], put_rest)):
+        for copy in waited:
+            copy.wait()
+
+        def both(first, second):
+            put(out_e, first)
+            put(out_o, second)
+
+        by_parity("gz", both, 1, 0)
+
+
+def land_pack(count_gx, count_gz, owners_in, h_in, a_in, n_in, tr_in, rt_in, send, keep, hot,
+              owners, means, counts, slots, h, a, n, tr, rt, sem, owners_sem):
     groups = count_gx * count_gz
     me_role, me_gx = place("role"), place("gx")
     me = me_gx * count_gz + place("gz")
+    owners_copy = pltpu.make_async_copy(owners_in, owners, owners_sem)
+    owners_copy.start()
     copies = []
     for layer in range(LAYERS_PER_BLOCK):
         some = pl.ds(layer * LEVELS_PER_LAYER, LEVELS_PER_LAYER)
@@ -218,7 +217,8 @@
 
         return carry
 
-    lax.fori_loop(0, ROWS, step, 0)
+    owners_copy.wait()
+    lax.fori_loop(0, ROWS, step, 0, unroll=8)
     for layer in range(LAYERS_PER_BLOCK):
         for copy in copies[3 * layer : 3 * layer + 3]:
             copy.wait()
@@ -937,7 +937,7 @@
     def swap(value, axis, odd):
         return lax.ppermute(value, AXES, pairing(sizes, axis, odd))
 
-    owners = tile_owner.T
+    owners = pltpu.with_memory_space_constraint(tile_owner.T, pltpu.HBM)
     land = (land_temp[0, 0], tr[0, 0, :, None], air[0, 0, :, None], rt[0, 0, :, None])
     h, a, n, s, p = (pltpu.with_memory_space_constraint(x, pltpu.HBM) for x in (h, a, n, s, p))
     land_temp, tr, air, rt = (pltpu.with_memory_space_constraint(x, pltpu.HBM) for x in land)
@@ -969,8 +969,9 @@
         send, keep, hot = call(
             functools.partial(land_pack, count_gx, count_gz),
             [(packed, COLS), (packed, COLS), (ROWS, groups * 8)],
-            [SMEM] + [HBM] * 5,
+            [HBM] * 6,
             [
+                pltpu.SMEM(tile_owner.shape[::-1], jnp.int32),
                 pltpu.VMEM((2 * LAYERS_PER_BLOCK, ROWS, COLS), f32),
                 pltpu.SMEM((groups,), jnp.int32),
                 pltpu.SMEM((groups * CAP,), jnp.int32),
@@ -980,6 +981,7 @@
                 pltpu.VMEM((slots, 1, COLS), f32),
                 pltpu.VMEM((slots, 1, COLS), jnp.int32),
                 pltpu.SemaphoreType.DMA((3 * LAYERS_PER_BLOCK + 2,)),
+                pltpu.SemaphoreType.DMA(()),
             ],
         )(owners, h, a, n, tr, rt)
 

time: 32.5 us -> 32.5 us (level)
  Pallas kernels: 18 us -> 17.3 us
  waiting for transfers between devices: 2.51 us -> 3.18 us
    ppermute x3, waiting for transfers between devices: 1.61 us -> 2.29 us  [land_stage(): lax.ppermute(parts[dist], AXES, xor_pairs(sizes, 'gz', dist))]
    pallas_call x1, Pallas kernels: 2.76 us -> 2.09 us  [land_stage(): call(functools.partial(land_pack, count_gx, count_gz), [(packed, COLS), (...]
  transfers between devices with their start and end apart: 9 -> 9, of which waited for: 2 -> 2; matrix products, arithmetic and copies ran while one was open for 0% -> 0% of each run, Pallas kernels for 40% -> 38%
where the time goes in v6:
time: 32.5 us; the launch traced here: 32.1 us
  Pallas kernels  17.3 us (53%)
  starting transfers between devices  10.8 us (33%)
  waiting for transfers between devices  3.18 us (10%)
  between operations  0.73 us (2%)
    pallas_call x1, Pallas kernels, local(): main_call(*sizes)(params, ext, edge, y, land_temp, tr, air, rt, p, *start)  5.63 us
    ppermute x3, starting transfers between devices, land_stage(): lax.ppermute(parts[dist], AXES, xor_pairs(sizes, 'gz', dist))  5.5 us
    ppermute x5, starting transfers between devices, swap(): return lax.ppermute(value, AXES, pairing(sizes, axis, odd))  4.76 us
    pallas_call x1, Pallas kernels, local(): head = strip_call(*sizes)(main, inner, strips, y_e, y_o)  2.53 us
    pallas_call x1, Pallas kernels, land_stage(): call(own_part, own_shapes, [HBM] * 5, [pltpu.VMEM((len(OWN_AT), ROWS, COL...  2.5 us
    ppermute x3, waiting for transfers between devices, land_stage(): lax.ppermute(parts[dist], AXES, xor_pairs(sizes, 'gz', dist))  2.29 us
    pallas_call x1, Pallas kernels, land_stage(): call(functools.partial(land_pack, count_gx, count_gz), [(packed, COLS), (...  2.09 us
    pallas_call x1, Pallas kernels, local(): call(own_curves, [(3 * LEVELS, ROWS, COLS)] + START_SHAPES, [HBM] * 4, [p...  1.88 us
  transfers between devices with their start and end apart: 9, of which 2 were waited for; matrix products, arithmetic and copies ran while one was open for 0% of the time, Pallas kernels for 38%

profile of v6, /device:TPU:2, one launch (start us, length us, event | category | flops | bytes accessed | tf_op | source)
XLA Modules:
  0.0 32.1 jit_solution(2799395659201581537)
XLA Ops:
  0.6 1.4 %shard_map.114 = (f32[12,64,128]{2,1,0:T(8,128)S(1)}, f32[12,64,128]{2,1,0:T(8,128)S(1)}) custom-call(f32[16,64,128]{2,1,0:T(8,128)} %h.1, f32[16,64,128]{2,1,0:T(8,128)} %a.1, f32[16,64,128]{2,1,0:T(8,128)} %n.1, f32[16,64,128]{2,1,0:T(8,128)} %s.1, f32[16,64,128]{2,1,0:T(8,128)} %refs_5_.1), custom_call_target="tpu_custom_call" | custom-call | tf_op jit(solution)/shard_map/pallas_call | solution.py:945
  2.1 1.6 %collective-permute-start.4 = (f32[12,64,128]{2,1,0:T(8,128)S(1)}, f32[12,64,128]{2,1,0:T(8,128)S(1)}, u32[]{:S(2)}, u32[]{:S(2)}) collective-permute-start(f32[12,64,128]{2,1,0:T(8,128)S(1)} %get-tuple-element.59), channel_id=1, source_target_pairs={{0,1},{1,0},{2,3},{3,2},{4,5},{5,4},{6,7},{7,6},{8,9},{9,8},{10,11... | collective-permute-start | bytes 1179656 | tf_op jit(solution)/shard_map/ppermute | solution.py:938
  3.7 0.0 collective-permute-start.5
  3.7 14.0 %conditional.1 = (f32[80,16,128]{2,1,0:T(8,128)S(1)}, f32[14,64,128]{2,1,0:T(8,128)S(1)}, f32[2,64,128]{2,1,0:T(8,128)S(1)}, f32[8,24,128]{2,1,0:T(8,128)S(1)}) conditional(s32[]{:T(128)} %convert_element_type.3, () %tuple.16, (f32[16,64,128]{2,1,0:T(8,128)}, f32[16,64,128]{2,1,0:T(8,128)}, f32[16,64,128]{2,1,0:T(8,128)}, f32[16,64,128]{2,1,0:T(8,128)}, ...), branch_computations={%region_0.0_spmd, %region_1.0_spmd} | conditional | bytes 1278000 | solution.py:1033
  3.7 2.1 %branch_1_fun.5 = (f32[104,128]{1,0:T(8,128)S(1)}, f32[104,128]{1,0:T(8,128)S(1)}, f32[64,64]{1,0:T(8,128)S(1)}) custom-call(s32[4,128]{1,0:T(4,128)} %get-tuple-element.23.owners_in, f32[16,64,128]{2,1,0:T(8,128)} %get-tuple-element.16.refs_0_.h_in, f32[16,64,128]{2,1,0:T(8,128)} %get-tuple-element.17.refs_1_.a_in, ...), custom_call_target="tpu_custom_call" | custom-call | tf_op jit(solution)/shard_map/cond/branch_1_fun/pallas_call | solution.py:969
  5.8 0.6 %collective-permute-start = (f32[104,128]{1,0:T(8,128)S(1)}, f32[104,128]{1,0:T(8,128)S(1)}, u32[]{:S(2)}, u32[]{:S(2)}) collective-permute-start(f32[104,128]{1,0:T(8,128)S(1)} %get-tuple-element.28), channel_id=1, source_target_pairs={{0,4},{1,5},{2,6},{3,7},{4,0},{5,1},{6,2},{7,3},{8,12},{9,13},{10,... | collective-permute-start | bytes 159752 | tf_op jit(solution)/shard_map/cond/branch_1_fun/ppermute | solution.py:988
  6.4 0.9 %collective-permute-done.got = f32[104,128]{1,0:T(8,128)S(1)} collective-permute-done((f32[104,128]{1,0:T(8,128)S(1)}, f32[104,128]{1,0:T(8,128)S(1)}, u32[]{:S(2)}, u32[]{:S(2)}) %collective-permute-start) | collective-permute-done | bytes 53280 | tf_op jit(solution)/shard_map/cond/branch_1_fun/ppermute | solution.py:988
  7.3 3.1 %collective-permute-start.1 = (f32[64,128]{1,0:T(8,128)S(1)}, f32[64,128]{1,0:T(8,128)S(1)}, u32[]{:S(2)}, u32[]{:S(2)}) collective-permute-start(f32[64,128]{1,0:T(8,128)S(1)} %get-tuple-element.30), channel_id=1, source_target_pairs={{0,1},{1,0},{2,3},{3,2},{4,5},{5,4},{6,7},{7,6},{8,9},{9,8},{10,11... | collective-permute-start | bytes 98312 | tf_op jit(solution)/shard_map/cond/branch_1_fun/ppermute | solution.py:1019
  10.3 0.0 collective-permute-start.2
  10.4 2.4 %collective-permute-start.3 = (f32[64,128]{1,0:T(8,128)S(1)}, f32[64,128]{1,0:T(8,128)S(1)}, u32[]{:S(2)}, u32[]{:S(2)}) collective-permute-start(f32[64,128]{1,0:T(8,128)S(1)} %get-tuple-element.32), channel_id=1, source_target_pairs={{0,3},{1,2},{2,1},{3,0},{4,7},{5,6},{6,5},{7,4},{8,11},{9,10},{10,... | collective-permute-start | bytes 98312 | tf_op jit(solution)/shard_map/cond/branch_1_fun/ppermute | solution.py:1019
  12.8 2.5 %branch_1_fun.4 = (f32[80,16,128]{2,1,0:T(8,128)S(1)}, f32[14,64,128]{2,1,0:T(8,128)S(1)}) custom-call(f32[16,64,128]{2,1,0:T(8,128)} %get-tuple-element.16.refs_0_.h_in, f32[16,64,128]{2,1,0:T(8,128)} %get-tuple-element.17.refs_1_.a_in, f32[16,64,128]{2,1,0:T(8,128)} %get-tuple-element.18.refs_2_.n_in, f32[16,64,128]{2,1,0:T(8,128)} %get-tuple-element.19.refs_3_, ...), custom_call_target="tpu_custom_call" | custom-call | tf_op jit(solution)/shard_map/cond/branch_1_fun/pallas_call | solution.py:1007
  15.3 0.0 collective-permute-done.1.refs_1_
  15.3 2.3 %collective-permute-done.2.refs_2_ = f32[64,128]{1,0:T(8,128)S(1)} collective-permute-done((f32[64,128]{1,0:T(8,128)S(1)}, f32[64,128]{1,0:T(8,128)S(1)}, u32[]{:S(2)}, u32[]{:S(2)}) %collective-permute-start.2) | collective-permute-done | bytes 32800 | tf_op jit(solution)/shard_map/cond/branch_1_fun/ppermute | solution.py:1019
  17.6 0.0 collective-permute-done.3.refs_3_
  17.6 0.2 branch_1_fun.7
  17.8 0.0 collective-permute-done.4.z_e
  17.8 0.0 collective-permute-done.5.z_o
  17.8 0.1 shard_map.115
  17.9 0.1 collective-permute-start.6
  18.0 1.9 %shard_map.113 = (f32[48,64,128]{2,1,0:T(8,128)S(1)}, f32[22,88,128]{2,1,0:T(8,128)S(1)}, f32[22,88,128]{2,1,0:T(8,128)S(1)}, f32[20,72,128]{2,1,0:T(8,128)S(1)}, f32[18,72,128]{2,1,0:T(8,128)S(1)}) custom-call(f32[16,64,128]{2,1,0:T(8,128)} %h.1, f32[16,64,128]{2,1,0:T(8,128)} %a.1, f32[16,64,128]{2,1,0:T(8,128)} %n.1, f32[16,64,128]{2,1,0:T(8,128)} %s.1), custom_call_target="tpu_custom_call" | custom-call | tf_op jit(solution)/shard_map/pallas_call | solution.py:1040
  19.9 0.0 collective-permute-done.6.refs_4_
  19.9 1.0 %shard_map.116 = (f32[106,8,128]{2,1,0:T(8,128)S(1)}, f32[1792,128]{1,0:T(8,128)S(1)}, f32[160,128]{1,0:T(8,128)S(1)}, f32[160,128]{1,0:T(8,128)S(1)}) custom-call(f32[80,16,128]{2,1,0:T(8,128)S(1)} %get-tuple-element.58.rim.refs_0_, f32[14,64,128]{2,1,0:T(8,128)S(1)} %get-tuple-element.63.refs_1_, f32[26,64,128]{2,1,0:T(8,128)S(1)} %get-tuple-element.62.refs_2_.ext, ...), custom_call_target="tpu_custom_call" | custom-call | tf_op jit(solution)/shard_map/pallas_call | solution.py:1048
  20.9 0.6 %collective-permute-start.7 = (f32[160,128]{1,0:T(8,128)S(1)}, f32[160,128]{1,0:T(8,128)S(1)}, u32[]{:S(2)}, u32[]{:S(2)}) collective-permute-start(f32[160,128]{1,0:T(8,128)S(1)} %get-tuple-element.74), channel_id=1, source_target_pairs={{0,8},{1,9},{2,10},{3,11},{4,12},{5,13},{6,14},{7,15},{8,0},{9,1},... | collective-permute-start | bytes 245768 | tf_op jit(solution)/shard_map/ppermute | solution.py:938
  21.5 2.5 %collective-permute-start.8 = (f32[160,128]{1,0:T(8,128)S(1)}, f32[160,128]{1,0:T(8,128)S(1)}, u32[]{:S(2)}, u32[]{:S(2)}) collective-permute-start(f32[160,128]{1,0:T(8,128)S(1)} %get-tuple-element.75), channel_id=1, source_target_pairs={{0,4},{1,5},{2,6},{3,7},{4,0},{5,1},{6,2},{7,3},{8,16},{9,17},{10,... | collective-permute-start | bytes 245768 | tf_op jit(solution)/shard_map/ppermute | solution.py:938
  23.9 5.6 %shard_map.117 = (f32[16,64,128]{2,1,0:T(8,128)S(1)}, f32[128,128]{1,0:T(8,128)S(1)}, f32[6,16,128]{2,1,0:T(8,128)}, f32[22,88,128]{2,1,0:T(8,128)S(1)}, f32[22,...) custom-call(f32[48,64,128]{2,1,0:T(8,128)S(1)} %get-tuple-element.57, ...), custom_call_target="tpu_custom_call", output_to_operand_aliasing={{3}: (9, {}), {4}: (10, {}), {5}: (11, {}), {6}: (12, {})} | custom-call | tf_op jit(solution)/shard_map/pallas_call | solution.py:1057
  29.6 0.0 collective-permute-done.7.y_e
  29.6 0.0 collective-permute-done.8.y_o
  29.6 2.5 %shard_map.118 = f32[16,64,128]{2,1,0:T(8,128)} custom-call(f32[16,64,128]{2,1,0:T(8,128)S(1)} %get-tuple-element.71.main, f32[128,128]{1,0:T(8,128)S(1)} %get-tuple-element.72.inner, f32[1792,128]{1,0:T(8,128)S(1)} %get-tuple-element.73.strips_in, f32[160,128]{1,0:T(8,128)S(1)} %collective-permute-done.7.y_e, f32[160,128]{1,0:T(8,128)S(1)} %collective-permute-done.8.y_o), custom_call_target="tpu_custom_call" | custom-call | tf_op jit(solution)/shard_map/pallas_call | solution.py:1058
  (1 shorter events, 0.0 us)
Async XLA Ops:
  2.1 15.7 %collective-permute-start.4 = (f32[12,64,128]{2,1,0:T(8,128)S(1)}, f32[12,64,128]{2,1,0:T(8,128)S(1)}, u32[]{:S(2)}, u32[]{:S(2)}) collective-permute-start(f32[12,64,128]{2,1,0:T(8,128)S(1)} %get-tuple-element.59), channel_id=1, source_target_pairs={{0,1},{1,0},{2,3},{3,2},{4,5},{5,4},{6,7},{7,6},{8,9},{9,8},{10,11... | collective-permute-start | bytes 1179656 | tf_op jit(solution)/shard_map/ppermute | solution.py:938
  3.7 14.1 %collective-permute-start.5 = (f32[12,64,128]{2,1,0:T(8,128)S(1)}, f32[12,64,128]{2,1,0:T(8,128)S(1)}, u32[]{:S(2)}, u32[]{:S(2)}) collective-permute-start(f32[12,64,128]{2,1,0:T(8,128)S(1)} %get-tuple-element.60), channel_id=1, source_target_pairs={{0,4},{1,2},{2,1},{3,7},{4,0},{5,6},{6,5},{7,3},{8,12},{9,10},{10,... | collective-permute-start | bytes 1179656 | tf_op jit(solution)/shard_map/ppermute | solution.py:938
  5.8 1.5 %collective-permute-start = (f32[104,128]{1,0:T(8,128)S(1)}, f32[104,128]{1,0:T(8,128)S(1)}, u32[]{:S(2)}, u32[]{:S(2)}) collective-permute-start(f32[104,128]{1,0:T(8,128)S(1)} %get-tuple-element.28), channel_id=1, source_target_pairs={{0,4},{1,5},{2,6},{3,7},{4,0},{5,1},{6,2},{7,3},{8,12},{9,13},{10,... | collective-permute-start | bytes 159752 | tf_op jit(solution)/shard_map/cond/branch_1_fun/ppermute | solution.py:988
  7.3 8.0 %collective-permute-start.1 = (f32[64,128]{1,0:T(8,128)S(1)}, f32[64,128]{1,0:T(8,128)S(1)}, u32[]{:S(2)}, u32[]{:S(2)}) collective-permute-start(f32[64,128]{1,0:T(8,128)S(1)} %get-tuple-element.30), channel_id=1, source_target_pairs={{0,1},{1,0},{2,3},{3,2},{4,5},{5,4},{6,7},{7,6},{8,9},{9,8},{10,11... | collective-permute-start | bytes 98312 | tf_op jit(solution)/shard_map/cond/branch_1_fun/ppermute | solution.py:1019
  10.3 7.2 %collective-permute-start.2 = (f32[64,128]{1,0:T(8,128)S(1)}, f32[64,128]{1,0:T(8,128)S(1)}, u32[]{:S(2)}, u32[]{:S(2)}) collective-permute-start(f32[64,128]{1,0:T(8,128)S(1)} %get-tuple-element.31), channel_id=1, source_target_pairs={{0,2},{1,3},{2,0},{3,1},{4,6},{5,7},{6,4},{7,5},{8,10},{9,11},{10,... | collective-permute-start | bytes 98312 | tf_op jit(solution)/shard_map/cond/branch_1_fun/ppermute | solution.py:1019
  10.4 7.2 %collective-permute-start.3 = (f32[64,128]{1,0:T(8,128)S(1)}, f32[64,128]{1,0:T(8,128)S(1)}, u32[]{:S(2)}, u32[]{:S(2)}) collective-permute-start(f32[64,128]{1,0:T(8,128)S(1)} %get-tuple-element.32), channel_id=1, source_target_pairs={{0,3},{1,2},{2,1},{3,0},{4,7},{5,6},{6,5},{7,4},{8,11},{9,10},{10,... | collective-permute-start | bytes 98312 | tf_op jit(solution)/shard_map/cond/branch_1_fun/ppermute | solution.py:1019
  17.9 2.0 %collective-permute-start.6 = (f32[106,4,128]{2,1,0:T(4,128)S(1)}, f32[106,4,128]{2,1,0:T(4,128)S(1)}, u32[]{:S(2)}, u32[]{:S(2)}) collective-permute-start(f32[106,4,128]{2,1,0:T(4,128)S(1)} %get-tuple-element.64), channel_id=1, source_target_pairs={{0,4},{1,5},{2,6},{3,7},{4,0},{5,1},{6,2},{7,3},{8,12},{9,13},{10,... | collective-permute-start | bytes 651272 | tf_op jit(solution)/shard_map/ppermute | solution.py:938
  20.9 8.7 %collective-permute-start.7 = (f32[160,128]{1,0:T(8,128)S(1)}, f32[160,128]{1,0:T(8,128)S(1)}, u32[]{:S(2)}, u32[]{:S(2)}) collective-permute-start(f32[160,128]{1,0:T(8,128)S(1)} %get-tuple-element.74), channel_id=1, source_target_pairs={{0,8},{1,9},{2,10},{3,11},{4,12},{5,13},{6,14},{7,15},{8,0},{9,1},... | collective-permute-start | bytes 245768 | tf_op jit(solution)/shard_map/ppermute | solution.py:938
  21.5 8.1 %collective-permute-start.8 = (f32[160,128]{1,0:T(8,128)S(1)}, f32[160,128]{1,0:T(8,128)S(1)}, u32[]{:S(2)}, u32[]{:S(2)}) collective-permute-start(f32[160,128]{1,0:T(8,128)S(1)} %get-tuple-element.75), channel_id=1, source_target_pairs={{0,4},{1,5},{2,6},{3,7},{4,0},{5,1},{6,2},{7,3},{8,16},{9,17},{10,... | collective-permute-start | bytes 245768 | tf_op jit(solution)/shard_map/ppermute | solution.py:938
